TPU v7x, 256 devices: a whole 4x4x8 slice. The times are simulated.
256 devices in a mesh: seq: 32 (over y, x, core), tp: 8 (over z).
Axes of the slice: x: 4, y: 4, z: 8, core: 2. Of those that a mesh axis runs over, the one named last changes fastest.
Arguments:
- head_queries: bfloat16 [16384, 8192], P('seq', 'tp'), may hold values from -8 to 8
- key_projection_rows: bfloat16 [16384, 1024], P('seq', 'tp'), may hold values from -8 to 8
- value_projection_rows: bfloat16 [16384, 1024], P('seq', 'tp'), may hold values from -6 to 6
- gate_logit: bfloat16 [16384], P('seq'), may hold values from -8 to 8
- upstream: bfloat16 [16384, 8192], P('seq', 'tp'), may hold values from -16 to 16
- picked: int32 [4096], P('seq'), may hold values from 0 to 512, as said below
Outputs:
- query_grad: bfloat16 [16384, 8192], P('seq', 'tp')
- key_grad: bfloat16 [16384, 1024], P('seq', 'tp')
- value_grad: bfloat16 [16384, 1024], P('seq', 'tp')
- logit_grad: bfloat16 [16384], P('seq')
Inputs may be any that keep to these rules, and one draw needn't show every extreme that they name: Block j of 128 entries belongs to seq shard j: that shard's picked local token positions in increasing order, then 512 in every empty slot. 2048 positions are picked in all, and some shard fills all 128 slots.
All inputs are finite; a program needn't handle non-finite values.
Results may differ from a plain program's by a relative error of at most 0.012.
The roundings to bfloat16 on the way count: a program that leaves them out, or rounds other values in their place, can miss the bound.
Values may be sent and summed in bfloat16 or wider, within the bound.
No kernel may reach another device: no remote copies, remote signals or barrier semaphores. Data moves between devices by JAX's collectives and lax.ppermute only.
A program may use at most 128 MiB of HBM per device.

v0:
```python
import math

import jax
import jax.numpy as jnp
from jax import lax
from jax.sharding import PartitionSpec as P

QUERY_HEADS = 64
KEY_VALUE_HEADS = 8
HEAD_SIZE = 128


def head_split(matrix, kv_local, block_count, head_width):
    row_count = matrix.shape[0]
    shaped = matrix.reshape(row_count, kv_local * block_count, -1, head_width)
    return jnp.transpose(shaped, (1, 2, 0, 3))


def key_split(matrix, kv_local, block_count, head_width):
    shaped = matrix.reshape(matrix.shape[0], kv_local, head_width)
    return jnp.repeat(jnp.transpose(shaped, (1, 0, 2)), block_count, axis=0)


def head_join(stacked, row_count):
    return jnp.transpose(stacked, (2, 0, 1, 3)).reshape(row_count, -1)


def attend(
    head_rows,
    incoming_rows,
    switch_rows,
    picked_key_rows,
    picked_value_rows,
    allowed,
    head_width,
    query_group_width,
):
    row_count = head_rows.shape[0]
    kv_local = picked_key_rows.shape[1] // head_width
    block_size = math.gcd(query_group_width, max(1, 512 // row_count))
    block_count = query_group_width // block_size
    factor = 1.0 / math.sqrt(head_width)
    query_blocks = head_split(head_rows, kv_local, block_count, head_width)
    incoming_blocks = head_split(incoming_rows, kv_local, block_count, head_width)
    key_blocks = key_split(picked_key_rows, kv_local, block_count, head_width)
    value_blocks = key_split(picked_value_rows, kv_local, block_count, head_width)

    def single(operands):
        query_part, incoming_part, key_part, value_part = operands
        scores = (
            jnp.einsum("hrd,kd->hrk", query_part, key_part, preferred_element_type=jnp.float32)
            * factor
        )
        scores = jnp.where(allowed[None], scores, -1e30)
        highest = jnp.max(scores, axis=-1, keepdims=True)
        raised = jnp.exp(scores - highest)
        weights = raised / jnp.sum(raised, axis=-1, keepdims=True)
        weights_low = weights.astype(jnp.bfloat16)
        attended = jnp.einsum(
            "hrk,kd->hrd", weights_low, value_part, preferred_element_type=jnp.float32
        )
        incoming = incoming_part.astype(jnp.float32)
        products = jnp.sum(incoming * attended, axis=-1)
        scaled = incoming * switch_rows[None, :, None]
        deltas = jnp.sum(scaled * attended, axis=-1, keepdims=True)
        scaled_low = scaled.astype(jnp.bfloat16)
        pushed = jnp.einsum(
            "hrd,kd->hrk", scaled_low, value_part, preferred_element_type=jnp.float32
        )
        slopes = (weights * (pushed - deltas)).astype(jnp.bfloat16)
        query_grad = (
            jnp.einsum("hrk,kd->hrd", slopes, key_part, preferred_element_type=jnp.float32) * factor
        )
        return (query_grad, jnp.sum(products, axis=0), weights_low, slopes, scaled_low)

    query_grad, products, weights_low, slopes, scaled_low = lax.map(
        single, (query_blocks, incoming_blocks, key_blocks, value_blocks)
    )
    retained = (weights_low, slopes, scaled_low, query_blocks)
    return (
        head_join(query_grad, row_count),
        jnp.sum(products, axis=0),
        retained,
        (kv_local, block_count, factor),
    )


def key_terms(retained, shape_info, count):
    weights_low, slopes, scaled_low, query_blocks = retained
    kv_local, block_count, factor = shape_info
    key_part = (
        jnp.einsum("nhrk,nhrd->nkd", slopes, query_blocks, preferred_element_type=jnp.float32)
        * factor
    )
    value_part = jnp.einsum(
        "nhrk,nhrd->nkd", weights_low, scaled_low, preferred_element_type=jnp.float32
    )
    key_part = key_part.reshape(kv_local, block_count, count, -1).sum(axis=1)
    value_part = value_part.reshape(kv_local, block_count, count, -1).sum(axis=1)
    flattened_keys = jnp.transpose(key_part, (1, 0, 2)).reshape(count, -1)
    flattened_values = jnp.transpose(value_part, (1, 0, 2)).reshape(count, -1)
    return jnp.concatenate([flattened_keys, flattened_values], axis=1)


def local(head_queries, key_projection_rows, value_projection_rows, gate_logit, upstream, picked):
    tokens = head_queries.shape[0]
    slots = picked.shape[0]
    shards = lax.axis_size("seq")
    own_index = lax.axis_index("seq")
    feature = head_queries.shape[1]
    kv_width = key_projection_rows.shape[1]
    query_group_width = QUERY_HEADS // KEY_VALUE_HEADS
    live_slot = picked < tokens
    clamped = jnp.minimum(picked, tokens - 1)
    mine_count = jnp.sum(live_slot.astype(jnp.int32))
    counts = lax.all_gather(mine_count[None], "seq", axis=0, tiled=True)
    local_kv = jnp.concatenate(
        [key_projection_rows[clamped], value_projection_rows[clamped]], axis=1
    )
    all_kv = lax.all_gather(local_kv, "seq", axis=0, tiled=True)
    key_order = jnp.arange(shards * slots, dtype=jnp.int32)
    key_shard = key_order // slots
    key_slot = key_order % slots
    key_live = key_slot < jnp.repeat(counts, slots)
    slot_row = jnp.arange(slots, dtype=jnp.int32)
    earlier = key_shard < own_index
    same_shard = key_shard == own_index
    allowed = key_live[None, :] & (
        earlier[None, :] | same_shard[None, :] & (key_slot[None, :] <= slot_row[:, None])
    )
    switch = jax.nn.sigmoid(gate_logit[clamped].astype(jnp.float32))
    gate_rows = switch * live_slot.astype(jnp.float32)
    query_rows_grad, products, retained, shape_info = attend(
        head_queries[clamped],
        upstream[clamped],
        gate_rows,
        all_kv[:, :kv_width],
        all_kv[:, kv_width:],
        allowed,
        HEAD_SIZE,
        query_group_width,
    )
    key_value_grad = lax.psum_scatter(
        key_terms(retained, shape_info, lax.axis_size("seq") * slots),
        "seq",
        scatter_dimension=0,
        tiled=True,
    )
    totals = lax.psum(products, "tp")
    logit_rows = (switch * (1.0 - switch) * totals).astype(jnp.bfloat16)
    returned = jnp.concatenate(
        [query_rows_grad.astype(jnp.bfloat16), key_value_grad.astype(jnp.bfloat16)], axis=1
    )
    query_out = (
        jnp.zeros((tokens, feature), jnp.bfloat16)
        .at[picked]
        .set(returned[:, :feature], mode="drop")
    )
    key_result = (
        jnp.zeros((tokens, kv_width), jnp.bfloat16)
        .at[picked]
        .set(returned[:, feature : feature + kv_width], mode="drop")
    )
    value_result = (
        jnp.zeros((tokens, kv_width), jnp.bfloat16)
        .at[picked]
        .set(returned[:, feature + kv_width :], mode="drop")
    )
    logit_out = jnp.zeros((tokens,), jnp.bfloat16).at[picked].set(logit_rows, mode="drop")
    return (query_out, key_result, value_result, logit_out)


def solution(mesh):
    placed = (P("seq", "tp"), P("seq", "tp"), P("seq", "tp"), P("seq"), P("seq", "tp"), P("seq"))
    return jax.shard_map(
        local,
        mesh=mesh,
        in_specs=placed,
        out_specs=(P("seq", "tp"), P("seq", "tp"), P("seq", "tp"), P("seq")),
        check_vma=False,
    )
```

profile of v0, /device:TPU:64, one launch (start us, length us, event | category | flops | bytes accessed | tf_op | source)
XLA Modules:
  0.0 243.8 jit_solution(11265635629896490658)
XLA Ops:
  7.2 1.9 fusion.69
  9.2 1.6 gather_fusion.2
  10.7 1.6 gather_fusion.1
  13.1 1.7 gather_fusion.4
  15.8 2.4 gather_fusion
  21.9 16.9 %all-reduce = s32[32]{0:T(128)S(1)} all-reduce(s32[32]{0:T(128)S(1)} %dynamic-update-slice), channel_id=1, replica_groups=mesh['seq'=32,'tp'=8] {'seq'}, use_global_device_ids=true, to_apply=%add | all-reduce | flops 32 | bytes 256
  41.3 22.9 %all-gather.2.cloned.1.call-done = bf16[4096,256]{1,0:T(8,128)(2,1)} async-done(((bf16[128,256]{1,0:T(8,128)(2,1)}), bf16[4096,256]{1,0:T(8,128)(2,1)}) %all-gather.2.cloned.1.call-update) | async-done | bytes 2097168 | tf_op jit(solution)/shard_map/all_gather | solution.py:120
  64.2 1.7 fusion.79
  66.1 1.5 reshape.74
  67.6 58.6 %while.19 = (s32[]{:T(128)}, bf16[2,4,128,128]{2,3,1,0:T(8,128)(2,1)}, f32[2,128]{1,0:T(2,128)}, bf16[2,4,128,4096]{3,2,0,1:T(8,128)(2,1)}, bf16[2,4,128,4096]{3...) while((s32[]{:T(128)}, ...), condition=%wide.region_6.7_spmd.clone, body=%wide.region_1.6_spmd.clone.sunk | while | flops 2171473408 | bytes 65319636 | solution.py:76
  68.8 2.0 fusion.100
  70.8 7.8 %fusion.101 = (f32[4,128]{1,0:T(4,128)S(1)}, f32[4,128,4096]{2,1,0:T(8,128)}) fusion(pred[128,4096]{1,0:T(8,128)(4,1)} %fusion.100, bf16[2,4096,128]{2,1,0:T(8,128)(2,1)} %get-tuple-element.308, s32[]{:T(128)S(6)} %copy.82, bf16[2,4,128,128]{3,2,1,0:T(8,128)(2,1)} %get-tuple-element.307), kind=kOutput, calls=%fused_computation.102.clone.1 | convolution fusion | flops 545263616 | bytes 10095616 | tf_op jit(solution)/shard_map/while/body/eval_jaxpr/sub | solution.py:56
  78.6 5.3 %bitcast_dynamic-update-slice_fusion.6 = (bf16[2,4,128,4096]{3,2,0,1:T(8,128)(2,1)}, bf16[4,128,4096]{2,1,0:T(8,128)(2,1)S(1)}) fusion(bf16[2,4,128,4096]{3,2,0,1:T(8,128)(2,1)} %get-tuple-element.287, s32[]{:T(128)S(6)} %copy.82, f32[4,128,4096]{2,1,0:T(8,128)} %get-tuple-element.259, f32[4,128]{1,0:T(4,128)S(1)} %get-tuple-element.260), kind=kLoop, calls=%fused_computation.15.clone.1 | loop fusion | flops 4194304 | bytes 16779268 | tf_op jit(solution)/shard_map/while/body/jit(dynamic_update_index_in_dim)/dynamic_update_slice | solution.py:76
  83.9 2.2 fusion.102
  87.4 5.9 %bitcast_dynamic-update-slice_fusion.7 = (bf16[2,4,128,4096]{3,2,1,0:T(8,128)(2,1)}, bf16[4,128,4096]{2,1,0:T(8,128)(2,1)S(1)}) fusion(bf16[2,4,128,4096]{3,2,1,0:T(8,128)(2,1)} %get-tuple-element.288, s32[]{:T(128)S(6)} %copy.82, f32[4,128]{1,0:T(4,128)S(1)} %get-tuple-element.262, bf16[2,4096,128]{2,1,0:T(8,128)(2,1)S(1)} %get-tuple-element.311, ...), kind=kOutput, calls=%fused_computation.16.clone.1 | convolution fusion | flops 545456128 | bytes 17963008 | tf_op jit(solution)/shard_map/while/body/eval_jaxpr/hrd,kd->hrk/dot_general | solution.py:67
  93.3 1.9 fusion.103
  98.1 2.0 fusion.100
  100.1 7.8 %fusion.101 = (f32[4,128]{1,0:T(4,128)S(1)}, f32[4,128,4096]{2,1,0:T(8,128)}) fusion(pred[128,4096]{1,0:T(8,128)(4,1)} %fusion.100, bf16[2,4096,128]{2,1,0:T(8,128)(2,1)} %get-tuple-element.308, s32[]{:T(128)S(6)} %copy.82, bf16[2,4,128,128]{3,2,1,0:T(8,128)(2,1)} %get-tuple-element.307), kind=kOutput, calls=%fused_computation.102.clone.1 | convolution fusion | flops 545263616 | bytes 10095616 | tf_op jit(solution)/shard_map/while/body/eval_jaxpr/sub | solution.py:56
  107.9 5.3 %bitcast_dynamic-update-slice_fusion.6 = (bf16[2,4,128,4096]{3,2,0,1:T(8,128)(2,1)}, bf16[4,128,4096]{2,1,0:T(8,128)(2,1)S(1)}) fusion(bf16[2,4,128,4096]{3,2,0,1:T(8,128)(2,1)} %get-tuple-element.287, s32[]{:T(128)S(6)} %copy.82, f32[4,128,4096]{2,1,0:T(8,128)} %get-tuple-element.259, f32[4,128]{1,0:T(4,128)S(1)} %get-tuple-element.260), kind=kLoop, calls=%fused_computation.15.clone.1 | loop fusion | flops 4194304 | bytes 16779268 | tf_op jit(solution)/shard_map/while/body/jit(dynamic_update_index_in_dim)/dynamic_update_slice | solution.py:76
  113.2 2.2 fusion.102
  116.6 5.9 %bitcast_dynamic-update-slice_fusion.7 = (bf16[2,4,128,4096]{3,2,1,0:T(8,128)(2,1)}, bf16[4,128,4096]{2,1,0:T(8,128)(2,1)S(1)}) fusion(bf16[2,4,128,4096]{3,2,1,0:T(8,128)(2,1)} %get-tuple-element.288, s32[]{:T(128)S(6)} %copy.82, f32[4,128]{1,0:T(4,128)S(1)} %get-tuple-element.262, bf16[2,4096,128]{2,1,0:T(8,128)(2,1)S(1)} %get-tuple-element.311, ...), kind=kOutput, calls=%fused_computation.16.clone.1 | convolution fusion | flops 545456128 | bytes 17963008 | tf_op jit(solution)/shard_map/while/body/eval_jaxpr/hrd,kd->hrk/dot_general | solution.py:67
  122.6 1.9 fusion.103
  126.2 8.2 %fusion.54 = f32[4096,128]{1,0:T(8,128)} fusion(bf16[2,4,128,4096]{3,2,1,0:T(8,128)(2,1)} %get-tuple-element.71, bf16[128,2,4,128]{3,2,1,0:T(4,128)(2,1)} %copy-done.1), kind=kOutput, calls=%fused_computation.68 | convolution fusion | flops 1075314688 | bytes 10747904 | tf_op jit(solution)/shard_map/nhrk,nhrd->nkd/dot_general | solution.py:92
  134.4 2.1 copy.47
  136.6 4.6 %convolution_bitcast_fusion.1 = f32[4096,128]{0,1:T(8,128)S(1)} fusion(bf16[2,4,128,128]{2,3,0,1:T(8,128)(2,1)S(1)} %copy-done.4, bf16[2,4,128,4096]{3,2,0,1:T(8,128)(2,1)} %get-tuple-element.72), kind=kOutput, calls=%fused_computation.66 | convolution fusion | flops 1073741824 | bytes 10747904 | tf_op jit(solution)/shard_map/nhrk,nhrd->nkd/dot_general | solution.py:95
  141.3 2.3 pad_maximum_fusion
  144.5 15.1 %psum.7 = f32[128]{0:T(128)S(1)} all-reduce(f32[128]{0:T(128)S(1)} %reduce_sum.64), channel_id=1, replica_groups=mesh['seq'=32,'tp'=8] {'tp'}, use_global_device_ids=true, to_apply=%region_13.14 | all-reduce | flops 128 | bytes 1024 | tf_op jit(solution)/shard_map/psum | solution.py:149
  159.6 2.0 scatter_custom_fusion.3
  161.6 2.3 scatter_custom_fusion
  163.9 68.6 %reduce-scatter.2.cloned.1.call-done = f32[128,256]{0,1:T(8,128)} async-done(((f32[4096,256]{0,1:T(8,128)}), f32[128,256]{0,1:T(8,128)}) %reduce-scatter.2.cloned.1.call-update) | async-done | bytes 131088 | tf_op jit(solution)/shard_map/reduce_scatter | solution.py:143
  233.7 1.6 scatter_custom_fusion.1
  235.4 1.6 scatter_custom_fusion.2
  (52 shorter events, 18.5 us)
Async XLA Ops:
  7.2 7.6 %copy-start = (bf16[512,1024]{1,0:T(8,128)(2,1)S(1)}, bf16[512,1024]{1,0:T(8,128)(2,1)}, u32[]{:S(2)}) copy-start(bf16[512,1024]{1,0:T(8,128)(2,1)} %param.12) | copy-start | bytes 3145732
  7.2 57.0 %all-gather.2.cloned.1.call-start = ((), (), s32[]{:S(2)}) async-start(), calls=%async_computation.1 | async-start | bytes 2162688 | tf_op jit(solution)/shard_map/all_gather | solution.py:120
  13.0 219.6 %reduce-scatter.2.cloned.1.call-start = ((), (), s32[]{:S(2)}) async-start(), calls=%async_computation.2 | async-start | bytes 4325376 | tf_op jit(solution)/shard_map/reduce_scatter | solution.py:143
  18.4 47.5 %copy-start.1 = (bf16[128,2,4,128]{3,2,1,0:T(4,128)(2,1)}, bf16[128,2,4,128]{3,2,1,0:T(4,128)(2,1)S(1)}, u32[]{:S(2)}) copy-start(bf16[128,2,4,128]{3,2,1,0:T(4,128)(2,1)S(1)} %reshape.73) | copy-start | bytes 786436
  87.4 5.9 %copy-start.2 = (bf16[2,4096,128]{2,1,0:T(8,128)(2,1)S(1)}, bf16[2,4096,128]{2,1,0:T(8,128)(2,1)}, u32[]{:S(2)}) copy-start(bf16[2,4096,128]{2,1,0:T(8,128)(2,1)} %get-tuple-element.308) | copy-start | bytes 6291460 | tf_op jit(solution)/shard_map/while
  116.6 6.0 %copy-start.2 = (bf16[2,4096,128]{2,1,0:T(8,128)(2,1)S(1)}, bf16[2,4096,128]{2,1,0:T(8,128)(2,1)}, u32[]{:S(2)}) copy-start(bf16[2,4096,128]{2,1,0:T(8,128)(2,1)} %get-tuple-element.308) | copy-start | bytes 6291460 | tf_op jit(solution)/shard_map/while
  126.2 10.4 %copy-start.4 = (bf16[2,4,128,128]{2,3,0,1:T(8,128)(2,1)S(1)}, bf16[2,4,128,128]{2,3,0,1:T(8,128)(2,1)}, u32[]{:S(2)}) copy-start(bf16[2,4,128,128]{2,3,0,1:T(8,128)(2,1)} %get-tuple-element.73) | copy-start | bytes 786436
  141.2 2.4 copy-start.3
  141.3 18.4 %copy-start.5 = (f32[128]{0:T(128)S(1)}, f32[128]{0:T(128)}, u32[]{:S(2)}) copy-start(f32[128]{0:T(128)} %get-tuple-element.146) | copy-start | bytes 1540
Sparse Core Ops, SparseCore 0:
  13.1 51.0 all-gather.1
  143.7 88.7 reduce-scatter.1
where the time goes:
time: 245 us; the launch traced here: 244 us
  waiting for transfers between devices  91.6 us (37%)
  matrix products  48.5 us (20%)
  blocking collectives  32.1 us (13%)
  local copies, waits for them, and re-layouts  31.3 us (13%)
  other arithmetic  26.1 us (11%)
  between operations  14.2 us (6%)
    reduce_scatter x1, waiting for transfers between devices, local(): lax.psum_scatter(key_terms(retained, shape_info, lax.axis_size('seq') * s...  68.6 us
    all_gather x1, waiting for transfers between devices, local(): all_kv = lax.all_gather(local_kv, 'seq', axis=0, tiled=True)  22.9 us
    unnamed x1, blocking collectives  16.9 us
    sub x2, matrix products, single(): raised = jnp.exp(scores - highest)  15.6 us
    psum x1, blocking collectives, local(): totals = lax.psum(products, 'tp')  15.1 us
    dynamic_update_slice x4, other arithmetic, attend(): lax.map(single, (query_blocks, incoming_blocks, key_blocks, value_blocks))  13.1 us
    dot_general x2, matrix products, single(): jnp.einsum('hrd,kd->hrk', scaled_low, value_part, preferred_element_type=...  11.9 us
    dot_general x1, matrix products, key_terms(): jnp.einsum('nhrk,nhrd->nkd', slopes, query_blocks, preferred_element_type...  8.24 us
  transfers between devices with their start and end apart: 2, of which 2 were waited for; matrix products, arithmetic and copies ran while one was open for 7% of the time, Pallas kernels for 0%

commit v1 on v0

v1 whole, which is shorter than its diff:
```python
import functools
import math

import jax
import jax.numpy as jnp
from jax import lax
from jax.experimental import pallas as pl
from jax.experimental.pallas import tpu as pltpu
from jax.sharding import Mesh, PartitionSpec as P

QUERY_HEADS = 64
KEY_VALUE_HEADS = 8
HEAD = 128
SLOTS = 128
TOKENS = 512
CHIPS = 16
PICKED = 2048
GROUP = QUERY_HEADS // KEY_VALUE_HEADS
FACTOR = 1.0 / math.sqrt(HEAD)
LOG_FACTOR = FACTOR * math.log2(math.e)
CHUNK = 32
CHUNKS = SLOTS // CHUNK
ROWS = GROUP * CHUNK
KEYS = 512
SENTINEL = 128.0
LIVE_BELOW = 32.0
NEGATIVE = -1e30
F32 = jnp.float32
BF16 = jnp.bfloat16
VMEM_BYTES = 48 * 1024 * 1024


def nt_dot(a, b):
    return lax.dot_general(a, b, (((1,), (1,)), ((), ())), preferred_element_type=F32)


def tn_dot(a, b):
    return lax.dot_general(a, b, (((0,), (0,)), ((), ())), preferred_element_type=F32)


def place_matrix(picked):
    token = lax.broadcasted_iota(jnp.int32, (TOKENS, SLOTS), 0)
    return jnp.where(token == picked, 1.0, 0.0).astype(F32)


def switch_of(gate, gather):
    rows = jnp.dot(
        jnp.broadcast_to(gate, (16, TOKENS)), gather.astype(BF16), preferred_element_type=F32
    )
    return 1.0 / (1.0 + jnp.exp(-rows))


def pick_kernel(picked_ref, gate_ref, k_ref, v_ref, q_ref, up_ref, kv_out, qs_out):
    placed = place_matrix(picked_ref[...])
    gather = placed.T.astype(BF16)
    slot_dead = (
        jnp.broadcast_to(
            jnp.where(picked_ref[...] >= TOKENS, 1.0, 0.0).astype(F32), (SLOTS, SLOTS)
        ).T
        * SENTINEL
    )
    switch = jnp.broadcast_to(switch_of(gate_ref[...], placed)[0:1], (SLOTS, SLOTS)).T
    keys = (jnp.dot(gather, k_ref[...], preferred_element_type=F32) + slot_dead).astype(BF16)
    values = jnp.dot(gather, v_ref[...], preferred_element_type=F32).astype(BF16)
    for chip in range(CHIPS):
        kv_out[chip, :, 0:HEAD] = keys
        kv_out[chip, :, HEAD : 2 * HEAD] = values
    for h in range(GROUP):
        lanes = slice(h * HEAD, (h + 1) * HEAD)
        q_rows = jnp.dot(gather, q_ref[:, lanes], preferred_element_type=F32)
        q_rows = (q_rows + slot_dead).astype(BF16)
        up_rows = jnp.dot(gather, up_ref[:, lanes], preferred_element_type=F32)
        scaled = (up_rows * switch).astype(BF16)
        for t in range(CHUNKS):
            rows = slice(t * CHUNK, (t + 1) * CHUNK)
            qs_out[0, t, h * CHUNK : (h + 1) * CHUNK, :] = q_rows[rows]
            qs_out[1, t, h * CHUNK : (h + 1) * CHUNK, :] = scaled[rows]


def count_live(block):
    live = jnp.where(block.astype(F32) < LIVE_BELOW, 1.0, 0.0)
    return jnp.sum(live, axis=0, keepdims=True)[0, 0].astype(jnp.int32)


def row_limit(t, offset, count, core):
    lane = lax.broadcasted_iota(jnp.int32, (1, ROWS), 1)
    own = offset + (t % CHUNKS) * CHUNK + lax.rem(lane, CHUNK) + 1
    other = offset + jnp.where(core == 0, count, 0)
    return jnp.where(t < CHUNKS, own, other)


def stats_kernel(kv_ref, own_ref, oth_ref, kc_out, vc_out, stats_out, info_out, k_pack, v_pack):
    chip = lax.axis_index("y") * 4 + lax.axis_index("x")
    core = lax.axis_index("c")
    k_pack[...] = jnp.zeros_like(k_pack)
    v_pack[...] = jnp.zeros_like(v_pack)
    offset = 0
    own_offset = 0
    own_count = 0
    counts = [count_live(kv_ref[s, :, 0:HEAD]) for s in range(CHIPS)]
    for s in range(CHIPS):
        k_pack[pl.ds(offset, SLOTS), :] = kv_ref[s, :, 0:HEAD].astype(F32)
        v_pack[pl.ds(offset, SLOTS), :] = kv_ref[s, :, HEAD : 2 * HEAD].astype(F32)
        info_out[s] = jnp.asarray(offset, jnp.int32)
        own_offset = jnp.where(chip == s, offset, own_offset)
        own_count = jnp.where(chip == s, counts[s], own_count)
        offset = offset + counts[s]
    other_count = 0
    for t in range(CHUNKS):
        other_count += count_live(oth_ref[0, t, 0:CHUNK, :])
    info_out[16] = own_offset
    info_out[17] = own_count
    info_out[18] = other_count
    kc_out[...] = k_pack[0:PICKED, :].astype(BF16)
    vc_out[...] = v_pack[0:PICKED, :].astype(BF16)
    stats_out[...] = jnp.zeros_like(stats_out)
    blocks = lax.div(own_offset + own_count + KEYS - 1, KEYS)
    key_index = lax.broadcasted_iota(jnp.int32, (KEYS, ROWS), 0)

    def attend(t, ref, live_count):
        tt = lax.rem(t, CHUNKS)

        @pl.when(tt * CHUNK < live_count)
        def _():
            limit = row_limit(t, own_offset, own_count, core)
            q_rows = ref[0, tt]
            s_rows = ref[1, tt]

            def step(b, carry):
                top, total, pull = carry
                base = pl.multiple_of(b * KEYS, KEYS)
                scores = nt_dot(kc_out[pl.ds(base, KEYS), :], q_rows) * LOG_FACTOR
                scores = jnp.where(key_index < limit - base, scores, NEGATIVE)
                pushed = nt_dot(vc_out[pl.ds(base, KEYS), :], s_rows)
                new_top = jnp.maximum(top, jnp.max(scores, axis=0, keepdims=True))
                raised = jnp.exp2(scores - new_top)
                fade = jnp.exp2(top - new_top)
                total = total * fade + jnp.sum(raised, axis=0, keepdims=True)
                pull = pull * fade + jnp.sum(raised * pushed, axis=0, keepdims=True)
                return new_top, total, pull

            zero = jnp.zeros((1, ROWS), F32)
            top, total, pull = lax.fori_loop(
                0, blocks, step, (jnp.full((1, ROWS), NEGATIVE, F32), zero, zero)
            )
            stats_out[t, 0:1, :] = top
            stats_out[t, 1:2, :] = total
            stats_out[t, 2:3, :] = pull

    lax.fori_loop(0, CHUNKS, lambda t, _: (attend(t, own_ref, own_count), 0)[1], 0)
    lax.fori_loop(CHUNKS, 2 * CHUNKS, lambda t, _: (attend(t, oth_ref, other_count), 0)[1], 0)


def grad_kernel(
    info_ref,
    kc_ref,
    vc_ref,
    own_ref,
    oth_ref,
    stats_ref,
    peer_ref,
    dkv_out,
    dq_own,
    dq_oth,
    delta_out,
    dk_sum,
    dv_sum,
    dq_sum,
):
    core = lax.axis_index("c")
    own_offset = info_ref[16]
    own_count = info_ref[17]
    other_count = info_ref[18]
    blocks = lax.div(own_offset + own_count + KEYS - 1, KEYS)
    dk_sum[...] = jnp.zeros_like(dk_sum)
    dv_sum[...] = jnp.zeros_like(dv_sum)
    dq_own[...] = jnp.zeros_like(dq_own)
    dq_oth[...] = jnp.zeros_like(dq_oth)
    delta_out[...] = jnp.zeros_like(delta_out)
    key_index = lax.broadcasted_iota(jnp.int32, (KEYS, ROWS), 0)

    def push_back(t, ref, live_count, is_own):
        tt = lax.rem(t, CHUNKS)

        @pl.when(tt * CHUNK < live_count)
        def _():
            limit = row_limit(t, own_offset, own_count, core)
            q_rows = ref[0, tt]
            s_rows = ref[1, tt]
            mine = stats_ref[t]
            theirs = peer_ref[lax.rem(t + CHUNKS, 2 * CHUNKS)]
            top = jnp.maximum(mine[0:1], theirs[0:1])
            mine_scale = jnp.exp2(mine[0:1] - top)
            their_scale = jnp.exp2(theirs[0:1] - top)
            total = mine[1:2] * mine_scale + theirs[1:2] * their_scale
            delta = (mine[2:3] * mine_scale + theirs[2:3] * their_scale) / total
            level = top + jnp.log2(total)
            if is_own:
                half = delta[:, 0:128] + delta[:, 128:256]
                half = half + pltpu.roll(half, 64, 1)
                half = half + pltpu.roll(half, 32, 1)
                lane = lax.broadcasted_iota(jnp.int32, (1, SLOTS), 1)
                delta_out[0:1, :] += jnp.where(lax.div(lane, CHUNK) == tt, half, 0.0)
            dq_sum[...] = jnp.zeros_like(dq_sum)

            def step(b, _):
                base = pl.multiple_of(b * KEYS, KEYS)
                keys = kc_ref[pl.ds(base, KEYS), :]
                scores = nt_dot(keys, q_rows) * LOG_FACTOR
                weights = jnp.where(
                    key_index < limit - base, jnp.exp2(scores - level), 0.0
                )
                pushed = nt_dot(vc_ref[pl.ds(base, KEYS), :], s_rows)
                slopes = (weights * (pushed - delta)).astype(BF16)
                dv_sum[pl.ds(base, KEYS), :] += jnp.dot(
                    weights.astype(BF16), s_rows, preferred_element_type=F32
                )
                dk_sum[pl.ds(base, KEYS), :] += jnp.dot(
                    slopes, q_rows, preferred_element_type=F32
                )
                dq_sum[...] += tn_dot(slopes, keys)
                return 0

            lax.fori_loop(0, blocks, step, 0)
            if is_own:
                dq_own[tt] = dq_sum[...]
            else:
                dq_oth[tt] = dq_sum[...].astype(BF16)

    lax.fori_loop(0, CHUNKS, lambda t, _: (push_back(t, own_ref, own_count, True), 0)[1], 0)
    lax.fori_loop(
        CHUNKS, 2 * CHUNKS, lambda t, _: (push_back(t, oth_ref, other_count, False), 0)[1], 0
    )
    for s in range(CHIPS):
        rows = pl.ds(info_ref[s], SLOTS)
        dkv_out[s, :, 0:HEAD] = dk_sum[rows, :].astype(BF16)
        dkv_out[s, :, HEAD : 2 * HEAD] = dv_sum[rows, :].astype(BF16)


def place_kernel(
    picked_ref, gate_ref, dkv_ref, dq_own, dq_peer, delta_ref, q_out, k_out, v_out, logit_out
):
    placed = place_matrix(picked_ref[...])
    scatter = placed.astype(BF16)
    total = dkv_ref[0].astype(F32)
    for s in range(1, CHIPS):
        total = total + dkv_ref[s].astype(F32)
    k_rows = (total[:, 0:HEAD] * FACTOR).astype(BF16)
    v_rows = total[:, HEAD : 2 * HEAD].astype(BF16)
    k_out[...] = jnp.dot(scatter, k_rows, preferred_element_type=F32).astype(BF16)
    v_out[...] = jnp.dot(scatter, v_rows, preferred_element_type=F32).astype(BF16)
    for h in range(GROUP):
        rows = slice(h * CHUNK, (h + 1) * CHUNK)
        parts = [
            ((dq_own[t, rows, :] + dq_peer[t, rows, :].astype(F32)) * FACTOR).astype(BF16)
            for t in range(CHUNKS)
        ]
        q_out[:, h * HEAD : (h + 1) * HEAD] = jnp.dot(
            scatter, jnp.concatenate(parts, axis=0), preferred_element_type=F32
        ).astype(BF16)
    switch = switch_of(gate_ref[...], placed)
    logit_rows = ((1.0 - switch) * delta_ref[0:1, :]).astype(BF16)
    logit_out[...] = nt_dot(logit_rows, scatter)[0:1].astype(BF16)


def whole(count):
    return [pl.BlockSpec(memory_space=pltpu.VMEM)] * count


def params():
    return pltpu.CompilerParams(vmem_limit_bytes=VMEM_BYTES)


def shape(dims, kind=BF16):
    return jax.ShapeDtypeStruct(dims, kind)


def local(head_queries, key_projection_rows, value_projection_rows, gate_logit, upstream, picked):
    picked_row = picked.reshape(1, SLOTS)
    gate_row = gate_logit.reshape(1, TOKENS)
    swap = [(0, 1), (1, 0)]
    kv_copies, qs_own = pl.pallas_call(
        pick_kernel,
        out_shape=(shape((CHIPS, SLOTS, 2 * HEAD)), shape((2, CHUNKS, ROWS, HEAD))),
        in_specs=whole(6),
        out_specs=tuple(whole(2)),
        compiler_params=params(),
        name="pick",
    )(picked_row, gate_row, key_projection_rows, value_projection_rows, head_queries, upstream)
    qs_peer = lax.ppermute(qs_own, "c", swap)
    kv_all = lax.all_to_all(kv_copies, ("y", "x"), 0, 0, tiled=True)
    kc, vc, stats, info = pl.pallas_call(
        stats_kernel,
        out_shape=(
            shape((PICKED, HEAD)),
            shape((PICKED, HEAD)),
            shape((2 * CHUNKS, 8, ROWS), F32),
            shape((32,), jnp.int32),
        ),
        in_specs=whole(3),
        out_specs=tuple(whole(3)) + (pl.BlockSpec(memory_space=pltpu.SMEM),),
        scratch_shapes=[pltpu.VMEM((PICKED + SLOTS, HEAD), F32)] * 2,
        compiler_params=params(),
        name="stats",
    )(kv_all, qs_own, qs_peer)
    stats_peer = lax.ppermute(stats, "c", swap)
    dkv, dq_own, dq_oth, deltas = pl.pallas_call(
        grad_kernel,
        out_shape=(
            shape((CHIPS, SLOTS, 2 * HEAD)),
            shape((CHUNKS, ROWS, HEAD), F32),
            shape((CHUNKS, ROWS, HEAD)),
            shape((8, SLOTS), F32),
        ),
        in_specs=[pl.BlockSpec(memory_space=pltpu.SMEM)] + whole(6),
        out_specs=tuple(whole(4)),
        scratch_shapes=[
            pltpu.VMEM((PICKED + SLOTS, HEAD), F32),
            pltpu.VMEM((PICKED + SLOTS, HEAD), F32),
            pltpu.VMEM((ROWS, HEAD), F32),
        ],
        compiler_params=params(),
        name="grads",
    )(info, kc, vc, qs_own, qs_peer, stats, stats_peer)
    dq_peer = lax.ppermute(dq_oth, "c", swap)
    delta_totals = lax.psum(deltas, "tp")
    dkv_all = lax.all_to_all(dkv, ("y", "x"), 0, 0, tiled=True)
    q_out, k_out, v_out, logit_out = pl.pallas_call(
        place_kernel,
        out_shape=(
            shape((TOKENS, GROUP * HEAD)),
            shape((TOKENS, HEAD)),
            shape((TOKENS, HEAD)),
            shape((1, TOKENS)),
        ),
        in_specs=whole(6),
        out_specs=tuple(whole(4)),
        compiler_params=params(),
        name="place",
    )(picked_row, gate_row, dkv_all, dq_own, dq_peer, delta_totals)
    return q_out, k_out, v_out, logit_out.reshape(TOKENS)


def solution(mesh):
    split = Mesh(mesh.devices.reshape(4, 4, 2, 8), ("y", "x", "c", "tp"))
    seq = ("y", "x", "c")
    return jax.shard_map(
        local,
        mesh=split,
        in_specs=(P(seq, "tp"), P(seq, "tp"), P(seq, "tp"), P(seq), P(seq, "tp"), P(seq)),
        out_specs=(P(seq, "tp"), P(seq, "tp"), P(seq, "tp"), P(seq)),
        check_vma=False,
    )
```

time: 245 us -> 75.2 us (0.31)
  the two profiles are of different devices: /device:TPU:64 before, /device:TPU:2 now
where the time goes in v1:
time: 75.2 us; the launch traced here: 73.7 us
  blocking collectives  20 us (27%)
  starting transfers between devices  17.9 us (24%)
  waiting for transfers between devices  17 us (23%)
  Pallas kernels  11.9 us (16%)
  local copies, waits for them, and re-layouts  5.59 us (7%)
    psum x1, blocking collectives, local(): delta_totals = lax.psum(deltas, 'tp')  20 us
    all_to_all x1, waiting for transfers between devices, local(): kv_all = lax.all_to_all(kv_copies, ('y', 'x'), 0, 0, tiled=True)  13.9 us
    all_to_all x1, starting transfers between devices, local(): dkv_all = lax.all_to_all(dkv, ('y', 'x'), 0, 0, tiled=True)  9.82 us
    all_to_all x1, starting transfers between devices, local(): kv_all = lax.all_to_all(kv_copies, ('y', 'x'), 0, 0, tiled=True)  7.48 us
    pallas_call x1, Pallas kernels, local(): pl.pallas_call(grad_kernel, out_shape=(shape((CHIPS, SLOTS, 2 * HEAD)), s...  5.39 us
    unnamed x10, local copies, waits for them, and re-layouts  4.91 us
    pallas_call x1, Pallas kernels, local(): pl.pallas_call(stats_kernel, out_shape=(shape((PICKED, HEAD)), shape((PIC...  3.48 us
    ppermute x1, waiting for transfers between devices, local(): qs_peer = lax.ppermute(qs_own, 'c', swap)  1.9 us
  transfers between devices with their start and end apart: 5, of which 3 were waited for; matrix products, arithmetic and copies ran while one was open for 0% of the time, Pallas kernels for 0%

profile of v1, /device:TPU:2, one launch (start us, length us, event | category | flops | bytes accessed | tf_op | source)
XLA Modules:
  0.0 73.7 jit_solution(11800895110866843037)
XLA Ops:
  0.6 0.7 reshape.18.gate_ref
  1.3 0.0 copy-start.4
  1.3 0.7 copy-done.4
  2.0 0.0 copy-start
  2.0 1.2 %copy-done = bf16[512,1024]{1,0:T(8,128)(2,1)S(1)} copy-done((bf16[512,1024]{1,0:T(8,128)(2,1)S(1)}, bf16[512,1024]{1,0:T(8,128)(2,1)}, u32[]{:S(2)}) %copy-start) | copy-done | bytes 1048600
  3.2 0.0 copy-start.1
  3.2 1.2 %copy-done.1 = bf16[512,1024]{1,0:T(8,128)(2,1)S(1)} copy-done((bf16[512,1024]{1,0:T(8,128)(2,1)S(1)}, bf16[512,1024]{1,0:T(8,128)(2,1)}, u32[]{:S(2)}) %copy-start.1) | copy-done | bytes 1048600
  4.4 0.0 copy-start.2
  4.4 0.9 %copy-done.2 = bf16[512,128]{1,0:T(8,128)(2,1)S(1)} copy-done((bf16[512,128]{1,0:T(8,128)(2,1)S(1)}, bf16[512,128]{1,0:T(8,128)(2,1)}, u32[]{:S(2)}) %copy-start.2) | copy-done | bytes 131096
  5.3 0.0 copy-start.3
  5.3 0.9 %copy-done.3 = bf16[512,128]{1,0:T(8,128)(2,1)S(1)} copy-done((bf16[512,128]{1,0:T(8,128)(2,1)S(1)}, bf16[512,128]{1,0:T(8,128)(2,1)}, u32[]{:S(2)}) %copy-start.3) | copy-done | bytes 131096
  6.2 1.4 %pick.1 = (bf16[16,128,256]{2,1,0:T(8,128)(2,1)}, bf16[2,4,256,128]{3,2,1,0:T(8,128)(2,1)S(1)}) custom-call(s32[1,128]{1,0:T(1,128)S(1)} %bitcast.1, bf16[1,512]{1,0:T(2,128)(2,1)S(1)} %reshape.18.gate_ref, bf16[512,128]{1,0:T(8,128)(2,1)S(1)} %copy-done.2, bf16[512,128]{1,0:T(8,128)(2,1)S(1)} %copy-done.3, bf16[512,1024]{1,0:T(8,128)(2,1)S(1)} %copy-done, ...), custom_call_target="tpu_custom_call" | custom-call | tf_op jit(solution)/shard_map/pick/pallas_call | solution.py:282
  7.7 7.5 %all-to-all-start = ((bf16[16,128,256]{2,1,0:T(8,128)(2,1)}), bf16[16,128,256]{2,1,0:T(8,128)(2,1)S(1)}, u32[]{:S(2)}, u32[]{:S(2)}) async-start(bf16[16,128,256]{2,1,0:T(8,128)(2,1)} %get-tuple-element.18), calls=%async_computation | async-start | bytes 2097152 | tf_op jit(solution)/shard_map/all_to_all | solution.py:291
  15.1 0.0 collective-permute-start
  15.1 1.9 %collective-permute-done.oth_ref = bf16[2,4,256,128]{3,2,1,0:T(8,128)(2,1)S(1)} collective-permute-done((bf16[2,4,256,128]{3,2,1,0:T(8,128)(2,1)S(1)}, bf16[2,4,256,128]{3,2,1,0:T(8,128)(2,1)S(1)}, u32[]{:S(2)}, u32[]{:S(2)}) %collective-permute-start) | collective-permute-done | bytes 524320 | tf_op jit(solution)/shard_map/ppermute | solution.py:290
  17.0 13.9 %all-to-all-done.kv_ref = bf16[16,128,256]{2,1,0:T(8,128)(2,1)S(1)} async-done(((bf16[16,128,256]{2,1,0:T(8,128)(2,1)}), bf16[16,128,256]{2,1,0:T(8,128)(2,1)S(1)}, u32[]{:S(2)}, u32[]{:S(2)}) %all-to-all-start) | async-done | bytes 1048608 | tf_op jit(solution)/shard_map/all_to_all | solution.py:291
  30.9 3.5 %stats.1 = (bf16[2048,128]{1,0:T(8,128)(2,1)S(1)}, bf16[2048,128]{1,0:T(8,128)(2,1)S(1)}, f32[8,8,256]{2,1,0:T(8,128)S(1)}, s32[32]{0:T(128)S(1)}) custom-call(bf16[16,128,256]{2,1,0:T(8,128)(2,1)S(1)} %all-to-all-done.kv_ref, bf16[2,4,256,128]{3,2,1,0:T(8,128)(2,1)S(1)} %get-tuple-element.19.own_ref, bf16[2,4,256,128]{3,2,1,0:T(8,128)(2,1)S(1)} %collective-permute-done.oth_ref), custom_call_target="tpu_custom_call" | custom-call | tf_op jit(solution)/shard_map/stats/pallas_call | solution.py:292
  34.4 0.1 collective-permute-start.1
  34.5 1.2 %collective-permute-done.1.peer_ref = f32[8,8,256]{2,1,0:T(8,128)S(1)} collective-permute-done((f32[8,8,256]{2,1,0:T(8,128)S(1)}, f32[8,8,256]{2,1,0:T(8,128)S(1)}, u32[]{:S(2)}, u32[]{:S(2)}) %collective-permute-start.1) | collective-permute-done | bytes 65568 | tf_op jit(solution)/shard_map/ppermute | solution.py:306
  35.8 5.4 %grads.1 = (bf16[16,128,256]{2,1,0:T(8,128)(2,1)}, f32[4,256,128]{2,1,0:T(8,128)S(1)}, bf16[4,256,128]{2,1,0:T(8,128)(2,1)S(1)}, f32[8,128]{1,0:T(8,128)S(1)}) custom-call(s32[32]{0:T(128)S(1)} %get-tuple-element.20.info_ref, bf16[2048,128]{1,0:T(8,128)(2,1)S(1)} %get-tuple-element.21.kc_ref, bf16[2048,128]{1,0:T(8,128)(2,1)S(1)} %get-tuple-element.22.vc_ref, ...), custom_call_target="tpu_custom_call" | custom-call | tf_op jit(solution)/shard_map/grads/pallas_call | solution.py:307
  41.1 9.8 %all-to-all-start.1 = ((bf16[16,128,256]{2,1,0:T(8,128)(2,1)}), bf16[16,128,256]{2,1,0:T(8,128)(2,1)S(1)}, u32[]{:S(2)}, u32[]{:S(2)}) async-start(bf16[16,128,256]{2,1,0:T(8,128)(2,1)} %get-tuple-element.24), calls=%async_computation.1 | async-start | bytes 2097152 | tf_op jit(solution)/shard_map/all_to_all | solution.py:327
  51.0 0.5 collective-permute-start.2
  51.5 20.0 %psum.7.delta_ref = f32[8,128]{1,0:T(8,128)S(1)} all-reduce(f32[8,128]{1,0:T(8,128)S(1)} %get-tuple-element.27), channel_id=1, replica_groups=mesh['y'=4,'x'=4,'c'=2,'tp'=8] {'tp'}, use_global_device_ids=true, to_apply=%region_0.0 | all-reduce | flops 1024 | bytes 8192 | tf_op jit(solution)/shard_map/psum | solution.py:326
  71.5 0.0 collective-permute-done.2.dq_peer
  71.5 0.0 all-to-all-done.1.dkv_ref
  71.5 1.6 %place.1 = (bf16[512,1024]{1,0:T(8,128)(2,1)}, bf16[512,128]{1,0:T(8,128)(2,1)}, bf16[512,128]{1,0:T(8,128)(2,1)}, bf16[1,512]{1,0:T(2,128)(2,1)S(1)}) custom-call(s32[1,128]{1,0:T(1,128)S(1)} %bitcast.2, bf16[1,512]{1,0:T(2,128)(2,1)S(1)} %reshape.18.gate_ref, bf16[16,128,256]{2,1,0:T(8,128)(2,1)S(1)} %all-to-all-done.1.dkv_ref, ...), custom_call_target="tpu_custom_call" | custom-call | tf_op jit(solution)/shard_map/place/pallas_call | solution.py:328
  73.1 0.6 reduce
Async XLA Ops:
  1.3 0.7 copy-start.4
  2.0 1.2 %copy-start = (bf16[512,1024]{1,0:T(8,128)(2,1)S(1)}, bf16[512,1024]{1,0:T(8,128)(2,1)}, u32[]{:S(2)}) copy-start(bf16[512,1024]{1,0:T(8,128)(2,1)} %q_ref.1) | copy-start | bytes 3145732
  3.2 1.2 %copy-start.1 = (bf16[512,1024]{1,0:T(8,128)(2,1)S(1)}, bf16[512,1024]{1,0:T(8,128)(2,1)}, u32[]{:S(2)}) copy-start(bf16[512,1024]{1,0:T(8,128)(2,1)} %up_ref.1) | copy-start | bytes 3145732
  4.4 0.9 %copy-start.2 = (bf16[512,128]{1,0:T(8,128)(2,1)S(1)}, bf16[512,128]{1,0:T(8,128)(2,1)}, u32[]{:S(2)}) copy-start(bf16[512,128]{1,0:T(8,128)(2,1)} %k_ref.1) | copy-start | bytes 393220
  5.3 0.9 %copy-start.3 = (bf16[512,128]{1,0:T(8,128)(2,1)S(1)}, bf16[512,128]{1,0:T(8,128)(2,1)}, u32[]{:S(2)}) copy-start(bf16[512,128]{1,0:T(8,128)(2,1)} %v_ref.1) | copy-start | bytes 393220
  7.7 23.3 %all-to-all-start = ((bf16[16,128,256]{2,1,0:T(8,128)(2,1)}), bf16[16,128,256]{2,1,0:T(8,128)(2,1)S(1)}, u32[]{:S(2)}, u32[]{:S(2)}) async-start(bf16[16,128,256]{2,1,0:T(8,128)(2,1)} %get-tuple-element.18), calls=%async_computation | async-start | bytes 2097152 | tf_op jit(solution)/shard_map/all_to_all | solution.py:291
  15.1 1.9 %collective-permute-start = (bf16[2,4,256,128]{3,2,1,0:T(8,128)(2,1)S(1)}, bf16[2,4,256,128]{3,2,1,0:T(8,128)(2,1)S(1)}, u32[]{:S(2)}, u32[]{:S(2)}) collective-permute-start(bf16[2,4,256,128]{3,2,1,0:T(8,128)(2,1)S(1)} %get-tuple-element.19.own_ref), channel_id=1, source_target_pairs={{0,8},{8,0},{1,9},{9,1},{2,10},{10,2},{3,11},{11,3},{4,12},{12,4},... | collective-permute-start | bytes 1572872 | tf_op jit(solution)/shard_map/ppermute | solution.py:290
  34.4 1.3 %collective-permute-start.1 = (f32[8,8,256]{2,1,0:T(8,128)S(1)}, f32[8,8,256]{2,1,0:T(8,128)S(1)}, u32[]{:S(2)}, u32[]{:S(2)}) collective-permute-start(f32[8,8,256]{2,1,0:T(8,128)S(1)} %get-tuple-element.23.stats_ref), channel_id=1, source_target_pairs={{0,8},{8,0},{1,9},{9,1},{2,10},{10,2},{3,11},{11,3},{4,12},{12,4},... | collective-permute-start | bytes 196616 | tf_op jit(solution)/shard_map/ppermute | solution.py:306
  41.1 30.3 %all-to-all-start.1 = ((bf16[16,128,256]{2,1,0:T(8,128)(2,1)}), bf16[16,128,256]{2,1,0:T(8,128)(2,1)S(1)}, u32[]{:S(2)}, u32[]{:S(2)}) async-start(bf16[16,128,256]{2,1,0:T(8,128)(2,1)} %get-tuple-element.24), calls=%async_computation.1 | async-start | bytes 2097152 | tf_op jit(solution)/shard_map/all_to_all | solution.py:327
  51.0 20.5 %collective-permute-start.2 = (bf16[4,256,128]{2,1,0:T(8,128)(2,1)S(1)}, bf16[4,256,128]{2,1,0:T(8,128)(2,1)S(1)}, u32[]{:S(2)}, u32[]{:S(2)}) collective-permute-start(bf16[4,256,128]{2,1,0:T(8,128)(2,1)S(1)} %get-tuple-element.26), channel_id=1, source_target_pairs={{0,8},{8,0},{1,9},{9,1},{2,10},{10,2},{3,11},{11,3},{4,12},{12,4},... | collective-permute-start | bytes 786440 | tf_op jit(solution)/shard_map/ppermute | solution.py:325

commit v2 on v1

v2 whole, which is shorter than its diff:
```python
import functools
import math

import jax
import jax.numpy as jnp
from jax import lax
from jax.experimental import pallas as pl
from jax.experimental.pallas import tpu as pltpu
from jax.sharding import Mesh, PartitionSpec as P

QUERY_HEADS = 64
KEY_VALUE_HEADS = 8
HEAD = 128
SLOTS = 128
TOKENS = 512
CHIPS = 16
PICKED = 2048
GROUP = QUERY_HEADS // KEY_VALUE_HEADS
FACTOR = 1.0 / math.sqrt(HEAD)
LOG_FACTOR = FACTOR * math.log2(math.e)
CHUNK = 32
CHUNKS = SLOTS // CHUNK
ROWS = GROUP * CHUNK
KEYS = 512
EDGE = 256
PART = 128
SPARE = 2 * CHUNKS
SENTINEL = 128.0
LIVE_BELOW = 32.0
NEGATIVE = -1e30
F32 = jnp.float32
BF16 = jnp.bfloat16
VMEM_BYTES = 48 * 1024 * 1024
VMEM_ALL = 64 * 1024 * 1024


def nt_dot(a, b):
    return lax.dot_general(a, b, (((1,), (1,)), ((), ())), preferred_element_type=F32)


def tn_dot(a, b):
    return lax.dot_general(a, b, (((0,), (0,)), ((), ())), preferred_element_type=F32)


def place_matrix(picked):
    token = lax.broadcasted_iota(jnp.int32, (TOKENS, SLOTS), 0)
    return jnp.where(token == picked, 1.0, 0.0).astype(F32)


def switch_of(gate, gather):
    rows = jnp.dot(
        jnp.broadcast_to(gate, (16, TOKENS)), gather.astype(BF16), preferred_element_type=F32
    )
    return 1.0 / (1.0 + jnp.exp(-rows))


def dead_column(picked):
    dead = jnp.where(picked >= TOKENS, SENTINEL, 0.0).astype(F32)
    return jnp.broadcast_to(dead, (SLOTS, SLOTS)).T


def fetch(pairs, sems):
    copies = [pltpu.make_async_copy(src, dst, sems.at[n]) for n, (src, dst) in enumerate(pairs)]
    for copy in copies:
        copy.start()
    for copy in copies:
        copy.wait()


def pick_kv_kernel(picked_hbm, k_hbm, v_hbm, kv_out, picked_ref, k_ref, v_ref, message, sems, out_sems):
    fetch([(picked_hbm, picked_ref), (k_hbm, k_ref), (v_hbm, v_ref)], sems)
    gather = place_matrix(picked_ref[...]).T.astype(BF16)
    keys = jnp.dot(gather, k_ref[...], preferred_element_type=F32)
    message[:, 0:HEAD] = (keys + dead_column(picked_ref[...])).astype(BF16)
    message[:, HEAD : 2 * HEAD] = jnp.dot(
        gather, v_ref[...], preferred_element_type=F32
    ).astype(BF16)
    fetch([(message, kv_out.at[chip]) for chip in range(CHIPS)], out_sems)


def pick_q_kernel(picked_hbm, gate_ref, q_hbm, up_hbm, qs_out, picked_ref, q_ref, up_ref, sems):
    fetch([(picked_hbm, picked_ref), (q_hbm, q_ref), (up_hbm, up_ref)], sems)
    placed = place_matrix(picked_ref[...])
    gather = placed.T.astype(BF16)
    switch = jnp.broadcast_to(switch_of(gate_ref[...], placed)[0:1], (SLOTS, SLOTS)).T
    for h in range(GROUP):
        lanes = slice(h * HEAD, (h + 1) * HEAD)
        q_rows = jnp.dot(gather, q_ref[:, lanes], preferred_element_type=F32).astype(BF16)
        up_rows = jnp.dot(gather, up_ref[:, lanes], preferred_element_type=F32)
        scaled = (up_rows * switch).astype(BF16)
        for t in range(CHUNKS):
            rows = slice(t * CHUNK, (t + 1) * CHUNK)
            qs_out[0, t, h * CHUNK : (h + 1) * CHUNK, :] = q_rows[rows]
            qs_out[1, t, h * CHUNK : (h + 1) * CHUNK, :] = scaled[rows]


def count_live(block):
    live = jnp.where(block.astype(F32) < LIVE_BELOW, 1.0, 0.0)
    return jnp.sum(live, axis=0, keepdims=True)[0, 0].astype(jnp.int32)


class Tiles:
    def __init__(self, core, offset, count, own_chunks, live_chunks):
        self.offset, self.count = offset, count
        self.own_chunks, self.live_chunks = own_chunks, live_chunks
        self.other_limit = offset + jnp.where(core == 0, count, 0)
        self.number = lax.div(live_chunks + 1, 2)

    def place(self, chunk):
        place = jnp.where(chunk < self.own_chunks, chunk, CHUNKS + chunk - self.own_chunks)
        return jnp.where(chunk < self.live_chunks, place, SPARE)

    def limit(self, chunk):
        slot = lax.rem(lax.broadcasted_iota(jnp.int32, (1, ROWS), 1), CHUNK)
        own = self.offset + chunk * CHUNK + 1
        step = jnp.where(chunk < self.own_chunks, 1, 0)
        return jnp.where(chunk < self.own_chunks, own, self.other_limit) + slot * step

    def bounds(self, chunk):
        own = chunk < self.own_chunks
        first = self.offset + chunk * CHUNK
        last = jnp.minimum(first + CHUNK, self.offset + self.count)
        return jnp.where(own, first + 1, self.other_limit), jnp.where(own, last, self.other_limit)

    def spans(self, tile):
        low_a, high_a = self.bounds(2 * tile)
        low_b, high_b = self.bounds(2 * tile + 1)
        paired = 2 * tile + 1 < self.live_chunks
        low = jnp.where(paired, jnp.minimum(low_a, low_b), low_a)
        high = jnp.where(paired, jnp.maximum(high_a, high_b), high_a)
        full = lax.div(low, KEYS)
        return full, lax.div(high - full * KEYS + EDGE - 1, EDGE)

    def limits(self, tile):
        return jnp.concatenate([self.limit(2 * tile), self.limit(2 * tile + 1)], axis=1)

    def sweep(self, tile, block, carry):
        full, edges = self.spans(tile)
        limits = self.limits(tile)
        start = full * KEYS
        carry = lax.fori_loop(
            0, full, lambda b, c: block(pl.multiple_of(b * KEYS, KEYS), KEYS, None, c), carry
        )
        return lax.fori_loop(
            0,
            edges,
            lambda b, c: block(pl.multiple_of(start + b * EDGE, EDGE), EDGE, limits, c),
            carry,
        )


def pair_rows(tile):
    return pl.ds(pl.multiple_of(tile * 2 * ROWS, 2 * ROWS), 2 * ROWS)


def stats_kernel(
    peer_picked, kv_ref, own_ref, oth_ref, kc_out, vc_out, q_out, s_out, stats_out, info_out,
    k_pack, v_pack,
):
    chip = lax.axis_index("y") * 4 + lax.axis_index("x")
    core = lax.axis_index("c")
    k_pack[...] = jnp.zeros_like(k_pack)
    v_pack[...] = jnp.zeros_like(v_pack)
    q_out[...] = jnp.zeros_like(q_out)
    s_out[...] = jnp.zeros_like(s_out)
    stats_out[...] = jnp.zeros_like(stats_out)
    offset = 0
    own_offset = 0
    own_count = 0
    counts = [count_live(kv_ref[s, :, 0:HEAD]) for s in range(CHIPS)]
    for s in range(CHIPS):
        k_pack[pl.ds(offset, SLOTS), :] = kv_ref[s, :, 0:HEAD].astype(F32)
        v_pack[pl.ds(offset, SLOTS), :] = kv_ref[s, :, HEAD : 2 * HEAD].astype(F32)
        info_out[s] = jnp.asarray(offset, jnp.int32)
        own_offset = jnp.where(chip == s, offset, own_offset)
        own_count = jnp.where(chip == s, counts[s], own_count)
        offset = offset + counts[s]
    peer_live = jnp.where(peer_picked[...] < TOKENS, 1.0, 0.0)
    other_count = jnp.sum(peer_live, axis=1, keepdims=True)[0, 0].astype(jnp.int32)
    own_chunks = lax.div(own_count + CHUNK - 1, CHUNK)
    live_chunks = own_chunks + lax.div(other_count + CHUNK - 1, CHUNK)
    info_out[16] = own_offset
    info_out[17] = own_count
    info_out[18] = own_chunks
    info_out[19] = live_chunks
    kc_out[...] = k_pack[0:PICKED, :].astype(BF16)
    vc_out[...] = v_pack[0:PICKED, :].astype(BF16)
    for t in range(CHUNKS):
        q_out[t * ROWS : (t + 1) * ROWS, :] = own_ref[0, t]
        s_out[t * ROWS : (t + 1) * ROWS, :] = own_ref[1, t]
    for t in range(CHUNKS):
        rows = pl.ds(pl.multiple_of((own_chunks + t) * ROWS, ROWS), ROWS)
        q_out[rows, :] = oth_ref[0, t]
        s_out[rows, :] = oth_ref[1, t]
    tiles = Tiles(core, own_offset, own_count, own_chunks, live_chunks)

    def attend(tile, _):
        q_rows = q_out[pair_rows(tile), :]
        s_rows = s_out[pair_rows(tile), :]

        def block(base, keys, limits, carry):
            top, total, pull = carry
            scores = nt_dot(kc_out[pl.ds(base, keys), :], q_rows)
            pushed = nt_dot(vc_out[pl.ds(base, keys), :], s_rows)
            for u in range(0, keys, PART):
                part = scores[u : u + PART] * LOG_FACTOR
                if limits is not None:
                    index = lax.broadcasted_iota(jnp.int32, (PART, 2 * ROWS), 0)
                    part = jnp.where(index < limits - (base + u), part, NEGATIVE)
                part = part.reshape(PART // 8, 8, 2 * ROWS)
                new_top = jnp.maximum(top, jnp.max(part, axis=0))
                raised = jnp.exp2(part - new_top[None])
                fade = jnp.exp2(top - new_top)
                total = total * fade + jnp.sum(raised, axis=0)
                pulled = raised * pushed[u : u + PART].reshape(PART // 8, 8, 2 * ROWS)
                pull = pull * fade + jnp.sum(pulled, axis=0)
                top = new_top
            return top, total, pull

        zero = jnp.zeros((8, 2 * ROWS), F32)
        top, total, pull = tiles.sweep(
            tile, block, (jnp.full((8, 2 * ROWS), NEGATIVE, F32), zero, zero)
        )
        best = jnp.max(top, axis=0, keepdims=True)
        fade = jnp.exp2(top - best)
        total = jnp.sum(total * fade, axis=0, keepdims=True)
        pull = jnp.sum(pull * fade, axis=0, keepdims=True)
        for half in range(2):
            place = tiles.place(2 * tile + half)
            lanes = slice(half * ROWS, (half + 1) * ROWS)
            stats_out[place, 0:1, :] = best[:, lanes]
            stats_out[place, 1:2, :] = total[:, lanes]
            stats_out[place, 2:3, :] = pull[:, lanes]
        return 0

    lax.fori_loop(0, tiles.number, attend, 0)


def combine_kernel(info_ref, stats_ref, peer_ref, comb_out, delta_out):
    own_chunks = info_ref[18]
    lane = lax.div(lax.broadcasted_iota(jnp.int32, (1, SLOTS), 1), CHUNK)
    comb_out[SPARE] = jnp.zeros((8, ROWS), F32)
    deltas = jnp.zeros((1, SLOTS), F32)
    for place in range(SPARE):
        mine = stats_ref[place]
        theirs = peer_ref[(place + CHUNKS) % SPARE]
        top = jnp.maximum(mine[0:1], theirs[0:1])
        mine_scale = jnp.exp2(mine[0:1] - top)
        their_scale = jnp.exp2(theirs[0:1] - top)
        total = mine[1:2] * mine_scale + theirs[1:2] * their_scale
        total = jnp.where(total > 0.0, total, 1.0)
        delta = (mine[2:3] * mine_scale + theirs[2:3] * their_scale) / total
        comb_out[place, 0:1, :] = top + jnp.log2(total)
        comb_out[place, 1:2, :] = delta
        if place < CHUNKS:
            heads = delta[:, 0:128] + delta[:, 128:256]
            heads = heads + pltpu.roll(heads, 64, 1)
            heads = heads + pltpu.roll(heads, 32, 1)
            mark = jnp.where(place < own_chunks, place, CHUNKS)
            deltas = deltas + jnp.where(lane == mark, heads, 0.0)
    delta_out[...] = jnp.broadcast_to(deltas, (8, SLOTS))


def grad_kernel(
    info_ref, kc_ref, vc_ref, q_ref, s_ref, comb_ref, dkv_out, dq_own, dq_oth,
    dk_sum, dv_sum, dq_sum,
):
    core = lax.axis_index("c")
    tiles = Tiles(core, info_ref[16], info_ref[17], info_ref[18], info_ref[19])
    dk_sum[...] = jnp.zeros_like(dk_sum)
    dv_sum[...] = jnp.zeros_like(dv_sum)
    dq_own[...] = jnp.zeros_like(dq_own)
    dq_oth[...] = jnp.zeros_like(dq_oth)

    def push_back(tile, _):
        q_rows = q_ref[pair_rows(tile), :]
        s_rows = s_ref[pair_rows(tile), :]
        chunks = (2 * tile, 2 * tile + 1)
        comb = jnp.concatenate([comb_ref[tiles.place(c)] for c in chunks], axis=1)
        level, delta = comb[0:1], comb[1:2]
        dq_sum[...] = jnp.zeros_like(dq_sum)

        def block(base, keys, limits, carry):
            span = pl.ds(base, keys)
            key_rows = kc_ref[span, :]
            scores = nt_dot(key_rows, q_rows)
            pushed = nt_dot(vc_ref[span, :], s_rows)
            weights = jnp.exp2(scores * LOG_FACTOR - level)
            if limits is not None:
                index = lax.broadcasted_iota(jnp.int32, (keys, 2 * ROWS), 0)
                weights = jnp.where(index < limits - base, weights, 0.0)
            slopes = (weights * (pushed - delta)).astype(BF16)
            dv_sum[span, :] += jnp.dot(
                weights.astype(BF16), s_rows, preferred_element_type=F32
            )
            dk_sum[span, :] += jnp.dot(slopes, q_rows, preferred_element_type=F32)
            dq_sum[...] += tn_dot(slopes, key_rows)
            return carry

        tiles.sweep(tile, block, 0)
        for half, chunk in enumerate(chunks):
            rows = slice(half * ROWS, (half + 1) * ROWS)

            @pl.when(chunk < tiles.own_chunks)
            def _():
                dq_own[chunk] = dq_sum[rows, :]

            @pl.when((chunk >= tiles.own_chunks) & (chunk < tiles.live_chunks))
            def _():
                dq_oth[chunk - tiles.own_chunks] = dq_sum[rows, :].astype(BF16)

        return 0

    lax.fori_loop(0, tiles.number, push_back, 0)
    for s in range(CHIPS):
        rows = pl.ds(info_ref[s], SLOTS)
        dkv_out[s, :, 0:HEAD] = dk_sum[rows, :].astype(BF16)
        dkv_out[s, :, HEAD : 2 * HEAD] = dv_sum[rows, :].astype(BF16)


def place_q_kernel(picked_ref, gate_ref, dq_own, dq_peer, q_out, closed_out):
    placed = place_matrix(picked_ref[...])
    scatter = placed.astype(BF16)
    closed_out[...] = 1.0 - switch_of(gate_ref[...], placed)
    for h in range(GROUP):
        rows = slice(h * CHUNK, (h + 1) * CHUNK)
        parts = [
            ((dq_own[t, rows, :] + dq_peer[t, rows, :].astype(F32)) * FACTOR).astype(BF16)
            for t in range(CHUNKS)
        ]
        q_out[:, h * HEAD : (h + 1) * HEAD] = jnp.dot(
            scatter, jnp.concatenate(parts, axis=0), preferred_element_type=F32
        ).astype(BF16)


def place_logit_kernel(picked_ref, closed_ref, delta_half, delta_rest, logit_out):
    scatter = place_matrix(picked_ref[...]).astype(BF16)
    deltas = delta_half[0:1, :] + delta_rest[0:1, :]
    logit_rows = (closed_ref[...] * deltas).astype(BF16)
    logit_out[...] = nt_dot(logit_rows, scatter)[0:1].astype(BF16)


def place_kv_kernel(picked_ref, dkv_ref, k_out, v_out):
    scatter = place_matrix(picked_ref[...]).astype(BF16)
    total = dkv_ref[0].astype(F32)
    for s in range(1, CHIPS):
        total = total + dkv_ref[s].astype(F32)
    k_rows = (total[:, 0:HEAD] * FACTOR).astype(BF16)
    v_rows = total[:, HEAD : 2 * HEAD].astype(BF16)
    k_out[...] = jnp.dot(scatter, k_rows, preferred_element_type=F32).astype(BF16)
    v_out[...] = jnp.dot(scatter, v_rows, preferred_element_type=F32).astype(BF16)


def whole(count):
    return [pl.BlockSpec(memory_space=pltpu.VMEM)] * count


def params(limit=VMEM_BYTES):
    return pltpu.CompilerParams(vmem_limit_bytes=limit)


def shape(dims, kind=BF16):
    return jax.ShapeDtypeStruct(dims, kind)


def hbm(count):
    return [pl.BlockSpec(memory_space=pltpu.HBM)] * count


def cost(flops):
    return pl.CostEstimate(flops=flops, bytes_accessed=1 << 20, transcendentals=0)


def local(head_queries, key_projection_rows, value_projection_rows, gate_logit, upstream, picked):
    picked_row = picked.reshape(1, SLOTS)
    swap = [(0, 1), (1, 0)]
    kv_copies = pl.pallas_call(
        pick_kv_kernel,
        out_shape=shape((CHIPS, SLOTS, 2 * HEAD)),
        in_specs=hbm(3),
        out_specs=hbm(1)[0],
        scratch_shapes=[
            pltpu.VMEM((1, SLOTS), jnp.int32),
            pltpu.VMEM((TOKENS, HEAD), BF16),
            pltpu.VMEM((TOKENS, HEAD), BF16),
            pltpu.VMEM((SLOTS, 2 * HEAD), BF16),
            pltpu.SemaphoreType.DMA((3,)),
            pltpu.SemaphoreType.DMA((CHIPS,)),
        ],
        compiler_params=params(VMEM_ALL),
        name="pick_kv",
    )(picked_row, key_projection_rows, value_projection_rows)
    kv_all = lax.all_to_all(kv_copies, ("y", "x"), 0, 0, tiled=True)
    gate_row = gate_logit.reshape(1, TOKENS)
    qs_own = pl.pallas_call(
        pick_q_kernel,
        out_shape=shape((2, CHUNKS, ROWS, HEAD)),
        in_specs=hbm(1) + whole(1) + hbm(2),
        out_specs=whole(1)[0],
        scratch_shapes=[
            pltpu.VMEM((1, SLOTS), jnp.int32),
            pltpu.VMEM((TOKENS, GROUP * HEAD), BF16),
            pltpu.VMEM((TOKENS, GROUP * HEAD), BF16),
            pltpu.SemaphoreType.DMA((3,)),
        ],
        compiler_params=params(),
        cost_estimate=cost(1 << 30),
        name="pick_q",
    )(picked_row, gate_row, head_queries, upstream)
    qs_peer = lax.ppermute(qs_own, "c", swap)
    peer_picked = lax.ppermute(picked_row, "c", swap)
    kc, vc, q_rows, s_rows, stats, info = pl.pallas_call(
        stats_kernel,
        out_shape=(
            shape((PICKED, HEAD)),
            shape((PICKED, HEAD)),
            shape((2 * CHUNKS * ROWS, HEAD)),
            shape((2 * CHUNKS * ROWS, HEAD)),
            shape((SPARE + 1, 8, ROWS), F32),
            shape((32,), jnp.int32),
        ),
        in_specs=whole(4),
        out_specs=tuple(whole(5)) + (pl.BlockSpec(memory_space=pltpu.SMEM),),
        scratch_shapes=[pltpu.VMEM((PICKED + SLOTS, HEAD), F32)] * 2,
        compiler_params=params(),
        name="stats",
    )(peer_picked, kv_all, qs_own, qs_peer)
    stats_peer = lax.ppermute(stats, "c", swap)
    comb, deltas = pl.pallas_call(
        combine_kernel,
        out_shape=(shape((SPARE + 1, 8, ROWS), F32), shape((8, SLOTS), F32)),
        in_specs=[pl.BlockSpec(memory_space=pltpu.SMEM)] + whole(2),
        out_specs=tuple(whole(2)),
        compiler_params=params(),
        name="combine",
    )(info, stats, stats_peer)
    delta_near = lax.ppermute(deltas, "tp", [(i, i ^ 1) for i in range(8)])
    dkv, dq_own, dq_oth = pl.pallas_call(
        grad_kernel,
        out_shape=(
            shape((CHIPS, SLOTS, 2 * HEAD)),
            shape((CHUNKS, ROWS, HEAD), F32),
            shape((CHUNKS, ROWS, HEAD)),
        ),
        in_specs=[pl.BlockSpec(memory_space=pltpu.SMEM)] + whole(5),
        out_specs=tuple(whole(3)),
        scratch_shapes=[
            pltpu.VMEM((PICKED + SLOTS, HEAD), F32),
            pltpu.VMEM((PICKED + SLOTS, HEAD), F32),
            pltpu.VMEM((2 * ROWS, HEAD), F32),
        ],
        compiler_params=params(),
        cost_estimate=cost(1 << 32),
        name="grads",
    )(info, kc, vc, q_rows, s_rows, comb)
    dkv, delta_near = lax.optimization_barrier((dkv, delta_near))
    dkv_all = lax.all_to_all(dkv, ("y", "x"), 0, 0, tiled=True)
    delta_pair = deltas + delta_near
    delta_half = delta_pair + lax.ppermute(delta_pair, "tp", [(i, i ^ 2) for i in range(8)])
    delta_rest = lax.ppermute(delta_half, "tp", [(i, i ^ 4) for i in range(8)])
    dq_peer = lax.ppermute(dq_oth, "c", swap)
    q_out, closed = pl.pallas_call(
        place_q_kernel,
        out_shape=(shape((TOKENS, GROUP * HEAD)), shape((16, SLOTS), F32)),
        in_specs=whole(4),
        out_specs=tuple(whole(2)),
        compiler_params=params(),
        cost_estimate=cost(1 << 29),
        name="place_q",
    )(picked_row, gate_row, dq_own, dq_peer)
    logit_out = pl.pallas_call(
        place_logit_kernel,
        out_shape=shape((1, TOKENS)),
        in_specs=whole(4),
        out_specs=whole(1)[0],
        compiler_params=params(),
        cost_estimate=cost(1 << 28),
        name="place_logit",
    )(picked_row, closed, delta_half, delta_rest)
    k_out, v_out = pl.pallas_call(
        place_kv_kernel,
        out_shape=(shape((TOKENS, HEAD)), shape((TOKENS, HEAD))),
        in_specs=whole(2),
        out_specs=tuple(whole(2)),
        compiler_params=params(),
        name="place_kv",
    )(picked_row, dkv_all)
    return q_out, k_out, v_out, logit_out.reshape(TOKENS)


def solution(mesh):
    split = Mesh(mesh.devices.reshape(4, 4, 2, 8), ("y", "x", "c", "tp"))
    seq = ("y", "x", "c")
    return jax.shard_map(
        local,
        mesh=split,
        in_specs=(P(seq, "tp"), P(seq, "tp"), P(seq, "tp"), P(seq), P(seq, "tp"), P(seq)),
        out_specs=(P(seq, "tp"), P(seq, "tp"), P(seq, "tp"), P(seq)),
        check_vma=False,
    )
```

time: 75.2 us -> 66.6 us (0.89)
  the two profiles are of different devices: /device:TPU:2 before, /device:TPU:64 now
where the time goes in v2:
time: 66.6 us; the launch traced here: 65.6 us
  waiting for transfers between devices  25.2 us (38%)
  starting transfers between devices  23.9 us (36%)
  Pallas kernels  13.3 us (20%)
  local copies, waits for them, and re-layouts  1.87 us (3%)
  between operations  0.77 us (1%)
    all_to_all x1, waiting for transfers between devices, local(): kv_all = lax.all_to_all(kv_copies, ('y', 'x'), 0, 0, tiled=True)  12.8 us
    all_to_all x1, starting transfers between devices, local(): dkv_all = lax.all_to_all(dkv, ('y', 'x'), 0, 0, tiled=True)  9.33 us
    all_to_all x1, starting transfers between devices, local(): kv_all = lax.all_to_all(kv_copies, ('y', 'x'), 0, 0, tiled=True)  7.17 us
    ppermute x1, starting transfers between devices, local(): delta_rest = lax.ppermute(delta_half, 'tp', [(i, i ^ 4) for i in range(8)])  4.51 us
    ppermute x1, waiting for transfers between devices, local(): lax.ppermute(delta_pair, 'tp', [(i, i ^ 2) for i in range(8)])  4.49 us
    pallas_call x1, Pallas kernels, local(): pl.pallas_call(grad_kernel, out_shape=(shape((CHIPS, SLOTS, 2 * HEAD)), s...  3.96 us
    all_to_all x1, waiting for transfers between devices, local(): dkv_all = lax.all_to_all(dkv, ('y', 'x'), 0, 0, tiled=True)  3.7 us
    pallas_call x1, Pallas kernels, local(): pl.pallas_call(stats_kernel, out_shape=(shape((PICKED, HEAD)), shape((PIC...  2.61 us
  transfers between devices with their start and end apart: 9, of which 6 were waited for; matrix products, arithmetic and copies ran while one was open for 1% of the time, Pallas kernels for 10%

profile of v2, /device:TPU:64, one launch (start us, length us, event | category | flops | bytes accessed | tf_op | source)
XLA Modules:
  0.0 65.6 jit_solution(1107541158538898767)
XLA Ops:
  0.6 2.4 %pick_kv.1 = bf16[16,128,256]{2,1,0:T(8,128)(2,1)} custom-call(s32[1,128]{1,0:T(1,128)} %bitcast.1, bf16[512,128]{1,0:T(8,128)(2,1)} %k_hbm.1, bf16[512,128]{1,0:T(8,128)(2,1)} %v_hbm.1), custom_call_target="tpu_custom_call" | custom-call | tf_op jit(solution)/shard_map/pick_kv/pallas_call | solution.py:377
  3.0 0.0 copy-start.3
  3.0 0.0 copy-start.1
  3.0 7.2 %all-to-all-start = ((bf16[16,128,256]{2,1,0:T(8,128)(2,1)}), bf16[16,128,256]{2,1,0:T(8,128)(2,1)S(1)}, u32[]{:S(2)}, u32[]{:S(2)}) async-start(bf16[16,128,256]{2,1,0:T(8,128)(2,1)} %pick_kv.1), calls=%async_computation | async-start | bytes 2097152 | tf_op jit(solution)/shard_map/all_to_all | solution.py:393
  10.2 0.0 copy-start
  10.3 0.6 copy-done
  10.9 1.2 %copy-done.2 = bf16[512,1024]{1,0:T(8,128)(2,1)S(1)} copy-done((bf16[512,1024]{1,0:T(8,128)(2,1)S(1)}, bf16[512,1024]{1,0:T(8,128)(2,1)}, u32[]{:S(2)}) %copy-start.2) | copy-done | bytes 1048600
  12.1 1.0 %pick_q.1.own_ref = bf16[2,4,256,128]{3,2,1,0:T(8,128)(2,1)S(1)} custom-call(s32[1,128]{1,0:T(1,128)S(1)} %bitcast.2, bf16[1,512]{1,0:T(2,128)(2,1)S(1)} %reshape.18.gate_ref, bf16[512,1024]{1,0:T(8,128)(2,1)S(1)} %copy-done.1, bf16[512,1024]{1,0:T(8,128)(2,1)S(1)} %copy-done.2), custom_call_target="tpu_custom_call" | custom-call | flops 1073741824 | bytes 1048576 | tf_op jit(solution)/shard_map/pick_q/pallas_call | solution.py:395
  13.1 0.1 collective-permute-start.1
  13.2 0.5 collective-permute-start
  13.7 1.4 %collective-permute-done.peer_picked = s32[1,128]{1,0:T(1,128)S(1)} collective-permute-done((s32[1,128]{1,0:T(1,128)S(1)}, s32[1,128]{1,0:T(1,128)S(1)}, u32[]{:S(2)}, u32[]{:S(2)}) %collective-permute-start) | collective-permute-done | bytes 544 | tf_op jit(solution)/shard_map/ppermute | solution.py:411
  15.1 0.0 collective-permute-done.1.oth_ref
  15.1 12.8 %all-to-all-done.kv_ref = bf16[16,128,256]{2,1,0:T(8,128)(2,1)S(1)} async-done(((bf16[16,128,256]{2,1,0:T(8,128)(2,1)}), bf16[16,128,256]{2,1,0:T(8,128)(2,1)S(1)}, u32[]{:S(2)}, u32[]{:S(2)}) %all-to-all-start) | async-done | bytes 1048608 | tf_op jit(solution)/shard_map/all_to_all | solution.py:393
  27.9 2.6 %stats.1 = (bf16[2048,128]{1,0:T(8,128)(2,1)S(1)}, bf16[2048,128]{1,0:T(8,128)(2,1)S(1)}, bf16[2048,128]{1,0:T(8,128)(2,1)S(1)}, bf16[2048,128]{1,0:T(8,128)(2,1...) custom-call(s32[1,128]{1,0:T(1,128)S(1)} %collective-permute-done.peer_picked, ...), custom_call_target="tpu_custom_call" | custom-call | tf_op jit(solution)/shard_map/stats/pallas_call | solution.py:412
  30.5 0.1 collective-permute-start.2
  30.6 1.3 %collective-permute-done.2.peer_ref = f32[9,8,256]{2,1,0:T(8,128)S(1)} collective-permute-done((f32[9,8,256]{2,1,0:T(8,128)S(1)}, f32[9,8,256]{2,1,0:T(8,128)S(1)}, u32[]{:S(2)}, u32[]{:S(2)}) %collective-permute-start.2) | collective-permute-done | bytes 73760 | tf_op jit(solution)/shard_map/ppermute | solution.py:428
  31.8 0.8 %combine.1 = (f32[9,8,256]{2,1,0:T(8,128)S(1)}, f32[8,128]{1,0:T(8,128)S(1)}) custom-call(s32[32]{0:T(128)S(1)} %get-tuple-element.21.info_ref, f32[9,8,256]{2,1,0:T(8,128)S(1)} %get-tuple-element.26.stats_ref, f32[9,8,256]{2,1,0:T(8,128)S(1)} %collective-permute-done.2.peer_ref), custom_call_target="tpu_custom_call" | custom-call | tf_op jit(solution)/shard_map/combine/pallas_call | solution.py:429
  32.6 2.0 %collective-permute-start.4 = (f32[8,128]{1,0:T(8,128)S(1)}, f32[8,128]{1,0:T(8,128)S(1)}, u32[]{:S(2)}, u32[]{:S(2)}) collective-permute-start(f32[8,128]{1,0:T(8,128)S(1)} %get-tuple-element.32), channel_id=1, source_target_pairs={{0,1},{1,0},{2,3},{3,2},{4,5},{5,4},{6,7},{7,6},{8,9},{9,8},{10,11... | collective-permute-start | bytes 12296 | tf_op jit(solution)/shard_map/ppermute | solution.py:437
  34.6 4.0 %grads.1 = (bf16[16,128,256]{2,1,0:T(8,128)(2,1)}, f32[4,256,128]{2,1,0:T(8,128)S(1)}, bf16[4,256,128]{2,1,0:T(8,128)(2,1)S(1)}) custom-call(s32[32]{0:T(128)S(1)} %get-tuple-element.21.info_ref, bf16[2048,128]{1,0:T(8,128)(2,1)S(1)} %get-tuple-element.22.kc_ref, bf16[2048,128]{1,0:T(8,128)(2,1)S(1)} %get-tuple-element.23.vc_ref, ...), custom_call_target="tpu_custom_call" | custom-call | flops 4294967296 | bytes 1048576 | tf_op jit(solution)/shard_map/grads/pallas_call | solution.py:438
  38.5 0.0 collective-permute-done.4
  38.5 9.3 %all-to-all-start.1 = ((bf16[16,128,256]{2,1,0:T(8,128)(2,1)}), bf16[16,128,256]{2,1,0:T(8,128)(2,1)S(1)}, u32[]{:S(2)}, u32[]{:S(2)}) async-start(bf16[16,128,256]{2,1,0:T(8,128)(2,1)} %get-tuple-element.33), calls=%async_computation.1 | async-start | bytes 2097152 | tf_op jit(solution)/shard_map/all_to_all | solution.py:457
  47.9 0.1 collective-permute-start.3
  48.0 0.1 collective-permute-start.5
  48.1 4.5 %collective-permute-done.5 = f32[8,128]{1,0:T(8,128)S(1)} collective-permute-done((f32[8,128]{1,0:T(8,128)S(1)}, f32[8,128]{1,0:T(8,128)S(1)}, u32[]{:S(2)}, u32[]{:S(2)}) %collective-permute-start.5) | collective-permute-done | bytes 4128 | tf_op jit(solution)/shard_map/ppermute | solution.py:459
  52.6 4.5 %collective-permute-start.6 = (f32[8,128]{1,0:T(8,128)S(1)}, f32[8,128]{1,0:T(8,128)S(1)}, u32[]{:S(2)}, u32[]{:S(2)}) collective-permute-start(f32[8,128]{1,0:T(8,128)S(1)} %add.7.delta_half), channel_id=1, source_target_pairs={{0,4},{1,5},{2,6},{3,7},{4,0},{5,1},{6,2},{7,3},{8,12},{9,13},{10,... | collective-permute-start | bytes 12296 | tf_op jit(solution)/shard_map/ppermute | solution.py:460
  57.1 0.0 collective-permute-done.3.dq_peer
  57.1 1.4 %place_q.1 = (bf16[512,1024]{1,0:T(8,128)(2,1)}, f32[16,128]{1,0:T(8,128)S(1)}) custom-call(s32[1,128]{1,0:T(1,128)S(1)} %bitcast.4, bf16[1,512]{1,0:T(2,128)(2,1)S(1)} %reshape.18.gate_ref, f32[4,256,128]{2,1,0:T(8,128)S(1)} %get-tuple-element.28.dq_own, bf16[4,256,128]{2,1,0:T(8,128)(2,1)S(1)} %collective-permute-done.3.dq_peer), custom_call_target="tpu_custom_call" | custom-call | flops 536870912 | bytes 1048576 | tf_op jit(solution)/shard_map/place_q/pallas_call | solution.py:462
  58.5 1.6 %collective-permute-done.6.delta_rest = f32[8,128]{1,0:T(8,128)S(1)} collective-permute-done((f32[8,128]{1,0:T(8,128)S(1)}, f32[8,128]{1,0:T(8,128)S(1)}, u32[]{:S(2)}, u32[]{:S(2)}) %collective-permute-start.6) | collective-permute-done | bytes 4128 | tf_op jit(solution)/shard_map/ppermute | solution.py:460
  60.1 0.1 place_logit.1
  60.3 0.6 reduce
  60.8 3.7 %all-to-all-done.1.dkv_ref = bf16[16,128,256]{2,1,0:T(8,128)(2,1)S(1)} async-done(((bf16[16,128,256]{2,1,0:T(8,128)(2,1)}), bf16[16,128,256]{2,1,0:T(8,128)(2,1)S(1)}, u32[]{:S(2)}, u32[]{:S(2)}) %all-to-all-start.1) | async-done | bytes 1048608 | tf_op jit(solution)/shard_map/all_to_all | solution.py:457
  64.5 1.0 %place_kv.1 = (bf16[512,128]{1,0:T(8,128)(2,1)}, bf16[512,128]{1,0:T(8,128)(2,1)}) custom-call(s32[1,128]{1,0:T(1,128)S(1)} %bitcast.6, bf16[16,128,256]{2,1,0:T(8,128)(2,1)S(1)} %all-to-all-done.1.dkv_ref), custom_call_target="tpu_custom_call" | custom-call | tf_op jit(solution)/shard_map/place_kv/pallas_call | solution.py:480
  (6 shorter events, 0.0 us)
Async XLA Ops:
  3.0 7.2 %copy-start.3 = (bf16[512]{0:T(512)(128)(2,1)S(1)}, bf16[512]{0:T(512)(128)(2,1)}, u32[]{:S(2)}) copy-start(bf16[512]{0:T(512)(128)(2,1)} %param.9) | copy-start | bytes 3076
  3.0 7.2 %copy-start.1 = (bf16[512,1024]{1,0:T(8,128)(2,1)S(1)}, bf16[512,1024]{1,0:T(8,128)(2,1)}, u32[]{:S(2)}) copy-start(bf16[512,1024]{1,0:T(8,128)(2,1)} %q_hbm.1) | copy-start | bytes 3145732
  3.0 24.8 %all-to-all-start = ((bf16[16,128,256]{2,1,0:T(8,128)(2,1)}), bf16[16,128,256]{2,1,0:T(8,128)(2,1)S(1)}, u32[]{:S(2)}, u32[]{:S(2)}) async-start(bf16[16,128,256]{2,1,0:T(8,128)(2,1)} %pick_kv.1), calls=%async_computation | async-start | bytes 2097152 | tf_op jit(solution)/shard_map/all_to_all | solution.py:393
  10.2 0.7 %copy-start = (s32[128]{0:T(128)S(1)}, s32[128]{0:T(128)}, u32[]{:S(2)}) copy-start(s32[128]{0:T(128)} %param.11) | copy-start | bytes 1540
  10.9 1.2 %copy-start.2 = (bf16[512,1024]{1,0:T(8,128)(2,1)S(1)}, bf16[512,1024]{1,0:T(8,128)(2,1)}, u32[]{:S(2)}) copy-start(bf16[512,1024]{1,0:T(8,128)(2,1)} %up_hbm.1) | copy-start | bytes 3145732
  13.1 2.0 %collective-permute-start.1 = (bf16[2,4,256,128]{3,2,1,0:T(8,128)(2,1)S(1)}, bf16[2,4,256,128]{3,2,1,0:T(8,128)(2,1)S(1)}, u32[]{:S(2)}, u32[]{:S(2)}) collective-permute-start(bf16[2,4,256,128]{3,2,1,0:T(8,128)(2,1)S(1)} %pick_q.1.own_ref), channel_id=1, source_target_pairs={{0,8},{8,0},{1,9},{9,1},{2,10},{10,2},{3,11},{11,3},{4,12},{12,4},... | collective-permute-start | bytes 1572872 | tf_op jit(solution)/shard_map/ppermute | solution.py:410
  13.2 1.9 %collective-permute-start = (s32[1,128]{1,0:T(1,128)S(1)}, s32[1,128]{1,0:T(1,128)S(1)}, u32[]{:S(2)}, u32[]{:S(2)}) collective-permute-start(s32[1,128]{1,0:T(1,128)S(1)} %bitcast.3), channel_id=1, source_target_pairs={{0,8},{8,0},{1,9},{9,1},{2,10},{10,2},{3,11},{11,3},{4,12},{12,4},... | collective-permute-start | bytes 1544 | tf_op jit(solution)/shard_map/ppermute | solution.py:411
  30.5 1.4 %collective-permute-start.2 = (f32[9,8,256]{2,1,0:T(8,128)S(1)}, f32[9,8,256]{2,1,0:T(8,128)S(1)}, u32[]{:S(2)}, u32[]{:S(2)}) collective-permute-start(f32[9,8,256]{2,1,0:T(8,128)S(1)} %get-tuple-element.26.stats_ref), channel_id=1, source_target_pairs={{0,8},{8,0},{1,9},{9,1},{2,10},{10,2},{3,11},{11,3},{4,12},{12,4},... | collective-permute-start | bytes 221192 | tf_op jit(solution)/shard_map/ppermute | solution.py:428
  32.6 5.9 %collective-permute-start.4 = (f32[8,128]{1,0:T(8,128)S(1)}, f32[8,128]{1,0:T(8,128)S(1)}, u32[]{:S(2)}, u32[]{:S(2)}) collective-permute-start(f32[8,128]{1,0:T(8,128)S(1)} %get-tuple-element.32), channel_id=1, source_target_pairs={{0,1},{1,0},{2,3},{3,2},{4,5},{5,4},{6,7},{7,6},{8,9},{9,8},{10,11... | collective-permute-start | bytes 12296 | tf_op jit(solution)/shard_map/ppermute | solution.py:437
  38.5 26.0 %all-to-all-start.1 = ((bf16[16,128,256]{2,1,0:T(8,128)(2,1)}), bf16[16,128,256]{2,1,0:T(8,128)(2,1)S(1)}, u32[]{:S(2)}, u32[]{:S(2)}) async-start(bf16[16,128,256]{2,1,0:T(8,128)(2,1)} %get-tuple-element.33), calls=%async_computation.1 | async-start | bytes 2097152 | tf_op jit(solution)/shard_map/all_to_all | solution.py:457
  47.9 9.2 %collective-permute-start.3 = (bf16[4,256,128]{2,1,0:T(8,128)(2,1)S(1)}, bf16[4,256,128]{2,1,0:T(8,128)(2,1)S(1)}, u32[]{:S(2)}, u32[]{:S(2)}) collective-permute-start(bf16[4,256,128]{2,1,0:T(8,128)(2,1)S(1)} %get-tuple-element.29), channel_id=1, source_target_pairs={{0,8},{8,0},{1,9},{9,1},{2,10},{10,2},{3,11},{11,3},{4,12},{12,4},... | collective-permute-start | bytes 786440 | tf_op jit(solution)/shard_map/ppermute | solution.py:461
  48.0 4.6 %collective-permute-start.5 = (f32[8,128]{1,0:T(8,128)S(1)}, f32[8,128]{1,0:T(8,128)S(1)}, u32[]{:S(2)}, u32[]{:S(2)}) collective-permute-start(f32[8,128]{1,0:T(8,128)S(1)} %add.6), channel_id=1, source_target_pairs={{0,2},{1,3},{2,0},{3,1},{4,6},{5,7},{6,4},{7,5},{8,10},{9,11},{10,... | collective-permute-start | bytes 12296 | tf_op jit(solution)/shard_map/ppermute | solution.py:459
  52.6 7.5 %collective-permute-start.6 = (f32[8,128]{1,0:T(8,128)S(1)}, f32[8,128]{1,0:T(8,128)S(1)}, u32[]{:S(2)}, u32[]{:S(2)}) collective-permute-start(f32[8,128]{1,0:T(8,128)S(1)} %add.7.delta_half), channel_id=1, source_target_pairs={{0,4},{1,5},{2,6},{3,7},{4,0},{5,1},{6,2},{7,3},{8,12},{9,13},{10,... | collective-permute-start | bytes 12296 | tf_op jit(solution)/shard_map/ppermute | solution.py:460

commit v3 on v2

--- a/solution.py
+++ b/solution.py
@@ -25,6 +25,8 @@
 EDGE = 256
 PART = 128
 SPARE = 2 * CHUNKS
+KEPT = 1536
+KERNEL_BYTES = 16 * 1024 * 1024
 SENTINEL = 128.0
 LIVE_BELOW = 32.0
 NEGATIVE = -1e30
@@ -54,11 +56,6 @@
     return 1.0 / (1.0 + jnp.exp(-rows))
 
 
-def dead_column(picked):
-    dead = jnp.where(picked >= TOKENS, SENTINEL, 0.0).astype(F32)
-    return jnp.broadcast_to(dead, (SLOTS, SLOTS)).T
-
-
 def fetch(pairs, sems):
     copies = [pltpu.make_async_copy(src, dst, sems.at[n]) for n, (src, dst) in enumerate(pairs)]
     for copy in copies:
@@ -68,10 +65,21 @@
 
 
 def pick_kv_kernel(picked_hbm, k_hbm, v_hbm, kv_out, picked_ref, k_ref, v_ref, message, sems, out_sems):
-    fetch([(picked_hbm, picked_ref), (k_hbm, k_ref), (v_hbm, v_ref)], sems)
-    gather = place_matrix(picked_ref[...]).T.astype(BF16)
+    pairs = [(picked_hbm, picked_ref), (k_hbm, k_ref), (v_hbm, v_ref)]
+    copies = [pltpu.make_async_copy(src, dst, sems.at[n]) for n, (src, dst) in enumerate(pairs)]
+    for copy in copies:
+        copy.start()
+    copies[0].wait()
+    column = jnp.broadcast_to(picked_ref[...], (SLOTS, SLOTS)).astype(F32).T
+    token = lax.broadcasted_iota(jnp.int32, (SLOTS, SLOTS), 1).astype(F32)
+    gather = jnp.concatenate(
+        [jnp.where(token + base == column, 1.0, 0.0) for base in range(0, TOKENS, SLOTS)], axis=1
+    ).astype(BF16)
+    dead = jnp.where(column >= TOKENS, SENTINEL, 0.0)
+    copies[1].wait()
     keys = jnp.dot(gather, k_ref[...], preferred_element_type=F32)
-    message[:, 0:HEAD] = (keys + dead_column(picked_ref[...])).astype(BF16)
+    message[:, 0:HEAD] = (keys + dead).astype(BF16)
+    copies[2].wait()
     message[:, HEAD : 2 * HEAD] = jnp.dot(
         gather, v_ref[...], preferred_element_type=F32
     ).astype(BF16)
@@ -110,6 +118,10 @@
         place = jnp.where(chunk < self.own_chunks, chunk, CHUNKS + chunk - self.own_chunks)
         return jnp.where(chunk < self.live_chunks, place, SPARE)
 
+    def peer_place(self, chunk):
+        place = self.place(chunk)
+        return jnp.where(place == SPARE, SPARE, lax.rem(place + CHUNKS, 2 * CHUNKS))
+
     def limit(self, chunk):
         slot = lax.rem(lax.broadcasted_iota(jnp.int32, (1, ROWS), 1), CHUNK)
         own = self.offset + chunk * CHUNK + 1
@@ -129,24 +141,31 @@
         low = jnp.where(paired, jnp.minimum(low_a, low_b), low_a)
         high = jnp.where(paired, jnp.maximum(high_a, high_b), high_a)
         full = lax.div(low, KEYS)
-        return full, lax.div(high - full * KEYS + EDGE - 1, EDGE)
+        rest = high - full * KEYS
+        wide = lax.div(rest + EDGE - 1, KEYS)
+        return full, wide, rest > wide * KEYS
 
     def limits(self, tile):
         return jnp.concatenate([self.limit(2 * tile), self.limit(2 * tile + 1)], axis=1)
 
     def sweep(self, tile, block, carry):
-        full, edges = self.spans(tile)
+        full, wide, narrow = self.spans(tile)
         limits = self.limits(tile)
-        start = full * KEYS
-        carry = lax.fori_loop(
-            0, full, lambda b, c: block(pl.multiple_of(b * KEYS, KEYS), KEYS, None, c), carry
-        )
-        return lax.fori_loop(
-            0,
-            edges,
-            lambda b, c: block(pl.multiple_of(start + b * EDGE, EDGE), EDGE, limits, c),
-            carry,
-        )
+
+        def run(first, count, keys, limits, carry):
+            def steps(kept):
+                return lambda b, carry: block(
+                    pl.multiple_of(first + b * keys, keys), keys, limits, kept, carry
+                )
+
+            inside = jnp.minimum(jnp.maximum(lax.div(KEPT - first, keys), 0), count)
+            carry = lax.fori_loop(0, inside, steps(True), carry)
+            return lax.fori_loop(inside, count, steps(False), carry)
+
+        carry = run(0, full, KEYS, None, carry)
+        carry = run(full * KEYS, wide, KEYS, limits, carry)
+        last = (full + wide) * KEYS
+        return run(last, jnp.where(narrow, 1, 0), EDGE, limits, carry)
 
 
 def pair_rows(tile):
@@ -154,15 +173,11 @@
 
 
 def stats_kernel(
-    peer_picked, kv_ref, own_ref, oth_ref, kc_out, vc_out, q_out, s_out, stats_out, info_out,
-    k_pack, v_pack,
+    peer_picked, kv_ref, own_ref, oth_ref, kc_out, vc_out, q_out, s_out, stats_out, scores_out,
+    pushed_out, info_out, k_pack, v_pack,
 ):
     chip = lax.axis_index("y") * 4 + lax.axis_index("x")
     core = lax.axis_index("c")
-    k_pack[...] = jnp.zeros_like(k_pack)
-    v_pack[...] = jnp.zeros_like(v_pack)
-    q_out[...] = jnp.zeros_like(q_out)
-    s_out[...] = jnp.zeros_like(s_out)
     stats_out[...] = jnp.zeros_like(stats_out)
     offset = 0
     own_offset = 0
@@ -183,8 +198,17 @@
     info_out[17] = own_count
     info_out[18] = own_chunks
     info_out[19] = live_chunks
-    kc_out[...] = k_pack[0:PICKED, :].astype(BF16)
-    vc_out[...] = v_pack[0:PICKED, :].astype(BF16)
+    tail = pl.ds(offset + SLOTS, KEYS)
+    k_pack[tail, :] = jnp.zeros((KEYS, HEAD), F32)
+    v_pack[tail, :] = jnp.zeros((KEYS, HEAD), F32)
+
+    def narrow_keys(b, _):
+        rows = pl.ds(pl.multiple_of(b * KEYS, KEYS), KEYS)
+        kc_out[rows, :] = k_pack[rows, :].astype(BF16)
+        vc_out[rows, :] = v_pack[rows, :].astype(BF16)
+        return 0
+
+    lax.fori_loop(0, lax.div(own_offset + own_count + KEYS - 1, KEYS), narrow_keys, 0)
     for t in range(CHUNKS):
         q_out[t * ROWS : (t + 1) * ROWS, :] = own_ref[0, t]
         s_out[t * ROWS : (t + 1) * ROWS, :] = own_ref[1, t]
@@ -192,16 +216,22 @@
         rows = pl.ds(pl.multiple_of((own_chunks + t) * ROWS, ROWS), ROWS)
         q_out[rows, :] = oth_ref[0, t]
         s_out[rows, :] = oth_ref[1, t]
+    spare = pl.ds(pl.multiple_of(live_chunks * ROWS, ROWS), ROWS)
+    q_out[spare, :] = jnp.zeros((ROWS, HEAD), BF16)
+    s_out[spare, :] = jnp.zeros((ROWS, HEAD), BF16)
     tiles = Tiles(core, own_offset, own_count, own_chunks, live_chunks)
 
     def attend(tile, _):
         q_rows = q_out[pair_rows(tile), :]
         s_rows = s_out[pair_rows(tile), :]
 
-        def block(base, keys, limits, carry):
+        def block(base, keys, limits, kept, carry):
             top, total, pull = carry
             scores = nt_dot(kc_out[pl.ds(base, keys), :], q_rows)
             pushed = nt_dot(vc_out[pl.ds(base, keys), :], s_rows)
+            if kept:
+                scores_out[tile, pl.ds(base, keys), :] = scores
+                pushed_out[tile, pl.ds(base, keys), :] = pushed
             for u in range(0, keys, PART):
                 part = scores[u : u + PART] * LOG_FACTOR
                 if limits is not None:
@@ -236,34 +266,9 @@
     lax.fori_loop(0, tiles.number, attend, 0)
 
 
-def combine_kernel(info_ref, stats_ref, peer_ref, comb_out, delta_out):
-    own_chunks = info_ref[18]
-    lane = lax.div(lax.broadcasted_iota(jnp.int32, (1, SLOTS), 1), CHUNK)
-    comb_out[SPARE] = jnp.zeros((8, ROWS), F32)
-    deltas = jnp.zeros((1, SLOTS), F32)
-    for place in range(SPARE):
-        mine = stats_ref[place]
-        theirs = peer_ref[(place + CHUNKS) % SPARE]
-        top = jnp.maximum(mine[0:1], theirs[0:1])
-        mine_scale = jnp.exp2(mine[0:1] - top)
-        their_scale = jnp.exp2(theirs[0:1] - top)
-        total = mine[1:2] * mine_scale + theirs[1:2] * their_scale
-        total = jnp.where(total > 0.0, total, 1.0)
-        delta = (mine[2:3] * mine_scale + theirs[2:3] * their_scale) / total
-        comb_out[place, 0:1, :] = top + jnp.log2(total)
-        comb_out[place, 1:2, :] = delta
-        if place < CHUNKS:
-            heads = delta[:, 0:128] + delta[:, 128:256]
-            heads = heads + pltpu.roll(heads, 64, 1)
-            heads = heads + pltpu.roll(heads, 32, 1)
-            mark = jnp.where(place < own_chunks, place, CHUNKS)
-            deltas = deltas + jnp.where(lane == mark, heads, 0.0)
-    delta_out[...] = jnp.broadcast_to(deltas, (8, SLOTS))
-
-
 def grad_kernel(
-    info_ref, kc_ref, vc_ref, q_ref, s_ref, comb_ref, dkv_out, dq_own, dq_oth,
-    dk_sum, dv_sum, dq_sum,
+    info_ref, kc_ref, vc_ref, q_ref, s_ref, stats_ref, peer_ref, scores_ref, pushed_ref, dkv_out, dq_own, dq_oth, delta_out,
+    dk_sum, dv_sum, dq_sum, message, sems,
 ):
     core = lax.axis_index("c")
     tiles = Tiles(core, info_ref[16], info_ref[17], info_ref[18], info_ref[19])
@@ -271,20 +276,40 @@
     dv_sum[...] = jnp.zeros_like(dv_sum)
     dq_own[...] = jnp.zeros_like(dq_own)
     dq_oth[...] = jnp.zeros_like(dq_oth)
+    delta_out[...] = jnp.zeros_like(delta_out)
 
     def push_back(tile, _):
         q_rows = q_ref[pair_rows(tile), :]
         s_rows = s_ref[pair_rows(tile), :]
         chunks = (2 * tile, 2 * tile + 1)
-        comb = jnp.concatenate([comb_ref[tiles.place(c)] for c in chunks], axis=1)
-        level, delta = comb[0:1], comb[1:2]
+        mine = jnp.concatenate([stats_ref[tiles.place(c)] for c in chunks], axis=1)
+        theirs = jnp.concatenate([peer_ref[tiles.peer_place(c)] for c in chunks], axis=1)
+        top = jnp.maximum(mine[0:1], theirs[0:1])
+        mine_scale = jnp.exp2(mine[0:1] - top)
+        their_scale = jnp.exp2(theirs[0:1] - top)
+        total = mine[1:2] * mine_scale + theirs[1:2] * their_scale
+        total = jnp.where(total > 0.0, total, 1.0)
+        delta = (mine[2:3] * mine_scale + theirs[2:3] * their_scale) / total
+        level = top + jnp.log2(total)
+        lane = lax.div(lax.broadcasted_iota(jnp.int32, (1, SLOTS), 1), CHUNK)
+        for half, chunk in enumerate(chunks):
+            first = half * ROWS
+            heads = delta[:, first : first + 128] + delta[:, first + 128 : first + 256]
+            heads = heads + pltpu.roll(heads, 64, 1)
+            heads = heads + pltpu.roll(heads, 32, 1)
+            mark = jnp.where(chunk < tiles.own_chunks, chunk, CHUNKS)
+            delta_out[0:1, :] += jnp.where(lane == mark, heads, 0.0)
         dq_sum[...] = jnp.zeros_like(dq_sum)
 
-        def block(base, keys, limits, carry):
+        def block(base, keys, limits, kept, carry):
             span = pl.ds(base, keys)
             key_rows = kc_ref[span, :]
-            scores = nt_dot(key_rows, q_rows)
-            pushed = nt_dot(vc_ref[span, :], s_rows)
+            if kept:
+                scores = scores_ref[tile, span, :]
+                pushed = pushed_ref[tile, span, :]
+            else:
+                scores = nt_dot(key_rows, q_rows)
+                pushed = nt_dot(vc_ref[span, :], s_rows)
             weights = jnp.exp2(scores * LOG_FACTOR - level)
             if limits is not None:
                 index = lax.broadcasted_iota(jnp.int32, (keys, 2 * ROWS), 0)
@@ -312,10 +337,15 @@
         return 0
 
     lax.fori_loop(0, tiles.number, push_back, 0)
+    copies = []
     for s in range(CHIPS):
         rows = pl.ds(info_ref[s], SLOTS)
-        dkv_out[s, :, 0:HEAD] = dk_sum[rows, :].astype(BF16)
-        dkv_out[s, :, HEAD : 2 * HEAD] = dv_sum[rows, :].astype(BF16)
+        message[s, :, 0:HEAD] = dk_sum[rows, :].astype(BF16)
+        message[s, :, HEAD : 2 * HEAD] = dv_sum[rows, :].astype(BF16)
+        copies.append(pltpu.make_async_copy(message.at[s], dkv_out.at[(s % 4) * 4 + s // 4], sems.at[s]))
+        copies[s].start()
+    for copy in copies:
+        copy.wait()
 
 
 def place_q_kernel(picked_ref, gate_ref, dq_own, dq_peer, q_out, closed_out):
@@ -333,11 +363,13 @@
         ).astype(BF16)
 
 
-def place_logit_kernel(picked_ref, closed_ref, delta_half, delta_rest, logit_out):
+def place_logit_kernel(picked_ref, closed_ref, delta_a, delta_b, delta_c, delta_d, logit_out):
     scatter = place_matrix(picked_ref[...]).astype(BF16)
-    deltas = delta_half[0:1, :] + delta_rest[0:1, :]
+    deltas = (delta_a[0:1, :] + delta_b[0:1, :]) + (delta_c[0:1, :] + delta_d[0:1, :])
     logit_rows = (closed_ref[...] * deltas).astype(BF16)
-    logit_out[...] = nt_dot(logit_rows, scatter)[0:1].astype(BF16)
+    for part in range(TOKENS // SLOTS):
+        rows = slice(part * SLOTS, (part + 1) * SLOTS)
+        logit_out[part : part + 1, :] = nt_dot(logit_rows, scatter[rows])[0:1].astype(BF16)
 
 
 def place_kv_kernel(picked_ref, dkv_ref, k_out, v_out):
@@ -409,55 +441,51 @@
     )(picked_row, gate_row, head_queries, upstream)
     qs_peer = lax.ppermute(qs_own, "c", swap)
     peer_picked = lax.ppermute(picked_row, "c", swap)
-    kc, vc, q_rows, s_rows, stats, info = pl.pallas_call(
+    kc, vc, q_rows, s_rows, stats, scores, pushed, info = pl.pallas_call(
         stats_kernel,
         out_shape=(
             shape((PICKED, HEAD)),
             shape((PICKED, HEAD)),
-            shape((2 * CHUNKS * ROWS, HEAD)),
-            shape((2 * CHUNKS * ROWS, HEAD)),
+            shape(((2 * CHUNKS + 1) * ROWS, HEAD)),
+            shape(((2 * CHUNKS + 1) * ROWS, HEAD)),
             shape((SPARE + 1, 8, ROWS), F32),
+            shape((CHUNKS, KEPT, 2 * ROWS), F32),
+            shape((CHUNKS, KEPT, 2 * ROWS), F32),
             shape((32,), jnp.int32),
         ),
         in_specs=whole(4),
-        out_specs=tuple(whole(5)) + (pl.BlockSpec(memory_space=pltpu.SMEM),),
-        scratch_shapes=[pltpu.VMEM((PICKED + SLOTS, HEAD), F32)] * 2,
-        compiler_params=params(),
+        out_specs=tuple(whole(7)) + (pl.BlockSpec(memory_space=pltpu.SMEM),),
+        scratch_shapes=[pltpu.VMEM((PICKED + SLOTS + KEYS, HEAD), F32)] * 2,
+        compiler_params=params(KERNEL_BYTES),
         name="stats",
     )(peer_picked, kv_all, qs_own, qs_peer)
     stats_peer = lax.ppermute(stats, "c", swap)
-    comb, deltas = pl.pallas_call(
-        combine_kernel,
-        out_shape=(shape((SPARE + 1, 8, ROWS), F32), shape((8, SLOTS), F32)),
-        in_specs=[pl.BlockSpec(memory_space=pltpu.SMEM)] + whole(2),
-        out_specs=tuple(whole(2)),
-        compiler_params=params(),
-        name="combine",
-    )(info, stats, stats_peer)
-    delta_near = lax.ppermute(deltas, "tp", [(i, i ^ 1) for i in range(8)])
-    dkv, dq_own, dq_oth = pl.pallas_call(
+    dkv, dq_own, dq_oth, deltas = pl.pallas_call(
         grad_kernel,
         out_shape=(
             shape((CHIPS, SLOTS, 2 * HEAD)),
             shape((CHUNKS, ROWS, HEAD), F32),
             shape((CHUNKS, ROWS, HEAD)),
+            shape((8, SLOTS), F32),
         ),
-        in_specs=[pl.BlockSpec(memory_space=pltpu.SMEM)] + whole(5),
-        out_specs=tuple(whole(3)),
+        in_specs=[pl.BlockSpec(memory_space=pltpu.SMEM)] + whole(8),
+        out_specs=tuple(hbm(1) + whole(3)),
         scratch_shapes=[
             pltpu.VMEM((PICKED + SLOTS, HEAD), F32),
             pltpu.VMEM((PICKED + SLOTS, HEAD), F32),
             pltpu.VMEM((2 * ROWS, HEAD), F32),
+            pltpu.VMEM((CHIPS, SLOTS, 2 * HEAD), BF16),
+            pltpu.SemaphoreType.DMA((CHIPS,)),
         ],
-        compiler_params=params(),
+        compiler_params=params(KERNEL_BYTES),
         cost_estimate=cost(1 << 32),
         name="grads",
-    )(info, kc, vc, q_rows, s_rows, comb)
-    dkv, delta_near = lax.optimization_barrier((dkv, delta_near))
-    dkv_all = lax.all_to_all(dkv, ("y", "x"), 0, 0, tiled=True)
-    delta_pair = deltas + delta_near
-    delta_half = delta_pair + lax.ppermute(delta_pair, "tp", [(i, i ^ 2) for i in range(8)])
-    delta_rest = lax.ppermute(delta_half, "tp", [(i, i ^ 4) for i in range(8)])
+    )(info, kc, vc, q_rows, s_rows, stats, stats_peer, scores, pushed)
+    dkv_all = lax.all_to_all(dkv, ("x", "y"), 0, 0, tiled=True)
+    delta_half = deltas + lax.ppermute(deltas, "tp", [(i, i ^ 4) for i in range(8)])
+    delta_parts = [delta_half] + [
+        lax.ppermute(delta_half, "tp", [(i, i ^ k) for i in range(8)]) for k in (1, 2, 3)
+    ]
     dq_peer = lax.ppermute(dq_oth, "c", swap)
     q_out, closed = pl.pallas_call(
         place_q_kernel,
@@ -470,13 +498,13 @@
     )(picked_row, gate_row, dq_own, dq_peer)
     logit_out = pl.pallas_call(
         place_logit_kernel,
-        out_shape=shape((1, TOKENS)),
-        in_specs=whole(4),
+        out_shape=shape((TOKENS // SLOTS, SLOTS)),
+        in_specs=whole(6),
         out_specs=whole(1)[0],
         compiler_params=params(),
         cost_estimate=cost(1 << 28),
         name="place_logit",
-    )(picked_row, closed, delta_half, delta_rest)
+    )(picked_row, closed, *delta_parts)
     k_out, v_out = pl.pallas_call(
         place_kv_kernel,
         out_shape=(shape((TOKENS, HEAD)), shape((TOKENS, HEAD))),

time: 66.6 us -> 64.5 us (0.968)
  the two profiles are of different devices: /device:TPU:64 before, /device:TPU:2 now
where the time goes in v3:
time: 64.5 us; the launch traced here: 64 us
  starting transfers between devices  31.4 us (49%)
  waiting for transfers between devices  15.3 us (24%)
  Pallas kernels  12.9 us (20%)
  local copies, waits for them, and re-layouts  3.79 us (6%)
  between operations  0.7 us (1%)
    all_to_all x1, starting transfers between devices, local(): dkv_all = lax.all_to_all(dkv, ('x', 'y'), 0, 0, tiled=True)  11.5 us
    all_to_all x1, waiting for transfers between devices, local(): kv_all = lax.all_to_all(kv_copies, ('y', 'x'), 0, 0, tiled=True)  9.03 us
    all_to_all x1, starting transfers between devices, local(): kv_all = lax.all_to_all(kv_copies, ('y', 'x'), 0, 0, tiled=True)  7.49 us
    ppermute x1, starting transfers between devices, local(): lax.ppermute(deltas, 'tp', [(i, i ^ 4) for i in range(8)])  7.28 us
    ppermute x3, starting transfers between devices, local(): lax.ppermute(delta_half, 'tp', [(i, i ^ k) for i in range(8)])  4.39 us
    pallas_call x1, Pallas kernels, local(): pl.pallas_call(grad_kernel, out_shape=(shape((CHIPS, SLOTS, 2 * HEAD)), s...  3.87 us
    unnamed x8, local copies, waits for them, and re-layouts  3.11 us
    pallas_call x1, Pallas kernels, local(): pl.pallas_call(stats_kernel, out_shape=(shape((PICKED, HEAD)), shape((PIC...  2.42 us
  transfers between devices with their start and end apart: 10, of which 5 were waited for; matrix products, arithmetic and copies ran while one was open for 1% of the time, Pallas kernels for 5%

profile of v3, /device:TPU:2, one launch (start us, length us, event | category | flops | bytes accessed | tf_op | source)
XLA Modules:
  0.0 64.0 jit_solution(3326953880816681425)
XLA Ops:
  0.6 2.4 %pick_kv.1 = bf16[16,128,256]{2,1,0:T(8,128)(2,1)} custom-call(s32[1,128]{1,0:T(1,128)} %bitcast.2, bf16[512,128]{1,0:T(8,128)(2,1)} %k_hbm.1, bf16[512,128]{1,0:T(8,128)(2,1)} %v_hbm.1), custom_call_target="tpu_custom_call" | custom-call | tf_op jit(solution)/shard_map/pick_kv/pallas_call | solution.py:409
  3.0 7.5 %all-to-all-start = ((bf16[16,128,256]{2,1,0:T(8,128)(2,1)}), bf16[16,128,256]{2,1,0:T(8,128)(2,1)S(1)}, u32[]{:S(2)}, u32[]{:S(2)}) async-start(bf16[16,128,256]{2,1,0:T(8,128)(2,1)} %pick_kv.1), calls=%async_computation | async-start | bytes 2097152 | tf_op jit(solution)/shard_map/all_to_all | solution.py:425
  10.5 0.7 %reshape.18.gate_ref = bf16[1,512]{1,0:T(2,128)(2,1)S(1)} reshape(bf16[512]{0:T(512)(128)(2,1)} %param.9) | data formatting | bytes 2048 | tf_op jit(solution)/shard_map/reshape | solution.py:426
  11.2 0.7 %copy-done = s32[128]{0:T(128)S(1)} copy-done((s32[128]{0:T(128)S(1)}, s32[128]{0:T(128)}, u32[]{:S(2)}) %copy-start) | copy-done | bytes 536
  11.9 1.2 %copy-done.2 = bf16[512,1024]{1,0:T(8,128)(2,1)S(1)} copy-done((bf16[512,1024]{1,0:T(8,128)(2,1)S(1)}, bf16[512,1024]{1,0:T(8,128)(2,1)}, u32[]{:S(2)}) %copy-start.2) | copy-done | bytes 1048600
  13.1 1.2 %copy-done.3 = bf16[512,1024]{1,0:T(8,128)(2,1)S(1)} copy-done((bf16[512,1024]{1,0:T(8,128)(2,1)S(1)}, bf16[512,1024]{1,0:T(8,128)(2,1)}, u32[]{:S(2)}) %copy-start.3) | copy-done | bytes 1048600
  14.3 1.0 %pick_q.1.own_ref = bf16[2,4,256,128]{3,2,1,0:T(8,128)(2,1)S(1)} custom-call(s32[1,128]{1,0:T(1,128)S(1)} %bitcast.3, bf16[1,512]{1,0:T(2,128)(2,1)S(1)} %reshape.18.gate_ref, bf16[512,1024]{1,0:T(8,128)(2,1)S(1)} %copy-done.2, bf16[512,1024]{1,0:T(8,128)(2,1)S(1)} %copy-done.3), custom_call_target="tpu_custom_call" | custom-call | flops 1073741824 | bytes 1048576 | tf_op jit(solution)/shard_map/pick_q/pallas_call | solution.py:427
  15.3 0.1 collective-permute-start.1
  15.4 0.5 collective-permute-start
  15.9 1.4 %collective-permute-done.peer_picked = s32[1,128]{1,0:T(1,128)S(1)} collective-permute-done((s32[1,128]{1,0:T(1,128)S(1)}, s32[1,128]{1,0:T(1,128)S(1)}, u32[]{:S(2)}, u32[]{:S(2)}) %collective-permute-start) | collective-permute-done | bytes 544 | tf_op jit(solution)/shard_map/ppermute | solution.py:443
  17.3 0.0 collective-permute-done.1.oth_ref
  17.3 9.0 %all-to-all-done.kv_ref = bf16[16,128,256]{2,1,0:T(8,128)(2,1)S(1)} async-done(((bf16[16,128,256]{2,1,0:T(8,128)(2,1)}), bf16[16,128,256]{2,1,0:T(8,128)(2,1)S(1)}, u32[]{:S(2)}, u32[]{:S(2)}) %all-to-all-start) | async-done | bytes 1048608 | tf_op jit(solution)/shard_map/all_to_all | solution.py:425
  26.3 2.4 %stats.1 = (bf16[2048,128]{1,0:T(8,128)(2,1)S(1)}, bf16[2048,128]{1,0:T(8,128)(2,1)S(1)}, bf16[2304,128]{1,0:T(8,128)(2,1)S(1)}, bf16[2304,128]{1,0:T(8,128)(2,1...) custom-call(s32[1,128]{1,0:T(1,128)S(1)} %collective-permute-done.pe, ...), custom_call_target="tpu_custom_call" | custom-call | tf_op jit(solution)/shard_map/stats/pallas_call | solution.py:444
  28.7 0.1 collective-permute-start.2
  28.8 1.3 %collective-permute-done.2.peer_ref = f32[9,8,256]{2,1,0:T(8,128)S(1)} collective-permute-done((f32[9,8,256]{2,1,0:T(8,128)S(1)}, f32[9,8,256]{2,1,0:T(8,128)S(1)}, u32[]{:S(2)}, u32[]{:S(2)}) %collective-permute-start.2) | collective-permute-done | bytes 73760 | tf_op jit(solution)/shard_map/ppermute | solution.py:462
  30.1 3.9 %grads.1 = (bf16[16,128,256]{2,1,0:T(8,128)(2,1)}, f32[4,256,128]{2,1,0:T(8,128)S(1)}, bf16[4,256,128]{2,1,0:T(8,128)(2,1)S(1)}, f32[8,128]{1,0:T(8,128)S(1)}) custom-call(s32[32]{0:T(128)S(1)} %get-tuple-element.20.info_ref, bf16[2048,128]{1,0:T(8,128)(2,1)S(1)} %get-tuple-element.21.kc_ref, bf16[2048,128]{1,0:T(8,128)(2,1)S(1)} %get-tuple-element.22.vc_ref, ...), custom_call_target="tpu_custom_call" | custom-call | flops 4294967296 | bytes 1048576 | tf_op jit(solution)/shard_map/grads/pallas_call | solution.py:463
  34.0 11.5 %all-to-all-start.1 = ((bf16[16,128,256]{2,1,0:T(8,128)(2,1)}), bf16[16,128,256]{2,1,0:T(8,128)(2,1)S(1)}, u32[]{:S(2)}, u32[]{:S(2)}) async-start(bf16[16,128,256]{2,1,0:T(8,128)(2,1)} %get-tuple-element.31), calls=%async_computation.1 | async-start | bytes 2097152 | tf_op jit(solution)/shard_map/all_to_all | solution.py:484
  45.5 0.0 collective-permute-start.3
  45.5 7.3 %collective-permute-start.4 = (f32[8,128]{1,0:T(8,128)S(1)}, f32[8,128]{1,0:T(8,128)S(1)}, u32[]{:S(2)}, u32[]{:S(2)}) collective-permute-start(f32[8,128]{1,0:T(8,128)S(1)} %get-tuple-element.35), channel_id=1, source_target_pairs={{0,4},{1,5},{2,6},{3,7},{4,0},{5,1},{6,2},{7,3},{8,12},{9,13},{10,... | collective-permute-start | bytes 12296 | tf_op jit(solution)/shard_map/ppermute | solution.py:485
  52.8 1.6 %collective-permute-done.4 = f32[8,128]{1,0:T(8,128)S(1)} collective-permute-done((f32[8,128]{1,0:T(8,128)S(1)}, f32[8,128]{1,0:T(8,128)S(1)}, u32[]{:S(2)}, u32[]{:S(2)}) %collective-permute-start.4) | collective-permute-done | bytes 4128 | tf_op jit(solution)/shard_map/ppermute | solution.py:485
  54.4 3.4 %collective-permute-start.7 = (f32[8,128]{1,0:T(8,128)S(1)}, f32[8,128]{1,0:T(8,128)S(1)}, u32[]{:S(2)}, u32[]{:S(2)}) collective-permute-start(f32[8,128]{1,0:T(8,128)S(1)} %add.3.delta_a), channel_id=1, source_target_pairs={{0,3},{1,2},{2,1},{3,0},{4,7},{5,6},{6,5},{7,4},{8,11},{9,10},{10,... | collective-permute-start | bytes 12296 | tf_op jit(solution)/shard_map/ppermute | solution.py:487
  57.7 0.0 collective-permute-start.6
  57.7 1.0 %collective-permute-start.5 = (f32[8,128]{1,0:T(8,128)S(1)}, f32[8,128]{1,0:T(8,128)S(1)}, u32[]{:S(2)}, u32[]{:S(2)}) collective-permute-start(f32[8,128]{1,0:T(8,128)S(1)} %add.3.delta_a), channel_id=1, source_target_pairs={{0,1},{1,0},{2,3},{3,2},{4,5},{5,4},{6,7},{7,6},{8,9},{9,8},{10,11... | collective-permute-start | bytes 12296 | tf_op jit(solution)/shard_map/ppermute | solution.py:487
  58.8 0.0 collective-permute-done.3.dq_peer
  58.8 0.0 copy-done.1
  58.8 1.4 %place_q.1 = (bf16[512,1024]{1,0:T(8,128)(2,1)}, f32[16,128]{1,0:T(8,128)S(1)}) custom-call(s32[1,128]{1,0:T(1,128)S(1)} %bitcast.5, bf16[1,512]{1,0:T(2,128)(2,1)S(1)} %reshape.18.gate_ref, f32[4,256,128]{2,1,0:T(8,128)S(1)} %get-tuple-element.28.dq_own, bf16[4,256,128]{2,1,0:T(8,128)(2,1)S(1)} %collective-permute-done.3.dq_peer), custom_call_target="tpu_custom_call" | custom-call | flops 536870912 | bytes 1048576 | tf_op jit(solution)/shard_map/place_q/pallas_call | solution.py:490
  60.2 0.0 collective-permute-done.7.delta_d
  60.2 2.0 %collective-permute-done.6.delta_c = f32[8,128]{1,0:T(8,128)S(1)} collective-permute-done((f32[8,128]{1,0:T(8,128)S(1)}, f32[8,128]{1,0:T(8,128)S(1)}, u32[]{:S(2)}, u32[]{:S(2)}) %collective-permute-start.6) | collective-permute-done | bytes 4128 | tf_op jit(solution)/shard_map/ppermute | solution.py:487
  62.2 0.0 collective-permute-done.5.delta_b
  62.2 0.8 %place_logit.1 = bf16[4,128]{1,0:T(4,128)(2,1)} custom-call(s32[1,128]{1,0:T(1,128)S(1)} %bitcast.6, f32[16,128]{1,0:T(8,128)S(1)} %get-tuple-element.34.closed_ref, f32[8,128]{1,0:T(8,128)S(1)} %add.3.delta_a, f32[8,128]{1,0:T(8,128)S(1)} %collective-permute-done.5.delta_b, f32[8,128]{1,0:T(8,128)S(1)} %collective-permute-done.6.delta_c, ...), custom_call_target="tpu_custom_call" | custom-call | flops 268435456 | bytes 1048576 | tf_op jit(solution)/shard_map/place_logit/pallas_call | solution.py:499
  63.0 0.0 all-to-all-done.1.dkv_ref
  63.0 1.0 %place_kv.1 = (bf16[512,128]{1,0:T(8,128)(2,1)}, bf16[512,128]{1,0:T(8,128)(2,1)}) custom-call(s32[1,128]{1,0:T(1,128)S(1)} %bitcast.7, bf16[16,128,256]{2,1,0:T(8,128)(2,1)S(1)} %all-to-all-done.1.dkv_ref), custom_call_target="tpu_custom_call" | custom-call | tf_op jit(solution)/shard_map/place_kv/pallas_call | solution.py:508
  (5 shorter events, 0.0 us)
Async XLA Ops:
  3.0 23.3 %all-to-all-start = ((bf16[16,128,256]{2,1,0:T(8,128)(2,1)}), bf16[16,128,256]{2,1,0:T(8,128)(2,1)S(1)}, u32[]{:S(2)}, u32[]{:S(2)}) async-start(bf16[16,128,256]{2,1,0:T(8,128)(2,1)} %pick_kv.1), calls=%async_computation | async-start | bytes 2097152 | tf_op jit(solution)/shard_map/all_to_all | solution.py:425
  11.2 0.7 %copy-start = (s32[128]{0:T(128)S(1)}, s32[128]{0:T(128)}, u32[]{:S(2)}) copy-start(s32[128]{0:T(128)} %param.11) | copy-start | bytes 1540
  11.9 1.2 %copy-start.2 = (bf16[512,1024]{1,0:T(8,128)(2,1)S(1)}, bf16[512,1024]{1,0:T(8,128)(2,1)}, u32[]{:S(2)}) copy-start(bf16[512,1024]{1,0:T(8,128)(2,1)} %q_hbm.1) | copy-start | bytes 3145732
  13.1 1.2 %copy-start.3 = (bf16[512,1024]{1,0:T(8,128)(2,1)S(1)}, bf16[512,1024]{1,0:T(8,128)(2,1)}, u32[]{:S(2)}) copy-start(bf16[512,1024]{1,0:T(8,128)(2,1)} %up_hbm.1) | copy-start | bytes 3145732
  15.3 2.0 %collective-permute-start.1 = (bf16[2,4,256,128]{3,2,1,0:T(8,128)(2,1)S(1)}, bf16[2,4,256,128]{3,2,1,0:T(8,128)(2,1)S(1)}, u32[]{:S(2)}, u32[]{:S(2)}) collective-permute-start(bf16[2,4,256,128]{3,2,1,0:T(8,128)(2,1)S(1)} %pick_q.1.own_ref), channel_id=1, source_target_pairs={{0,8},{8,0},{1,9},{9,1},{2,10},{10,2},{3,11},{11,3},{4,12},{12,4},... | collective-permute-start | bytes 1572872 | tf_op jit(solution)/shard_map/ppermute | solution.py:442
  15.4 1.9 %collective-permute-start = (s32[1,128]{1,0:T(1,128)S(1)}, s32[1,128]{1,0:T(1,128)S(1)}, u32[]{:S(2)}, u32[]{:S(2)}) collective-permute-start(s32[1,128]{1,0:T(1,128)S(1)} %bitcast.4), channel_id=1, source_target_pairs={{0,8},{8,0},{1,9},{9,1},{2,10},{10,2},{3,11},{11,3},{4,12},{12,4},... | collective-permute-start | bytes 1544 | tf_op jit(solution)/shard_map/ppermute | solution.py:443
  28.7 1.4 %collective-permute-start.2 = (f32[9,8,256]{2,1,0:T(8,128)S(1)}, f32[9,8,256]{2,1,0:T(8,128)S(1)}, u32[]{:S(2)}, u32[]{:S(2)}) collective-permute-start(f32[9,8,256]{2,1,0:T(8,128)S(1)} %get-tuple-element.25.stats_ref), channel_id=1, source_target_pairs={{0,8},{8,0},{1,9},{9,1},{2,10},{10,2},{3,11},{11,3},{4,12},{12,4},... | collective-permute-start | bytes 221192 | tf_op jit(solution)/shard_map/ppermute | solution.py:462
  30.1 28.7 %copy-start.1 = (s32[128]{0:T(128)S(1)}, s32[128]{0:T(128)}, u32[]{:S(2)}) copy-start(s32[128]{0:T(128)} %param.11) | copy-start | bytes 1540
  34.0 29.0 %all-to-all-start.1 = ((bf16[16,128,256]{2,1,0:T(8,128)(2,1)}), bf16[16,128,256]{2,1,0:T(8,128)(2,1)S(1)}, u32[]{:S(2)}, u32[]{:S(2)}) async-start(bf16[16,128,256]{2,1,0:T(8,128)(2,1)} %get-tuple-element.31), calls=%async_computation.1 | async-start | bytes 2097152 | tf_op jit(solution)/shard_map/all_to_all | solution.py:484
  45.5 13.3 %collective-permute-start.3 = (bf16[4,256,128]{2,1,0:T(8,128)(2,1)S(1)}, bf16[4,256,128]{2,1,0:T(8,128)(2,1)S(1)}, u32[]{:S(2)}, u32[]{:S(2)}) collective-permute-start(bf16[4,256,128]{2,1,0:T(8,128)(2,1)S(1)} %get-tuple-element.29), channel_id=1, source_target_pairs={{0,8},{8,0},{1,9},{9,1},{2,10},{10,2},{3,11},{11,3},{4,12},{12,4},... | collective-permute-start | bytes 786440 | tf_op jit(solution)/shard_map/ppermute | solution.py:489
  45.5 8.9 %collective-permute-start.4 = (f32[8,128]{1,0:T(8,128)S(1)}, f32[8,128]{1,0:T(8,128)S(1)}, u32[]{:S(2)}, u32[]{:S(2)}) collective-permute-start(f32[8,128]{1,0:T(8,128)S(1)} %get-tuple-element.35), channel_id=1, source_target_pairs={{0,4},{1,5},{2,6},{3,7},{4,0},{5,1},{6,2},{7,3},{8,12},{9,13},{10,... | collective-permute-start | bytes 12296 | tf_op jit(solution)/shard_map/ppermute | solution.py:485
  54.4 5.8 %collective-permute-start.7 = (f32[8,128]{1,0:T(8,128)S(1)}, f32[8,128]{1,0:T(8,128)S(1)}, u32[]{:S(2)}, u32[]{:S(2)}) collective-permute-start(f32[8,128]{1,0:T(8,128)S(1)} %add.3.delta_a), channel_id=1, source_target_pairs={{0,3},{1,2},{2,1},{3,0},{4,7},{5,6},{6,5},{7,4},{8,11},{9,10},{10,... | collective-permute-start | bytes 12296 | tf_op jit(solution)/shard_map/ppermute | solution.py:487
  57.7 4.5 %collective-permute-start.6 = (f32[8,128]{1,0:T(8,128)S(1)}, f32[8,128]{1,0:T(8,128)S(1)}, u32[]{:S(2)}, u32[]{:S(2)}) collective-permute-start(f32[8,128]{1,0:T(8,128)S(1)} %add.3.delta_a), channel_id=1, source_target_pairs={{0,2},{1,3},{2,0},{3,1},{4,6},{5,7},{6,4},{7,5},{8,10},{9,11},{10,... | collective-permute-start | bytes 12296 | tf_op jit(solution)/shard_map/ppermute | solution.py:487
  57.7 4.5 %collective-permute-start.5 = (f32[8,128]{1,0:T(8,128)S(1)}, f32[8,128]{1,0:T(8,128)S(1)}, u32[]{:S(2)}, u32[]{:S(2)}) collective-permute-start(f32[8,128]{1,0:T(8,128)S(1)} %add.3.delta_a), channel_id=1, source_target_pairs={{0,1},{1,0},{2,3},{3,2},{4,5},{5,4},{6,7},{7,6},{8,9},{9,8},{10,11... | collective-permute-start | bytes 12296 | tf_op jit(solution)/shard_map/ppermute | solution.py:487

commit v4 on v3

--- a/solution.py
+++ b/solution.py
@@ -173,8 +173,8 @@
 
 
 def stats_kernel(
-    peer_picked, kv_ref, own_ref, oth_ref, kc_out, vc_out, q_out, s_out, stats_out, scores_out,
-    pushed_out, info_out, k_pack, v_pack,
+    peer_picked, kv_ref, own_ref, oth_ref, kc_out, vc_out, q_out, s_out, stats_out, raised_out,
+    pushed_out, tops_out, info_out, k_pack, v_pack,
 ):
     chip = lax.axis_index("y") * 4 + lax.axis_index("x")
     core = lax.axis_index("c")
@@ -230,7 +230,6 @@
             scores = nt_dot(kc_out[pl.ds(base, keys), :], q_rows)
             pushed = nt_dot(vc_out[pl.ds(base, keys), :], s_rows)
             if kept:
-                scores_out[tile, pl.ds(base, keys), :] = scores
                 pushed_out[tile, pl.ds(base, keys), :] = pushed
             for u in range(0, keys, PART):
                 part = scores[u : u + PART] * LOG_FACTOR
@@ -240,6 +239,10 @@
                 part = part.reshape(PART // 8, 8, 2 * ROWS)
                 new_top = jnp.maximum(top, jnp.max(part, axis=0))
                 raised = jnp.exp2(part - new_top[None])
+                if kept:
+                    rows = pl.ds(pl.multiple_of(base + u, PART), PART)
+                    raised_out[tile, rows, :] = raised.reshape(PART, 2 * ROWS)
+                    tops_out[tile, lax.div(base + u, PART)] = new_top
                 fade = jnp.exp2(top - new_top)
                 total = total * fade + jnp.sum(raised, axis=0)
                 pulled = raised * pushed[u : u + PART].reshape(PART // 8, 8, 2 * ROWS)
@@ -267,7 +270,7 @@
 
 
 def grad_kernel(
-    info_ref, kc_ref, vc_ref, q_ref, s_ref, stats_ref, peer_ref, scores_ref, pushed_ref, dkv_out, dq_own, dq_oth, delta_out,
+    info_ref, kc_ref, vc_ref, q_ref, s_ref, stats_ref, peer_ref, raised_ref, pushed_ref, tops_ref, dkv_out, dq_own, dq_oth, delta_out,
     dk_sum, dv_sum, dq_sum, message, sems,
 ):
     core = lax.axis_index("c")
@@ -305,15 +308,21 @@
             span = pl.ds(base, keys)
             key_rows = kc_ref[span, :]
             if kept:
-                scores = scores_ref[tile, span, :]
                 pushed = pushed_ref[tile, span, :]
+                parts = []
+                for u in range(0, keys, PART):
+                    rows = pl.ds(pl.multiple_of(base + u, PART), PART)
+                    scale = jnp.exp2(tops_ref[tile, lax.div(base + u, PART)] - level)
+                    part = raised_ref[tile, rows, :].reshape(PART // 8, 8, 2 * ROWS)
+                    parts.append((part * scale[None]).reshape(PART, 2 * ROWS))
+                weights = jnp.concatenate(parts, axis=0)
             else:
                 scores = nt_dot(key_rows, q_rows)
                 pushed = nt_dot(vc_ref[span, :], s_rows)
-            weights = jnp.exp2(scores * LOG_FACTOR - level)
-            if limits is not None:
-                index = lax.broadcasted_iota(jnp.int32, (keys, 2 * ROWS), 0)
-                weights = jnp.where(index < limits - base, weights, 0.0)
+                weights = jnp.exp2(scores * LOG_FACTOR - level)
+                if limits is not None:
+                    index = lax.broadcasted_iota(jnp.int32, (keys, 2 * ROWS), 0)
+                    weights = jnp.where(index < limits - base, weights, 0.0)
             slopes = (weights * (pushed - delta)).astype(BF16)
             dv_sum[span, :] += jnp.dot(
                 weights.astype(BF16), s_rows, preferred_element_type=F32
@@ -351,7 +360,7 @@
 def place_q_kernel(picked_ref, gate_ref, dq_own, dq_peer, q_out, closed_out):
     placed = place_matrix(picked_ref[...])
     scatter = placed.astype(BF16)
-    closed_out[...] = 1.0 - switch_of(gate_ref[...], placed)
+    closed_out[...] = 1.0 - switch_of(gate_ref[...], placed)[0:8]
     for h in range(GROUP):
         rows = slice(h * CHUNK, (h + 1) * CHUNK)
         parts = [
@@ -363,16 +372,9 @@
         ).astype(BF16)
 
 
-def place_logit_kernel(picked_ref, closed_ref, delta_a, delta_b, delta_c, delta_d, logit_out):
-    scatter = place_matrix(picked_ref[...]).astype(BF16)
-    deltas = (delta_a[0:1, :] + delta_b[0:1, :]) + (delta_c[0:1, :] + delta_d[0:1, :])
-    logit_rows = (closed_ref[...] * deltas).astype(BF16)
-    for part in range(TOKENS // SLOTS):
-        rows = slice(part * SLOTS, (part + 1) * SLOTS)
-        logit_out[part : part + 1, :] = nt_dot(logit_rows, scatter[rows])[0:1].astype(BF16)
-
-
-def place_kv_kernel(picked_ref, dkv_ref, k_out, v_out):
+def place_kv_kernel(
+    picked_ref, dkv_ref, part_a, part_b, part_c, part_d, k_out, v_out, logit_out
+):
     scatter = place_matrix(picked_ref[...]).astype(BF16)
     total = dkv_ref[0].astype(F32)
     for s in range(1, CHIPS):
@@ -381,6 +383,11 @@
     v_rows = total[:, HEAD : 2 * HEAD].astype(BF16)
     k_out[...] = jnp.dot(scatter, k_rows, preferred_element_type=F32).astype(BF16)
     v_out[...] = jnp.dot(scatter, v_rows, preferred_element_type=F32).astype(BF16)
+    logits = (part_a[...] + part_b[...]) + (part_c[...] + part_d[...])
+    logit_rows = jnp.concatenate([logits, logits], axis=0).astype(BF16)
+    for part in range(TOKENS // SLOTS):
+        rows = slice(part * SLOTS, (part + 1) * SLOTS)
+        logit_out[part : part + 1, :] = nt_dot(logit_rows, scatter[rows])[0:1].astype(BF16)
 
 
 def whole(count):
@@ -441,7 +448,7 @@
     )(picked_row, gate_row, head_queries, upstream)
     qs_peer = lax.ppermute(qs_own, "c", swap)
     peer_picked = lax.ppermute(picked_row, "c", swap)
-    kc, vc, q_rows, s_rows, stats, scores, pushed, info = pl.pallas_call(
+    kc, vc, q_rows, s_rows, stats, raised, pushed, tops, info = pl.pallas_call(
         stats_kernel,
         out_shape=(
             shape((PICKED, HEAD)),
@@ -451,10 +458,11 @@
             shape((SPARE + 1, 8, ROWS), F32),
             shape((CHUNKS, KEPT, 2 * ROWS), F32),
             shape((CHUNKS, KEPT, 2 * ROWS), F32),
+            shape((CHUNKS, KEPT // PART, 8, 2 * ROWS), F32),
             shape((32,), jnp.int32),
         ),
         in_specs=whole(4),
-        out_specs=tuple(whole(7)) + (pl.BlockSpec(memory_space=pltpu.SMEM),),
+        out_specs=tuple(whole(8)) + (pl.BlockSpec(memory_space=pltpu.SMEM),),
         scratch_shapes=[pltpu.VMEM((PICKED + SLOTS + KEYS, HEAD), F32)] * 2,
         compiler_params=params(KERNEL_BYTES),
         name="stats",
@@ -468,7 +476,7 @@
             shape((CHUNKS, ROWS, HEAD)),
             shape((8, SLOTS), F32),
         ),
-        in_specs=[pl.BlockSpec(memory_space=pltpu.SMEM)] + whole(8),
+        in_specs=[pl.BlockSpec(memory_space=pltpu.SMEM)] + whole(9),
         out_specs=tuple(hbm(1) + whole(3)),
         scratch_shapes=[
             pltpu.VMEM((PICKED + SLOTS, HEAD), F32),
@@ -480,39 +488,35 @@
         compiler_params=params(KERNEL_BYTES),
         cost_estimate=cost(1 << 32),
         name="grads",
-    )(info, kc, vc, q_rows, s_rows, stats, stats_peer, scores, pushed)
+    )(info, kc, vc, q_rows, s_rows, stats, stats_peer, raised, pushed, tops)
     dkv_all = lax.all_to_all(dkv, ("x", "y"), 0, 0, tiled=True)
-    delta_half = deltas + lax.ppermute(deltas, "tp", [(i, i ^ 4) for i in range(8)])
-    delta_parts = [delta_half] + [
-        lax.ppermute(delta_half, "tp", [(i, i ^ k) for i in range(8)]) for k in (1, 2, 3)
-    ]
+    delta_far = lax.ppermute(deltas, "tp", [(i, i ^ 4) for i in range(8)])
     dq_peer = lax.ppermute(dq_oth, "c", swap)
     q_out, closed = pl.pallas_call(
         place_q_kernel,
-        out_shape=(shape((TOKENS, GROUP * HEAD)), shape((16, SLOTS), F32)),
+        out_shape=(shape((TOKENS, GROUP * HEAD)), shape((8, SLOTS), F32)),
         in_specs=whole(4),
         out_specs=tuple(whole(2)),
         compiler_params=params(),
         cost_estimate=cost(1 << 29),
         name="place_q",
     )(picked_row, gate_row, dq_own, dq_peer)
-    logit_out = pl.pallas_call(
-        place_logit_kernel,
-        out_shape=shape((TOKENS // SLOTS, SLOTS)),
+    logit_half = (deltas + delta_far) * closed
+    logit_parts = [logit_half] + [
+        lax.ppermute(logit_half, "tp", [(i, i ^ k) for i in range(8)]) for k in (1, 2, 3)
+    ]
+    k_out, v_out, logit_out = pl.pallas_call(
+        place_kv_kernel,
+        out_shape=(
+            shape((TOKENS, HEAD)),
+            shape((TOKENS, HEAD)),
+            shape((TOKENS // SLOTS, SLOTS)),
+        ),
         in_specs=whole(6),
-        out_specs=whole(1)[0],
-        compiler_params=params(),
-        cost_estimate=cost(1 << 28),
-        name="place_logit",
-    )(picked_row, closed, *delta_parts)
-    k_out, v_out = pl.pallas_call(
-        place_kv_kernel,
-        out_shape=(shape((TOKENS, HEAD)), shape((TOKENS, HEAD))),
-        in_specs=whole(2),
-        out_specs=tuple(whole(2)),
+        out_specs=tuple(whole(3)),
         compiler_params=params(),
         name="place_kv",
-    )(picked_row, dkv_all)
+    )(picked_row, dkv_all, *logit_parts)
     return q_out, k_out, v_out, logit_out.reshape(TOKENS)
 
 

time: 64.5 us -> 62.3 us (0.966)
  the two profiles are of different devices: /device:TPU:2 before, /device:TPU:64 now
where the time goes in v4:
time: 62.3 us; the launch traced here: 61.8 us
  starting transfers between devices  24.8 us (40%)
  waiting for transfers between devices  20.4 us (33%)
  Pallas kernels  12.1 us (19%)
  local copies, waits for them, and re-layouts  3.79 us (6%)
  between operations  0.72 us (1%)
    all_to_all x1, waiting for transfers between devices, local(): kv_all = lax.all_to_all(kv_copies, ('y', 'x'), 0, 0, tiled=True)  10.9 us
    all_to_all x1, starting transfers between devices, local(): dkv_all = lax.all_to_all(dkv, ('x', 'y'), 0, 0, tiled=True)  7.23 us
    all_to_all x1, starting transfers between devices, local(): kv_all = lax.all_to_all(kv_copies, ('y', 'x'), 0, 0, tiled=True)  7.05 us
    ppermute x1, starting transfers between devices, local(): delta_far = lax.ppermute(deltas, 'tp', [(i, i ^ 4) for i in range(8)])  5.48 us
    ppermute x3, starting transfers between devices, local(): lax.ppermute(logit_half, 'tp', [(i, i ^ k) for i in range(8)])  4.28 us
    pallas_call x1, Pallas kernels, local(): pl.pallas_call(grad_kernel, out_shape=(shape((CHIPS, SLOTS, 2 * HEAD)), s...  3.84 us
    ppermute x3, waiting for transfers between devices, local(): lax.ppermute(logit_half, 'tp', [(i, i ^ k) for i in range(8)])  3.6 us
    unnamed x8, local copies, waits for them, and re-layouts  3.11 us
  transfers between devices with their start and end apart: 10, of which 7 were waited for; matrix products, arithmetic and copies ran while one was open for 1% of the time, Pallas kernels for 4%

profile of v4, /device:TPU:64, one launch (start us, length us, event | category | flops | bytes accessed | tf_op | source)
XLA Modules:
  0.0 61.8 jit_solution(14350506587434025262)
XLA Ops:
  0.6 2.4 %pick_kv.1 = bf16[16,128,256]{2,1,0:T(8,128)(2,1)} custom-call(s32[1,128]{1,0:T(1,128)} %bitcast.2, bf16[512,128]{1,0:T(8,128)(2,1)} %k_hbm.1, bf16[512,128]{1,0:T(8,128)(2,1)} %v_hbm.1), custom_call_target="tpu_custom_call" | custom-call | tf_op jit(solution)/shard_map/pick_kv/pallas_call | solution.py:416
  3.0 7.0 %all-to-all-start = ((bf16[16,128,256]{2,1,0:T(8,128)(2,1)}), bf16[16,128,256]{2,1,0:T(8,128)(2,1)S(1)}, u32[]{:S(2)}, u32[]{:S(2)}) async-start(bf16[16,128,256]{2,1,0:T(8,128)(2,1)} %pick_kv.1), calls=%async_computation | async-start | bytes 2097152 | tf_op jit(solution)/shard_map/all_to_all | solution.py:432
  10.1 0.7 %reshape.18.gate_ref = bf16[1,512]{1,0:T(2,128)(2,1)S(1)} reshape(bf16[512]{0:T(512)(128)(2,1)} %param.9) | data formatting | bytes 2048 | tf_op jit(solution)/shard_map/reshape | solution.py:433
  10.8 0.0 copy-start
  10.8 0.7 %copy-done = s32[128]{0:T(128)S(1)} copy-done((s32[128]{0:T(128)S(1)}, s32[128]{0:T(128)}, u32[]{:S(2)}) %copy-start) | copy-done | bytes 536
  11.4 1.2 %copy-done.2 = bf16[512,1024]{1,0:T(8,128)(2,1)S(1)} copy-done((bf16[512,1024]{1,0:T(8,128)(2,1)S(1)}, bf16[512,1024]{1,0:T(8,128)(2,1)}, u32[]{:S(2)}) %copy-start.2) | copy-done | bytes 1048600
  12.7 1.2 %copy-done.3 = bf16[512,1024]{1,0:T(8,128)(2,1)S(1)} copy-done((bf16[512,1024]{1,0:T(8,128)(2,1)S(1)}, bf16[512,1024]{1,0:T(8,128)(2,1)}, u32[]{:S(2)}) %copy-start.3) | copy-done | bytes 1048600
  13.9 1.0 %pick_q.1.own_ref = bf16[2,4,256,128]{3,2,1,0:T(8,128)(2,1)S(1)} custom-call(s32[1,128]{1,0:T(1,128)S(1)} %bitcast.3, bf16[1,512]{1,0:T(2,128)(2,1)S(1)} %reshape.18.gate_ref, bf16[512,1024]{1,0:T(8,128)(2,1)S(1)} %copy-done.2, bf16[512,1024]{1,0:T(8,128)(2,1)S(1)} %copy-done.3), custom_call_target="tpu_custom_call" | custom-call | flops 1073741824 | bytes 1048576 | tf_op jit(solution)/shard_map/pick_q/pallas_call | solution.py:434
  14.8 0.1 collective-permute-start.1
  14.9 0.5 collective-permute-start
  15.4 1.4 %collective-permute-done.peer_picked = s32[1,128]{1,0:T(1,128)S(1)} collective-permute-done((s32[1,128]{1,0:T(1,128)S(1)}, s32[1,128]{1,0:T(1,128)S(1)}, u32[]{:S(2)}, u32[]{:S(2)}) %collective-permute-start) | collective-permute-done | bytes 544 | tf_op jit(solution)/shard_map/ppermute | solution.py:450
  16.8 0.0 collective-permute-done.1.oth_ref
  16.8 10.9 %all-to-all-done.kv_ref = bf16[16,128,256]{2,1,0:T(8,128)(2,1)S(1)} async-done(((bf16[16,128,256]{2,1,0:T(8,128)(2,1)}), bf16[16,128,256]{2,1,0:T(8,128)(2,1)S(1)}, u32[]{:S(2)}, u32[]{:S(2)}) %all-to-all-start) | async-done | bytes 1048608 | tf_op jit(solution)/shard_map/all_to_all | solution.py:432
  27.7 2.4 %stats.1 = (bf16[2048,128]{1,0:T(8,128)(2,1)S(1)}, bf16[2048,128]{1,0:T(8,128)(2,1)S(1)}, bf16[2304,128]{1,0:T(8,128)(2,1)S(1)}, bf16[2304,128]{1,0:T(8,128)(2,1...) custom-call(s32[1,128]{1,0:T(1,128)S(1)} %collective-permute-done.pe, ...), custom_call_target="tpu_custom_call" | custom-call | tf_op jit(solution)/shard_map/stats/pallas_call | solution.py:451
  30.2 0.1 collective-permute-start.2
  30.3 1.3 %collective-permute-done.2.peer_ref = f32[9,8,256]{2,1,0:T(8,128)S(1)} collective-permute-done((f32[9,8,256]{2,1,0:T(8,128)S(1)}, f32[9,8,256]{2,1,0:T(8,128)S(1)}, u32[]{:S(2)}, u32[]{:S(2)}) %collective-permute-start.2) | collective-permute-done | bytes 73760 | tf_op jit(solution)/shard_map/ppermute | solution.py:470
  31.5 3.8 %grads.1 = (bf16[16,128,256]{2,1,0:T(8,128)(2,1)}, f32[4,256,128]{2,1,0:T(8,128)S(1)}, bf16[4,256,128]{2,1,0:T(8,128)(2,1)S(1)}, f32[8,128]{1,0:T(8,128)S(1)}) custom-call(s32[32]{0:T(128)S(1)} %get-tuple-element.22.info_ref, bf16[2048,128]{1,0:T(8,128)(2,1)S(1)} %get-tuple-element.23.kc_ref, bf16[2048,128]{1,0:T(8,128)(2,1)S(1)} %get-tuple-element.24.vc_ref, ...), custom_call_target="tpu_custom_call" | custom-call | flops 4294967296 | bytes 1048576 | tf_op jit(solution)/shard_map/grads/pallas_call | solution.py:471
  35.4 7.2 %all-to-all-start.1 = ((bf16[16,128,256]{2,1,0:T(8,128)(2,1)}), bf16[16,128,256]{2,1,0:T(8,128)(2,1)S(1)}, u32[]{:S(2)}, u32[]{:S(2)}) async-start(bf16[16,128,256]{2,1,0:T(8,128)(2,1)} %get-tuple-element.34), calls=%async_computation.1 | async-start | bytes 2097152 | tf_op jit(solution)/shard_map/all_to_all | solution.py:492
  42.6 0.1 collective-permute-start.3
  42.7 5.5 %collective-permute-start.4 = (f32[8,128]{1,0:T(8,128)S(1)}, f32[8,128]{1,0:T(8,128)S(1)}, u32[]{:S(2)}, u32[]{:S(2)}) collective-permute-start(f32[8,128]{1,0:T(8,128)S(1)} %get-tuple-element.35), channel_id=1, source_target_pairs={{0,4},{1,5},{2,6},{3,7},{4,0},{5,1},{6,2},{7,3},{8,12},{9,13},{10,... | collective-permute-start | bytes 12296 | tf_op jit(solution)/shard_map/ppermute | solution.py:493
  48.2 0.0 collective-permute-done.3.dq_peer
  48.2 0.0 copy-done.1
  48.2 1.4 %place_q.1 = (bf16[512,1024]{1,0:T(8,128)(2,1)}, f32[8,128]{1,0:T(8,128)S(1)}) custom-call(s32[1,128]{1,0:T(1,128)S(1)} %bitcast.5, bf16[1,512]{1,0:T(2,128)(2,1)S(1)} %reshape.18.gate_ref, f32[4,256,128]{2,1,0:T(8,128)S(1)} %get-tuple-element.31.dq_own, bf16[4,256,128]{2,1,0:T(8,128)(2,1)S(1)} %collective-permute-done.3.dq_peer), custom_call_target="tpu_custom_call" | custom-call | flops 536870912 | bytes 1048576 | tf_op jit(solution)/shard_map/place_q/pallas_call | solution.py:495
  49.6 0.7 %collective-permute-done.4 = f32[8,128]{1,0:T(8,128)S(1)} collective-permute-done((f32[8,128]{1,0:T(8,128)S(1)}, f32[8,128]{1,0:T(8,128)S(1)}, u32[]{:S(2)}, u32[]{:S(2)}) %collective-permute-start.4) | collective-permute-done | bytes 4128 | tf_op jit(solution)/shard_map/ppermute | solution.py:493
  50.3 0.5 collective-permute-start.7
  50.8 3.8 %collective-permute-start.6 = (f32[8,128]{1,0:T(8,128)S(1)}, f32[8,128]{1,0:T(8,128)S(1)}, u32[]{:S(2)}, u32[]{:S(2)}) collective-permute-start(f32[8,128]{1,0:T(8,128)S(1)} %add_multiply_fusion.part_a), channel_id=1, source_target_pairs={{0,2},{1,3},{2,0},{3,1},{4,6},{5,7},{6,4},{7,5},{8,10},{9,11},{10,... | collective-permute-start | bytes 12296 | tf_op jit(solution)/shard_map/ppermute | solution.py:506
  54.6 0.0 collective-permute-start.5
  54.6 0.0 collective-permute-done.7.part_d
  54.6 1.6 %collective-permute-done.6.part_c = f32[8,128]{1,0:T(8,128)S(1)} collective-permute-done((f32[8,128]{1,0:T(8,128)S(1)}, f32[8,128]{1,0:T(8,128)S(1)}, u32[]{:S(2)}, u32[]{:S(2)}) %collective-permute-start.6) | collective-permute-done | bytes 4128 | tf_op jit(solution)/shard_map/ppermute | solution.py:506
  56.2 2.0 %collective-permute-done.5.part_b = f32[8,128]{1,0:T(8,128)S(1)} collective-permute-done((f32[8,128]{1,0:T(8,128)S(1)}, f32[8,128]{1,0:T(8,128)S(1)}, u32[]{:S(2)}, u32[]{:S(2)}) %collective-permute-start.5) | collective-permute-done | bytes 4128 | tf_op jit(solution)/shard_map/ppermute | solution.py:506
  58.2 2.5 %all-to-all-done.1.dkv_ref = bf16[16,128,256]{2,1,0:T(8,128)(2,1)S(1)} async-done(((bf16[16,128,256]{2,1,0:T(8,128)(2,1)}), bf16[16,128,256]{2,1,0:T(8,128)(2,1)S(1)}, u32[]{:S(2)}, u32[]{:S(2)}) %all-to-all-start.1) | async-done | bytes 1048608 | tf_op jit(solution)/shard_map/all_to_all | solution.py:492
  60.8 1.0 %place_kv.1 = (bf16[512,128]{1,0:T(8,128)(2,1)}, bf16[512,128]{1,0:T(8,128)(2,1)}, bf16[4,128]{1,0:T(4,128)(2,1)}) custom-call(s32[1,128]{1,0:T(1,128)S(1)} %bitcast.6, bf16[16,128,256]{2,1,0:T(8,128)(2,1)S(1)} %all-to-all-done.1.dkv_ref, f32[8,128]{1,0:T(8,128)S(1)} %add_multiply_fusion.part_a, f32[8,128]{1,0:T(8,128)S(1)} %collective-permute-done.5.part_b, ...), custom_call_target="tpu_custom_call" | custom-call | tf_op jit(solution)/shard_map/place_kv/pallas_call | solution.py:508
  (4 shorter events, 0.0 us)
Async XLA Ops:
  3.0 24.7 %all-to-all-start = ((bf16[16,128,256]{2,1,0:T(8,128)(2,1)}), bf16[16,128,256]{2,1,0:T(8,128)(2,1)S(1)}, u32[]{:S(2)}, u32[]{:S(2)}) async-start(bf16[16,128,256]{2,1,0:T(8,128)(2,1)} %pick_kv.1), calls=%async_computation | async-start | bytes 2097152 | tf_op jit(solution)/shard_map/all_to_all | solution.py:432
  10.8 0.7 %copy-start = (s32[128]{0:T(128)S(1)}, s32[128]{0:T(128)}, u32[]{:S(2)}) copy-start(s32[128]{0:T(128)} %param.11) | copy-start | bytes 1540
  11.4 1.2 %copy-start.2 = (bf16[512,1024]{1,0:T(8,128)(2,1)S(1)}, bf16[512,1024]{1,0:T(8,128)(2,1)}, u32[]{:S(2)}) copy-start(bf16[512,1024]{1,0:T(8,128)(2,1)} %q_hbm.1) | copy-start | bytes 3145732
  12.6 1.2 %copy-start.3 = (bf16[512,1024]{1,0:T(8,128)(2,1)S(1)}, bf16[512,1024]{1,0:T(8,128)(2,1)}, u32[]{:S(2)}) copy-start(bf16[512,1024]{1,0:T(8,128)(2,1)} %up_hbm.1) | copy-start | bytes 3145732
  14.8 2.0 %collective-permute-start.1 = (bf16[2,4,256,128]{3,2,1,0:T(8,128)(2,1)S(1)}, bf16[2,4,256,128]{3,2,1,0:T(8,128)(2,1)S(1)}, u32[]{:S(2)}, u32[]{:S(2)}) collective-permute-start(bf16[2,4,256,128]{3,2,1,0:T(8,128)(2,1)S(1)} %pick_q.1.own_ref), channel_id=1, source_target_pairs={{0,8},{8,0},{1,9},{9,1},{2,10},{10,2},{3,11},{11,3},{4,12},{12,4},... | collective-permute-start | bytes 1572872 | tf_op jit(solution)/shard_map/ppermute | solution.py:449
  14.9 1.9 %collective-permute-start = (s32[1,128]{1,0:T(1,128)S(1)}, s32[1,128]{1,0:T(1,128)S(1)}, u32[]{:S(2)}, u32[]{:S(2)}) collective-permute-start(s32[1,128]{1,0:T(1,128)S(1)} %bitcast.4), channel_id=1, source_target_pairs={{0,8},{8,0},{1,9},{9,1},{2,10},{10,2},{3,11},{11,3},{4,12},{12,4},... | collective-permute-start | bytes 1544 | tf_op jit(solution)/shard_map/ppermute | solution.py:450
  30.2 1.4 %collective-permute-start.2 = (f32[9,8,256]{2,1,0:T(8,128)S(1)}, f32[9,8,256]{2,1,0:T(8,128)S(1)}, u32[]{:S(2)}, u32[]{:S(2)}) collective-permute-start(f32[9,8,256]{2,1,0:T(8,128)S(1)} %get-tuple-element.27.stats_ref), channel_id=1, source_target_pairs={{0,8},{8,0},{1,9},{9,1},{2,10},{10,2},{3,11},{11,3},{4,12},{12,4},... | collective-permute-start | bytes 221192 | tf_op jit(solution)/shard_map/ppermute | solution.py:470
  31.5 16.7 %copy-start.1 = (s32[128]{0:T(128)S(1)}, s32[128]{0:T(128)}, u32[]{:S(2)}) copy-start(s32[128]{0:T(128)} %param.11) | copy-start | bytes 1540
  35.4 25.4 %all-to-all-start.1 = ((bf16[16,128,256]{2,1,0:T(8,128)(2,1)}), bf16[16,128,256]{2,1,0:T(8,128)(2,1)S(1)}, u32[]{:S(2)}, u32[]{:S(2)}) async-start(bf16[16,128,256]{2,1,0:T(8,128)(2,1)} %get-tuple-element.34), calls=%async_computation.1 | async-start | bytes 2097152 | tf_op jit(solution)/shard_map/all_to_all | solution.py:492
  42.6 5.6 %collective-permute-start.3 = (bf16[4,256,128]{2,1,0:T(8,128)(2,1)S(1)}, bf16[4,256,128]{2,1,0:T(8,128)(2,1)S(1)}, u32[]{:S(2)}, u32[]{:S(2)}) collective-permute-start(bf16[4,256,128]{2,1,0:T(8,128)(2,1)S(1)} %get-tuple-element.32), channel_id=1, source_target_pairs={{0,8},{8,0},{1,9},{9,1},{2,10},{10,2},{3,11},{11,3},{4,12},{12,4},... | collective-permute-start | bytes 786440 | tf_op jit(solution)/shard_map/ppermute | solution.py:494
  42.7 7.6 %collective-permute-start.4 = (f32[8,128]{1,0:T(8,128)S(1)}, f32[8,128]{1,0:T(8,128)S(1)}, u32[]{:S(2)}, u32[]{:S(2)}) collective-permute-start(f32[8,128]{1,0:T(8,128)S(1)} %get-tuple-element.35), channel_id=1, source_target_pairs={{0,4},{1,5},{2,6},{3,7},{4,0},{5,1},{6,2},{7,3},{8,12},{9,13},{10,... | collective-permute-start | bytes 12296 | tf_op jit(solution)/shard_map/ppermute | solution.py:493
  50.3 4.3 %collective-permute-start.7 = (f32[8,128]{1,0:T(8,128)S(1)}, f32[8,128]{1,0:T(8,128)S(1)}, u32[]{:S(2)}, u32[]{:S(2)}) collective-permute-start(f32[8,128]{1,0:T(8,128)S(1)} %add_multiply_fusion.part_a), channel_id=1, source_target_pairs={{0,3},{1,2},{2,1},{3,0},{4,7},{5,6},{6,5},{7,4},{8,11},{9,10},{10,... | collective-permute-start | bytes 12296 | tf_op jit(solution)/shard_map/ppermute | solution.py:506
  50.8 5.4 %collective-permute-start.6 = (f32[8,128]{1,0:T(8,128)S(1)}, f32[8,128]{1,0:T(8,128)S(1)}, u32[]{:S(2)}, u32[]{:S(2)}) collective-permute-start(f32[8,128]{1,0:T(8,128)S(1)} %add_multiply_fusion.part_a), channel_id=1, source_target_pairs={{0,2},{1,3},{2,0},{3,1},{4,6},{5,7},{6,4},{7,5},{8,10},{9,11},{10,... | collective-permute-start | bytes 12296 | tf_op jit(solution)/shard_map/ppermute | solution.py:506
  54.6 3.6 %collective-permute-start.5 = (f32[8,128]{1,0:T(8,128)S(1)}, f32[8,128]{1,0:T(8,128)S(1)}, u32[]{:S(2)}, u32[]{:S(2)}) collective-permute-start(f32[8,128]{1,0:T(8,128)S(1)} %add_multiply_fusion.part_a), channel_id=1, source_target_pairs={{0,1},{1,0},{2,3},{3,2},{4,5},{5,4},{6,7},{7,6},{8,9},{9,8},{10,11... | collective-permute-start | bytes 12296 | tf_op jit(solution)/shard_map/ppermute | solution.py:506

commit v5 on v4

--- a/solution.py
+++ b/solution.py
@@ -117,10 +117,6 @@
     def place(self, chunk):
         place = jnp.where(chunk < self.own_chunks, chunk, CHUNKS + chunk - self.own_chunks)
         return jnp.where(chunk < self.live_chunks, place, SPARE)
-
-    def peer_place(self, chunk):
-        place = self.place(chunk)
-        return jnp.where(place == SPARE, SPARE, lax.rem(place + CHUNKS, 2 * CHUNKS))
 
     def limit(self, chunk):
         slot = lax.rem(lax.broadcasted_iota(jnp.int32, (1, ROWS), 1), CHUNK)
@@ -269,9 +265,34 @@
     lax.fori_loop(0, tiles.number, attend, 0)
 
 
+def combine_kernel(info_ref, stats_ref, peer_ref, comb_out, delta_out):
+    own_chunks = info_ref[18]
+    lane = lax.div(lax.broadcasted_iota(jnp.int32, (1, SLOTS), 1), CHUNK)
+    comb_out[SPARE] = jnp.zeros((8, ROWS), F32)
+    deltas = jnp.zeros((1, SLOTS), F32)
+    for place in range(SPARE):
+        mine = stats_ref[place]
+        theirs = peer_ref[(place + CHUNKS) % SPARE]
+        top = jnp.maximum(mine[0:1], theirs[0:1])
+        mine_scale = jnp.exp2(mine[0:1] - top)
+        their_scale = jnp.exp2(theirs[0:1] - top)
+        total = mine[1:2] * mine_scale + theirs[1:2] * their_scale
+        total = jnp.where(total > 0.0, total, 1.0)
+        delta = (mine[2:3] * mine_scale + theirs[2:3] * their_scale) / total
+        comb_out[place, 0:1, :] = top + jnp.log2(total)
+        comb_out[place, 1:2, :] = delta
+        if place < CHUNKS:
+            heads = delta[:, 0:128] + delta[:, 128:256]
+            heads = heads + pltpu.roll(heads, 64, 1)
+            heads = heads + pltpu.roll(heads, 32, 1)
+            mark = jnp.where(place < own_chunks, place, CHUNKS)
+            deltas = deltas + jnp.where(lane == mark, heads, 0.0)
+    delta_out[...] = jnp.broadcast_to(deltas, (8, SLOTS))
+
+
 def grad_kernel(
-    info_ref, kc_ref, vc_ref, q_ref, s_ref, stats_ref, peer_ref, raised_ref, pushed_ref, tops_ref, dkv_out, dq_own, dq_oth, delta_out,
-    dk_sum, dv_sum, dq_sum, message, sems,
+    info_ref, kc_ref, vc_ref, q_ref, s_ref, comb_ref, raised_ref, pushed_ref, tops_ref,
+    line_0, line_1, line_2, line_3, dq_own, dq_oth, dk_sum, dv_sum, dq_sum,
 ):
     core = lax.axis_index("c")
     tiles = Tiles(core, info_ref[16], info_ref[17], info_ref[18], info_ref[19])
@@ -279,29 +300,13 @@
     dv_sum[...] = jnp.zeros_like(dv_sum)
     dq_own[...] = jnp.zeros_like(dq_own)
     dq_oth[...] = jnp.zeros_like(dq_oth)
-    delta_out[...] = jnp.zeros_like(delta_out)
 
     def push_back(tile, _):
         q_rows = q_ref[pair_rows(tile), :]
         s_rows = s_ref[pair_rows(tile), :]
         chunks = (2 * tile, 2 * tile + 1)
-        mine = jnp.concatenate([stats_ref[tiles.place(c)] for c in chunks], axis=1)
-        theirs = jnp.concatenate([peer_ref[tiles.peer_place(c)] for c in chunks], axis=1)
-        top = jnp.maximum(mine[0:1], theirs[0:1])
-        mine_scale = jnp.exp2(mine[0:1] - top)
-        their_scale = jnp.exp2(theirs[0:1] - top)
-        total = mine[1:2] * mine_scale + theirs[1:2] * their_scale
-        total = jnp.where(total > 0.0, total, 1.0)
-        delta = (mine[2:3] * mine_scale + theirs[2:3] * their_scale) / total
-        level = top + jnp.log2(total)
-        lane = lax.div(lax.broadcasted_iota(jnp.int32, (1, SLOTS), 1), CHUNK)
-        for half, chunk in enumerate(chunks):
-            first = half * ROWS
-            heads = delta[:, first : first + 128] + delta[:, first + 128 : first + 256]
-            heads = heads + pltpu.roll(heads, 64, 1)
-            heads = heads + pltpu.roll(heads, 32, 1)
-            mark = jnp.where(chunk < tiles.own_chunks, chunk, CHUNKS)
-            delta_out[0:1, :] += jnp.where(lane == mark, heads, 0.0)
+        comb = jnp.concatenate([comb_ref[tiles.place(c)] for c in chunks], axis=1)
+        level, delta = comb[0:1], comb[1:2]
         dq_sum[...] = jnp.zeros_like(dq_sum)
 
         def block(base, keys, limits, kept, carry):
@@ -346,15 +351,14 @@
         return 0
 
     lax.fori_loop(0, tiles.number, push_back, 0)
-    copies = []
-    for s in range(CHIPS):
-        rows = pl.ds(info_ref[s], SLOTS)
-        message[s, :, 0:HEAD] = dk_sum[rows, :].astype(BF16)
-        message[s, :, HEAD : 2 * HEAD] = dv_sum[rows, :].astype(BF16)
-        copies.append(pltpu.make_async_copy(message.at[s], dkv_out.at[(s % 4) * 4 + s // 4], sems.at[s]))
-        copies[s].start()
-    for copy in copies:
-        copy.wait()
+    row, column = lax.axis_index("y"), lax.axis_index("x")
+    for k, line in enumerate((line_0, line_1, line_2, line_3)):
+        for j in range(4):
+            down, right = jnp.where(core == 0, k, j), jnp.where(core == 0, j, k)
+            chip = lax.rem(row + down, 4) * 4 + lax.rem(column + right, 4)
+            rows = pl.ds(info_ref[chip], SLOTS)
+            line[j, :, 0:HEAD] = dk_sum[rows, :].astype(BF16)
+            line[j, :, HEAD : 2 * HEAD] = dv_sum[rows, :].astype(BF16)
 
 
 def place_q_kernel(picked_ref, gate_ref, dq_own, dq_peer, q_out, closed_out):
@@ -373,17 +377,17 @@
 
 
 def place_kv_kernel(
-    picked_ref, dkv_ref, part_a, part_b, part_c, part_d, k_out, v_out, logit_out
+    picked_ref, closed_ref, own_ref, sum_1, sum_2, sum_3, part_a, part_b, k_out, v_out, logit_out
 ):
     scatter = place_matrix(picked_ref[...]).astype(BF16)
-    total = dkv_ref[0].astype(F32)
-    for s in range(1, CHIPS):
-        total = total + dkv_ref[s].astype(F32)
+    total = own_ref[...]
+    for other in (sum_1, sum_2, sum_3):
+        total = total + other[...].astype(F32)
     k_rows = (total[:, 0:HEAD] * FACTOR).astype(BF16)
     v_rows = total[:, HEAD : 2 * HEAD].astype(BF16)
     k_out[...] = jnp.dot(scatter, k_rows, preferred_element_type=F32).astype(BF16)
     v_out[...] = jnp.dot(scatter, v_rows, preferred_element_type=F32).astype(BF16)
-    logits = (part_a[...] + part_b[...]) + (part_c[...] + part_d[...])
+    logits = (part_a[...] + part_b[...]) * closed_ref[...]
     logit_rows = jnp.concatenate([logits, logits], axis=0).astype(BF16)
     for part in range(TOKENS // SLOTS):
         rows = slice(part * SLOTS, (part + 1) * SLOTS)
@@ -408,6 +412,20 @@
 
 def cost(flops):
     return pl.CostEstimate(flops=flops, bytes_accessed=1 << 20, transcendentals=0)
+
+
+def across(block, step, first):
+    def device(y, x, c):
+        return (y % 4 * 4 + x % 4) * 2 + c
+
+    pairs = []
+    for y in range(4):
+        for x in range(4):
+            for c in range(2):
+                along_x = (c == 0) == first
+                target = device(y, x + step, c) if along_x else device(y + step, x, c)
+                pairs.append((device(y, x, c), target))
+    return lax.ppermute(block, ("y", "x", "c"), pairs)
 
 
 def local(head_queries, key_projection_rows, value_projection_rows, gate_logit, upstream, picked):
@@ -468,28 +486,37 @@
         name="stats",
     )(peer_picked, kv_all, qs_own, qs_peer)
     stats_peer = lax.ppermute(stats, "c", swap)
-    dkv, dq_own, dq_oth, deltas = pl.pallas_call(
+    comb, deltas = pl.pallas_call(
+        combine_kernel,
+        out_shape=(shape((SPARE + 1, 8, ROWS), F32), shape((8, SLOTS), F32)),
+        in_specs=[pl.BlockSpec(memory_space=pltpu.SMEM)] + whole(2),
+        out_specs=tuple(whole(2)),
+        compiler_params=params(KERNEL_BYTES),
+        name="combine",
+    )(info, stats, stats_peer)
+    delta_near = lax.ppermute(deltas, "tp", [(i, i ^ 1) for i in range(8)])
+    *lines, dq_own, dq_oth = pl.pallas_call(
         grad_kernel,
-        out_shape=(
-            shape((CHIPS, SLOTS, 2 * HEAD)),
+        out_shape=(shape((4, SLOTS, 2 * HEAD)),) * 4
+        + (
             shape((CHUNKS, ROWS, HEAD), F32),
             shape((CHUNKS, ROWS, HEAD)),
-            shape((8, SLOTS), F32),
         ),
-        in_specs=[pl.BlockSpec(memory_space=pltpu.SMEM)] + whole(9),
-        out_specs=tuple(hbm(1) + whole(3)),
+        in_specs=[pl.BlockSpec(memory_space=pltpu.SMEM)] + whole(8),
+        out_specs=tuple(whole(6)),
         scratch_shapes=[
             pltpu.VMEM((PICKED + SLOTS, HEAD), F32),
             pltpu.VMEM((PICKED + SLOTS, HEAD), F32),
             pltpu.VMEM((2 * ROWS, HEAD), F32),
-            pltpu.VMEM((CHIPS, SLOTS, 2 * HEAD), BF16),
-            pltpu.SemaphoreType.DMA((CHIPS,)),
         ],
         compiler_params=params(KERNEL_BYTES),
         cost_estimate=cost(1 << 32),
         name="grads",
-    )(info, kc, vc, q_rows, s_rows, stats, stats_peer, raised, pushed, tops)
-    dkv_all = lax.all_to_all(dkv, ("x", "y"), 0, 0, tiled=True)
+    )(info, kc, vc, q_rows, s_rows, comb, raised, pushed, tops)
+    delta_near, *lines = lax.optimization_barrier((delta_near, *lines))
+    deltas = deltas + delta_near
+    lines = lines[:1] + [across(lines[k], k, False) for k in (1, 2, 3)]
+    sums = [sum(line[j].astype(F32) for line in lines) for j in range(4)]
     delta_far = lax.ppermute(deltas, "tp", [(i, i ^ 4) for i in range(8)])
     dq_peer = lax.ppermute(dq_oth, "c", swap)
     q_out, closed = pl.pallas_call(
@@ -501,10 +528,11 @@
         cost_estimate=cost(1 << 29),
         name="place_q",
     )(picked_row, gate_row, dq_own, dq_peer)
-    logit_half = (deltas + delta_far) * closed
-    logit_parts = [logit_half] + [
-        lax.ppermute(logit_half, "tp", [(i, i ^ k) for i in range(8)]) for k in (1, 2, 3)
-    ]
+    parts = [sums[j].astype(BF16) for j in (1, 2, 3)]
+    delta_far, *parts = lax.optimization_barrier((delta_far, *parts))
+    arrived = [across(parts[j - 1], j, True) for j in (1, 2, 3)]
+    logit_half = deltas + delta_far
+    logit_rest = lax.ppermute(logit_half, "tp", [(i, i ^ 2) for i in range(8)])
     k_out, v_out, logit_out = pl.pallas_call(
         place_kv_kernel,
         out_shape=(
@@ -512,11 +540,11 @@
             shape((TOKENS, HEAD)),
             shape((TOKENS // SLOTS, SLOTS)),
         ),
-        in_specs=whole(6),
+        in_specs=whole(8),
         out_specs=tuple(whole(3)),
         compiler_params=params(),
         name="place_kv",
-    )(picked_row, dkv_all, *logit_parts)
+    )(picked_row, closed, sums[0], *arrived, logit_half, logit_rest)
     return q_out, k_out, v_out, logit_out.reshape(TOKENS)
 
 

time: 62.3 us -> 61.6 us (0.989)
  waiting for transfers between devices: 20.4 us -> 19.5 us
  Pallas kernels: 12.1 us -> 11.4 us
    ppermute x3 -> x8, starting transfers between devices: 4.28 us -> 12.7 us  [the longest x6 10.7 us: across(): return lax.ppermute(block, ('y', 'x', 'c'), pairs)]
    all_to_all x1 -> x0, starting transfers between devices: 7.23 us -> none  [local(): dkv_all = lax.all_to_all(dkv, ('x', 'y'), 0, 0, tiled=True)]
    all_to_all x1 -> x0, waiting for transfers between devices: 2.54 us -> none  [local(): dkv_all = lax.all_to_all(dkv, ('x', 'y'), 0, 0, tiled=True)]
    ppermute x3 -> x8, waiting for transfers between devices: 3.6 us -> 5.63 us  [the longest x1 3.06 us: local(): logit_rest = lax.ppermute(logit_half, 'tp', [(i, i ^ 2) for i in range(8)])]
    ppermute x1, starting transfers between devices: 5.48 us -> 4.58 us  [local(): delta_far = lax.ppermute(deltas, 'tp', [(i, i ^ 4) for i in range(8)])]
    pallas_call x1 -> x2, Pallas kernels: 3.84 us -> 3.27 us  [the longest x1 2.52 us: local(): pl.pallas_call(grad_kernel, out_shape=(shape((4, SLOTS, 2 * HEAD)),) * 4...]
  transfers between devices with their start and end apart: 10 -> 14, of which waited for: 7 -> 6; matrix products, arithmetic and copies ran while one was open for 1% -> 1% of each run, Pallas kernels for 4% -> 8%
where the time goes in v5:
time: 61.6 us; the launch traced here: 60.6 us
  starting transfers between devices  25 us (41%)
  waiting for transfers between devices  19.5 us (32%)
  Pallas kernels  11.4 us (19%)
  local copies, waits for them, and re-layouts  3.79 us (6%)
  between operations  0.72 us (1%)
    all_to_all x1, waiting for transfers between devices, local(): kv_all = lax.all_to_all(kv_copies, ('y', 'x'), 0, 0, tiled=True)  10.9 us
    ppermute x6, starting transfers between devices, across(): return lax.ppermute(block, ('y', 'x', 'c'), pairs)  10.7 us
    all_to_all x1, starting transfers between devices, local(): kv_all = lax.all_to_all(kv_copies, ('y', 'x'), 0, 0, tiled=True)  7.05 us
    ppermute x1, starting transfers between devices, local(): delta_far = lax.ppermute(deltas, 'tp', [(i, i ^ 4) for i in range(8)])  4.58 us
    unnamed x8, local copies, waits for them, and re-layouts  3.11 us
    ppermute x1, waiting for transfers between devices, local(): logit_rest = lax.ppermute(logit_half, 'tp', [(i, i ^ 2) for i in range(8)])  3.06 us
    ppermute x6, waiting for transfers between devices, across(): return lax.ppermute(block, ('y', 'x', 'c'), pairs)  2.57 us
    pallas_call x1, Pallas kernels, local(): pl.pallas_call(grad_kernel, out_shape=(shape((4, SLOTS, 2 * HEAD)),) * 4...  2.52 us
  transfers between devices with their start and end apart: 14, of which 6 were waited for; matrix products, arithmetic and copies ran while one was open for 1% of the time, Pallas kernels for 8%

profile of v5, /device:TPU:64, one launch (start us, length us, event | category | flops | bytes accessed | tf_op | source)
XLA Modules:
  0.0 60.6 jit_solution(14030423206394491675)
XLA Ops:
  0.6 2.4 %pick_kv.1 = bf16[16,128,256]{2,1,0:T(8,128)(2,1)} custom-call(s32[1,128]{1,0:T(1,128)} %bitcast.10, bf16[512,128]{1,0:T(8,128)(2,1)} %k_hbm.1, bf16[512,128]{1,0:T(8,128)(2,1)} %v_hbm.1), custom_call_target="tpu_custom_call" | custom-call | tf_op jit(solution)/shard_map/pick_kv/pallas_call | solution.py:434
  3.0 7.1 %all-to-all-start = ((bf16[16,128,256]{2,1,0:T(8,128)(2,1)}), bf16[16,128,256]{2,1,0:T(8,128)(2,1)S(1)}, u32[]{:S(2)}, u32[]{:S(2)}) async-start(bf16[16,128,256]{2,1,0:T(8,128)(2,1)} %pick_kv.1), calls=%async_computation | async-start | bytes 2097152 | tf_op jit(solution)/shard_map/all_to_all | solution.py:450
  10.1 0.7 %reshape.49.gate_ref = bf16[1,512]{1,0:T(2,128)(2,1)S(1)} reshape(bf16[512]{0:T(512)(128)(2,1)} %param.9) | data formatting | bytes 2048 | tf_op jit(solution)/shard_map/reshape | solution.py:451
  10.8 0.7 %copy-done = s32[128]{0:T(128)S(1)} copy-done((s32[128]{0:T(128)S(1)}, s32[128]{0:T(128)}, u32[]{:S(2)}) %copy-start) | copy-done | bytes 536
  11.4 1.2 %copy-done.2 = bf16[512,1024]{1,0:T(8,128)(2,1)S(1)} copy-done((bf16[512,1024]{1,0:T(8,128)(2,1)S(1)}, bf16[512,1024]{1,0:T(8,128)(2,1)}, u32[]{:S(2)}) %copy-start.2) | copy-done | bytes 1048600
  12.7 1.2 %copy-done.3 = bf16[512,1024]{1,0:T(8,128)(2,1)S(1)} copy-done((bf16[512,1024]{1,0:T(8,128)(2,1)S(1)}, bf16[512,1024]{1,0:T(8,128)(2,1)}, u32[]{:S(2)}) %copy-start.3) | copy-done | bytes 1048600
  13.9 1.0 %pick_q.1.own_ref = bf16[2,4,256,128]{3,2,1,0:T(8,128)(2,1)S(1)} custom-call(s32[1,128]{1,0:T(1,128)S(1)} %bitcast.11, bf16[1,512]{1,0:T(2,128)(2,1)S(1)} %reshape.49.gate_ref, bf16[512,1024]{1,0:T(8,128)(2,1)S(1)} %copy-done.2, bf16[512,1024]{1,0:T(8,128)(2,1)S(1)} %copy-done.3), custom_call_target="tpu_custom_call" | custom-call | flops 1073741824 | bytes 1048576 | tf_op jit(solution)/shard_map/pick_q/pallas_call | solution.py:452
  14.8 0.1 collective-permute-start.1
  14.9 0.5 collective-permute-start
  15.4 1.4 %collective-permute-done.peer_picked = s32[1,128]{1,0:T(1,128)S(1)} collective-permute-done((s32[1,128]{1,0:T(1,128)S(1)}, s32[1,128]{1,0:T(1,128)S(1)}, u32[]{:S(2)}, u32[]{:S(2)}) %collective-permute-start) | collective-permute-done | bytes 544 | tf_op jit(solution)/shard_map/ppermute | solution.py:468
  16.8 0.0 collective-permute-done.1.oth_ref
  16.8 10.9 %all-to-all-done.kv_ref = bf16[16,128,256]{2,1,0:T(8,128)(2,1)S(1)} async-done(((bf16[16,128,256]{2,1,0:T(8,128)(2,1)}), bf16[16,128,256]{2,1,0:T(8,128)(2,1)S(1)}, u32[]{:S(2)}, u32[]{:S(2)}) %all-to-all-start) | async-done | bytes 1048608 | tf_op jit(solution)/shard_map/all_to_all | solution.py:450
  27.7 2.4 %stats.1 = (bf16[2048,128]{1,0:T(8,128)(2,1)S(1)}, bf16[2048,128]{1,0:T(8,128)(2,1)S(1)}, bf16[2304,128]{1,0:T(8,128)(2,1)S(1)}, bf16[2304,128]{1,0:T(8,128)(2,1...) custom-call(s32[1,128]{1,0:T(1,128)S(1)} %collective-permute-done.pe, ...), custom_call_target="tpu_custom_call" | custom-call | tf_op jit(solution)/shard_map/stats/pallas_call | solution.py:469
  30.2 0.1 collective-permute-start.2
  30.3 1.3 %collective-permute-done.2.peer_ref = f32[9,8,256]{2,1,0:T(8,128)S(1)} collective-permute-done((f32[9,8,256]{2,1,0:T(8,128)S(1)}, f32[9,8,256]{2,1,0:T(8,128)S(1)}, u32[]{:S(2)}, u32[]{:S(2)}) %collective-permute-start.2) | collective-permute-done | bytes 73760 | tf_op jit(solution)/shard_map/ppermute | solution.py:488
  31.5 0.8 %combine.1 = (f32[9,8,256]{2,1,0:T(8,128)S(1)}, f32[8,128]{1,0:T(8,128)S(1)}) custom-call(s32[32]{0:T(128)S(1)} %get-tuple-element.35.info_ref, f32[9,8,256]{2,1,0:T(8,128)S(1)} %get-tuple-element.40.stats_ref, f32[9,8,256]{2,1,0:T(8,128)S(1)} %collective-permute-done.2.peer_ref), custom_call_target="tpu_custom_call" | custom-call | tf_op jit(solution)/shard_map/combine/pallas_call | solution.py:489
  32.3 2.0 %collective-permute-start.4 = (f32[8,128]{1,0:T(8,128)S(1)}, f32[8,128]{1,0:T(8,128)S(1)}, u32[]{:S(2)}, u32[]{:S(2)}) collective-permute-start(f32[8,128]{1,0:T(8,128)S(1)} %get-tuple-element.49), channel_id=1, source_target_pairs={{0,1},{1,0},{2,3},{3,2},{4,5},{5,4},{6,7},{7,6},{8,9},{9,8},{10,11... | collective-permute-start | bytes 12296 | tf_op jit(solution)/shard_map/ppermute | solution.py:497
  34.3 2.5 %grads.1 = (bf16[4,128,256]{2,1,0:T(8,128)(2,1)S(1)}, bf16[4,128,256]{2,1,0:T(8,128)(2,1)S(1)}, bf16[4,128,256]{2,1,0:T(8,128)(2,1)S(1)}, bf16[4,128,256]{2,1,0:...) custom-call(s32[32]{0:T(128)S(1)} %get-tuple-element.35.info_ref, ...), custom_call_target="tpu_custom_call" | custom-call | flops 4294967296 | bytes 1048576 | tf_op jit(solution)/shard_map/grads/pallas_call | solution.py:498
  36.8 0.2 collective-permute-start.5
  37.0 6.4 %collective-permute-start.6 = (bf16[4,128,256]{2,1,0:T(8,128)(2,1)S(1)}, bf16[4,128,256]{2,1,0:T(8,128)(2,1)S(1)}, u32[]{:S(2)}, u32[]{:S(2)}) collective-permute-start(bf16[4,128,256]{2,1,0:T(8,128)(2,1)S(1)} %get-tuple-element.56), channel_id=1, source_target_pairs={{0,128},{8,40},{16,144},{24,56},{32,160},{40,8},{48,176},{56,24},{... | collective-permute-start | bytes 786440 | tf_op jit(solution)/shard_map/ppermute | solution.py:428
  43.5 4.6 %collective-permute-start.8 = (f32[8,128]{1,0:T(8,128)S(1)}, f32[8,128]{1,0:T(8,128)S(1)}, u32[]{:S(2)}, u32[]{:S(2)}) collective-permute-start(f32[8,128]{1,0:T(8,128)S(1)} %add.65), channel_id=1, source_target_pairs={{0,4},{1,5},{2,6},{3,7},{4,0},{5,1},{6,2},{7,3},{8,12},{9,13},{10,... | collective-permute-start | bytes 12296 | tf_op jit(solution)/shard_map/ppermute | solution.py:520
  48.0 0.0 collective-permute-done.5
  48.0 2.6 %collective-permute-done.6 = bf16[4,128,256]{2,1,0:T(8,128)(2,1)S(1)} collective-permute-done((bf16[4,128,256]{2,1,0:T(8,128)(2,1)S(1)}, bf16[4,128,256]{2,1,0:T(8,128)(2,1)S(1)}, u32[]{:S(2)}, u32[]{:S(2)}) %collective-permute-start.6) | collective-permute-done | bytes 262176 | tf_op jit(solution)/shard_map/ppermute | solution.py:428
  50.6 0.1 fusion.2
  50.7 0.3 collective-permute-done.8
  51.1 0.6 collective-permute-start.9
  51.6 2.0 %collective-permute-start.10 = (bf16[128,256]{1,0:T(8,128)(2,1)S(1)}, bf16[128,256]{1,0:T(8,128)(2,1)S(1)}, u32[]{:S(2)}, u32[]{:S(2)}) collective-permute-start(bf16[128,256]{1,0:T(8,128)(2,1)S(1)} %get-tuple-element.60), channel_id=1, source_target_pairs={{0,32},{8,136},{16,48},{24,152},{32,0},{40,168},{48,16},{56,184},{... | collective-permute-start | bytes 196616 | tf_op jit(solution)/shard_map/ppermute | solution.py:428
  53.7 1.5 %collective-permute-start.11 = (bf16[128,256]{1,0:T(8,128)(2,1)S(1)}, bf16[128,256]{1,0:T(8,128)(2,1)S(1)}, u32[]{:S(2)}, u32[]{:S(2)}) collective-permute-start(bf16[128,256]{1,0:T(8,128)(2,1)S(1)} %get-tuple-element.61), channel_id=1, source_target_pairs={{0,48},{8,200},{16,0},{24,216},{32,16},{40,232},{48,32},{56,248},{... | collective-permute-start | bytes 196616 | tf_op jit(solution)/shard_map/ppermute | solution.py:428
  55.1 0.0 collective-permute-start.12
  55.2 1.4 %place_q.1 = (bf16[512,1024]{1,0:T(8,128)(2,1)}, f32[8,128]{1,0:T(8,128)S(1)}) custom-call(s32[1,128]{1,0:T(1,128)S(1)} %bitcast.13, bf16[1,512]{1,0:T(2,128)(2,1)S(1)} %reshape.49.gate_ref, f32[4,256,128]{2,1,0:T(8,128)S(1)} %get-tuple-element.45.dq_own, bf16[4,256,128]{2,1,0:T(8,128)(2,1)S(1)} %collective-permute-done.3.dq_peer), custom_call_target="tpu_custom_call" | custom-call | flops 536870912 | bytes 1048576 | tf_op jit(solution)/shard_map/place_q/pallas_call | solution.py:522
  56.6 3.1 %collective-permute-done.12.part_b = f32[8,128]{1,0:T(8,128)S(1)} collective-permute-done((f32[8,128]{1,0:T(8,128)S(1)}, f32[8,128]{1,0:T(8,128)S(1)}, u32[]{:S(2)}, u32[]{:S(2)}) %collective-permute-start.12) | collective-permute-done | bytes 4128 | tf_op jit(solution)/shard_map/ppermute | solution.py:535
  59.7 0.9 %place_kv.1 = (bf16[512,128]{1,0:T(8,128)(2,1)}, bf16[512,128]{1,0:T(8,128)(2,1)}, bf16[4,128]{1,0:T(4,128)(2,1)}) custom-call(s32[1,128]{1,0:T(1,128)S(1)} %bitcast.14, f32[8,128]{1,0:T(8,128)S(1)} %get-tuple-element.48.closed_ref, f32[128,256]{1,0:T(8,128)S(1)} %get-tuple-element.69.own_ref, bf16[128,256]{1,0:T(8,128)(2,1)S(1)} %collective-permute-done.9.sum_1, ...), custom_call_target="tpu_custom_call" | custom-call | tf_op jit(solution)/shard_map/place_kv/pallas_call | solution.py:536
  (15 shorter events, 0.0 us)
Async XLA Ops:
  3.0 24.7 %all-to-all-start = ((bf16[16,128,256]{2,1,0:T(8,128)(2,1)}), bf16[16,128,256]{2,1,0:T(8,128)(2,1)S(1)}, u32[]{:S(2)}, u32[]{:S(2)}) async-start(bf16[16,128,256]{2,1,0:T(8,128)(2,1)} %pick_kv.1), calls=%async_computation | async-start | bytes 2097152 | tf_op jit(solution)/shard_map/all_to_all | solution.py:450
  10.8 0.7 %copy-start = (s32[128]{0:T(128)S(1)}, s32[128]{0:T(128)}, u32[]{:S(2)}) copy-start(s32[128]{0:T(128)} %param.11) | copy-start | bytes 1540
  11.4 1.2 %copy-start.2 = (bf16[512,1024]{1,0:T(8,128)(2,1)S(1)}, bf16[512,1024]{1,0:T(8,128)(2,1)}, u32[]{:S(2)}) copy-start(bf16[512,1024]{1,0:T(8,128)(2,1)} %q_hbm.1) | copy-start | bytes 3145732
  12.7 1.2 %copy-start.3 = (bf16[512,1024]{1,0:T(8,128)(2,1)S(1)}, bf16[512,1024]{1,0:T(8,128)(2,1)}, u32[]{:S(2)}) copy-start(bf16[512,1024]{1,0:T(8,128)(2,1)} %up_hbm.1) | copy-start | bytes 3145732
  14.8 2.0 %collective-permute-start.1 = (bf16[2,4,256,128]{3,2,1,0:T(8,128)(2,1)S(1)}, bf16[2,4,256,128]{3,2,1,0:T(8,128)(2,1)S(1)}, u32[]{:S(2)}, u32[]{:S(2)}) collective-permute-start(bf16[2,4,256,128]{3,2,1,0:T(8,128)(2,1)S(1)} %pick_q.1.own_ref), channel_id=1, source_target_pairs={{0,8},{8,0},{1,9},{9,1},{2,10},{10,2},{3,11},{11,3},{4,12},{12,4},... | collective-permute-start | bytes 1572872 | tf_op jit(solution)/shard_map/ppermute | solution.py:467
  14.9 1.9 %collective-permute-start = (s32[1,128]{1,0:T(1,128)S(1)}, s32[1,128]{1,0:T(1,128)S(1)}, u32[]{:S(2)}, u32[]{:S(2)}) collective-permute-start(s32[1,128]{1,0:T(1,128)S(1)} %bitcast.12), channel_id=1, source_target_pairs={{0,8},{8,0},{1,9},{9,1},{2,10},{10,2},{3,11},{11,3},{4,12},{12,4},... | collective-permute-start | bytes 1544 | tf_op jit(solution)/shard_map/ppermute | solution.py:468
  30.2 1.4 %collective-permute-start.2 = (f32[9,8,256]{2,1,0:T(8,128)S(1)}, f32[9,8,256]{2,1,0:T(8,128)S(1)}, u32[]{:S(2)}, u32[]{:S(2)}) collective-permute-start(f32[9,8,256]{2,1,0:T(8,128)S(1)} %get-tuple-element.40.stats_ref), channel_id=1, source_target_pairs={{0,8},{8,0},{1,9},{9,1},{2,10},{10,2},{3,11},{11,3},{4,12},{12,4},... | collective-permute-start | bytes 221192 | tf_op jit(solution)/shard_map/ppermute | solution.py:488
  32.3 4.5 %collective-permute-start.4 = (f32[8,128]{1,0:T(8,128)S(1)}, f32[8,128]{1,0:T(8,128)S(1)}, u32[]{:S(2)}, u32[]{:S(2)}) collective-permute-start(f32[8,128]{1,0:T(8,128)S(1)} %get-tuple-element.49), channel_id=1, source_target_pairs={{0,1},{1,0},{2,3},{3,2},{4,5},{5,4},{6,7},{7,6},{8,9},{9,8},{10,11... | collective-permute-start | bytes 12296 | tf_op jit(solution)/shard_map/ppermute | solution.py:497
  34.3 20.9 %copy-start.1 = (s32[128]{0:T(128)S(1)}, s32[128]{0:T(128)}, u32[]{:S(2)}) copy-start(s32[128]{0:T(128)} %param.11) | copy-start | bytes 1540
  36.8 11.2 %collective-permute-start.5 = (bf16[4,128,256]{2,1,0:T(8,128)(2,1)S(1)}, bf16[4,128,256]{2,1,0:T(8,128)(2,1)S(1)}, u32[]{:S(2)}, u32[]{:S(2)}) collective-permute-start(bf16[4,128,256]{2,1,0:T(8,128)(2,1)S(1)} %get-tuple-element.55), channel_id=1, source_target_pairs={{0,64},{8,24},{16,80},{24,40},{32,96},{40,56},{48,112},{56,8},{64,... | collective-permute-start | bytes 786440 | tf_op jit(solution)/shard_map/ppermute | solution.py:428
  37.0 13.6 %collective-permute-start.6 = (bf16[4,128,256]{2,1,0:T(8,128)(2,1)S(1)}, bf16[4,128,256]{2,1,0:T(8,128)(2,1)S(1)}, u32[]{:S(2)}, u32[]{:S(2)}) collective-permute-start(bf16[4,128,256]{2,1,0:T(8,128)(2,1)S(1)} %get-tuple-element.56), channel_id=1, source_target_pairs={{0,128},{8,40},{16,144},{24,56},{32,160},{40,8},{48,176},{56,24},{... | collective-permute-start | bytes 786440 | tf_op jit(solution)/shard_map/ppermute | solution.py:428
  43.4 7.2 %collective-permute-start.7 = (bf16[4,128,256]{2,1,0:T(8,128)(2,1)S(1)}, bf16[4,128,256]{2,1,0:T(8,128)(2,1)S(1)}, u32[]{:S(2)}, u32[]{:S(2)}) collective-permute-start(bf16[4,128,256]{2,1,0:T(8,128)(2,1)S(1)} %get-tuple-element.57), channel_id=1, source_target_pairs={{0,192},{8,56},{16,208},{24,8},{32,224},{40,24},{48,240},{56,40},{... | collective-permute-start | bytes 786440 | tf_op jit(solution)/shard_map/ppermute | solution.py:428
  43.4 11.7 %collective-permute-start.3 = (bf16[4,256,128]{2,1,0:T(8,128)(2,1)S(1)}, bf16[4,256,128]{2,1,0:T(8,128)(2,1)S(1)}, u32[]{:S(2)}, u32[]{:S(2)}) collective-permute-start(bf16[4,256,128]{2,1,0:T(8,128)(2,1)S(1)} %get-tuple-element.46), channel_id=1, source_target_pairs={{0,8},{8,0},{1,9},{9,1},{2,10},{10,2},{3,11},{11,3},{4,12},{12,4},... | collective-permute-start | bytes 786440 | tf_op jit(solution)/shard_map/ppermute | solution.py:521
  43.5 7.6 %collective-permute-start.8 = (f32[8,128]{1,0:T(8,128)S(1)}, f32[8,128]{1,0:T(8,128)S(1)}, u32[]{:S(2)}, u32[]{:S(2)}) collective-permute-start(f32[8,128]{1,0:T(8,128)S(1)} %add.65), channel_id=1, source_target_pairs={{0,4},{1,5},{2,6},{3,7},{4,0},{5,1},{6,2},{7,3},{8,12},{9,13},{10,... | collective-permute-start | bytes 12296 | tf_op jit(solution)/shard_map/ppermute | solution.py:520
  51.1 8.6 %collective-permute-start.9 = (bf16[128,256]{1,0:T(8,128)(2,1)S(1)}, bf16[128,256]{1,0:T(8,128)(2,1)S(1)}, u32[]{:S(2)}, u32[]{:S(2)}) collective-permute-start(bf16[128,256]{1,0:T(8,128)(2,1)S(1)} %get-tuple-element.59), channel_id=1, source_target_pairs={{0,16},{8,72},{16,32},{24,88},{32,48},{40,104},{48,0},{56,120},{64... | collective-permute-start | bytes 196616 | tf_op jit(solution)/shard_map/ppermute | solution.py:428
  51.6 8.0 %collective-permute-start.10 = (bf16[128,256]{1,0:T(8,128)(2,1)S(1)}, bf16[128,256]{1,0:T(8,128)(2,1)S(1)}, u32[]{:S(2)}, u32[]{:S(2)}) collective-permute-start(bf16[128,256]{1,0:T(8,128)(2,1)S(1)} %get-tuple-element.60), channel_id=1, source_target_pairs={{0,32},{8,136},{16,48},{24,152},{32,0},{40,168},{48,16},{56,184},{... | collective-permute-start | bytes 196616 | tf_op jit(solution)/shard_map/ppermute | solution.py:428
  53.7 6.0 %collective-permute-start.11 = (bf16[128,256]{1,0:T(8,128)(2,1)S(1)}, bf16[128,256]{1,0:T(8,128)(2,1)S(1)}, u32[]{:S(2)}, u32[]{:S(2)}) collective-permute-start(bf16[128,256]{1,0:T(8,128)(2,1)S(1)} %get-tuple-element.61), channel_id=1, source_target_pairs={{0,48},{8,200},{16,0},{24,216},{32,16},{40,232},{48,32},{56,248},{... | collective-permute-start | bytes 196616 | tf_op jit(solution)/shard_map/ppermute | solution.py:428
  55.1 4.5 %collective-permute-start.12 = (f32[8,128]{1,0:T(8,128)S(1)}, f32[8,128]{1,0:T(8,128)S(1)}, u32[]{:S(2)}, u32[]{:S(2)}) collective-permute-start(f32[8,128]{1,0:T(8,128)S(1)} %add.78.part_a), channel_id=1, source_target_pairs={{0,2},{1,3},{2,0},{3,1},{4,6},{5,7},{6,4},{7,5},{8,10},{9,11},{10,... | collective-permute-start | bytes 12296 | tf_op jit(solution)/shard_map/ppermute | solution.py:535

commit v6 on v5

--- a/solution.py
+++ b/solution.py
@@ -267,26 +267,27 @@
 
 def combine_kernel(info_ref, stats_ref, peer_ref, comb_out, delta_out):
     own_chunks = info_ref[18]
-    lane = lax.div(lax.broadcasted_iota(jnp.int32, (1, SLOTS), 1), CHUNK)
-    comb_out[SPARE] = jnp.zeros((8, ROWS), F32)
-    deltas = jnp.zeros((1, SLOTS), F32)
-    for place in range(SPARE):
-        mine = stats_ref[place]
-        theirs = peer_ref[(place + CHUNKS) % SPARE]
-        top = jnp.maximum(mine[0:1], theirs[0:1])
-        mine_scale = jnp.exp2(mine[0:1] - top)
-        their_scale = jnp.exp2(theirs[0:1] - top)
-        total = mine[1:2] * mine_scale + theirs[1:2] * their_scale
-        total = jnp.where(total > 0.0, total, 1.0)
-        delta = (mine[2:3] * mine_scale + theirs[2:3] * their_scale) / total
-        comb_out[place, 0:1, :] = top + jnp.log2(total)
-        comb_out[place, 1:2, :] = delta
-        if place < CHUNKS:
-            heads = delta[:, 0:128] + delta[:, 128:256]
-            heads = heads + pltpu.roll(heads, 64, 1)
-            heads = heads + pltpu.roll(heads, 32, 1)
-            mark = jnp.where(place < own_chunks, place, CHUNKS)
-            deltas = deltas + jnp.where(lane == mark, heads, 0.0)
+
+    def of(ref, kind, swap):
+        first, second = ref[0:CHUNKS, kind, :], ref[CHUNKS:SPARE, kind, :]
+        return jnp.concatenate([second, first] if swap else [first, second], axis=0)
+
+    top_a, top_b = of(stats_ref, 0, False), of(peer_ref, 0, True)
+    top = jnp.maximum(top_a, top_b)
+    scale_a, scale_b = jnp.exp2(top_a - top), jnp.exp2(top_b - top)
+    total = of(stats_ref, 1, False) * scale_a + of(peer_ref, 1, True) * scale_b
+    total = jnp.where(total > 0.0, total, 1.0)
+    delta = (of(stats_ref, 2, False) * scale_a + of(peer_ref, 2, True) * scale_b) / total
+    comb_out[...] = jnp.zeros_like(comb_out)
+    comb_out[0:SPARE, 0, :] = top + jnp.log2(total)
+    comb_out[0:SPARE, 1, :] = delta
+    heads = delta[:, 0:128] + delta[:, 128:256]
+    heads = heads + pltpu.roll(heads, 64, 1)
+    heads = heads + pltpu.roll(heads, 32, 1)
+    lane = lax.div(lax.broadcasted_iota(jnp.int32, (SPARE, SLOTS), 1), CHUNK)
+    chunk = lax.broadcasted_iota(jnp.int32, (SPARE, SLOTS), 0)
+    heads = jnp.where((lane == chunk) & (chunk < own_chunks), heads, 0.0)
+    deltas = jnp.sum(heads, axis=0, keepdims=True)
     delta_out[...] = jnp.broadcast_to(deltas, (8, SLOTS))
 
 
@@ -515,7 +516,8 @@
     )(info, kc, vc, q_rows, s_rows, comb, raised, pushed, tops)
     delta_near, *lines = lax.optimization_barrier((delta_near, *lines))
     deltas = deltas + delta_near
-    lines = lines[:1] + [across(lines[k], k, False) for k in (1, 2, 3)]
+    moved = {k: across(lines[k], k, False) for k in (2, 3, 1)}
+    lines = lines[:1] + [moved[k] for k in (1, 2, 3)]
     sums = [sum(line[j].astype(F32) for line in lines) for j in range(4)]
     delta_far = lax.ppermute(deltas, "tp", [(i, i ^ 4) for i in range(8)])
     dq_peer = lax.ppermute(dq_oth, "c", swap)

time: 61.6 us -> 61.5 us (level)
  Pallas kernels: 11.4 us -> 10.4 us
  starting transfers between devices: 25 us -> 26 us
    ppermute x6, starting transfers between devices: 10.7 us -> 11.8 us  [across(): return lax.ppermute(block, ('y', 'x', 'c'), pairs)]
  transfers between devices with their start and end apart: 14 -> 14, of which waited for: 6 -> 6; matrix products, arithmetic and copies ran while one was open for 1% -> 1% of each run, Pallas kernels for 8% -> 7%
where the time goes in v6:
time: 61.5 us; the launch traced here: 60.5 us
  starting transfers between devices  26 us (42%)
  waiting for transfers between devices  19.5 us (32%)
  Pallas kernels  10.4 us (17%)
  local copies, waits for them, and re-layouts  3.79 us (6%)
  between operations  0.72 us (1%)
    ppermute x6, starting transfers between devices, across(): return lax.ppermute(block, ('y', 'x', 'c'), pairs)  11.8 us
    all_to_all x1, waiting for transfers between devices, local(): kv_all = lax.all_to_all(kv_copies, ('y', 'x'), 0, 0, tiled=True)  10.9 us
    all_to_all x1, starting transfers between devices, local(): kv_all = lax.all_to_all(kv_copies, ('y', 'x'), 0, 0, tiled=True)  7.05 us
    ppermute x1, starting transfers between devices, local(): delta_far = lax.ppermute(deltas, 'tp', [(i, i ^ 4) for i in range(8)])  4.58 us
    unnamed x8, local copies, waits for them, and re-layouts  3.11 us
    ppermute x1, waiting for transfers between devices, local(): logit_rest = lax.ppermute(logit_half, 'tp', [(i, i ^ 2) for i in range(8)])  3.06 us
    ppermute x6, waiting for transfers between devices, across(): return lax.ppermute(block, ('y', 'x', 'c'), pairs)  2.57 us
    pallas_call x1, Pallas kernels, local(): pl.pallas_call(pick_kv_kernel, out_shape=shape((CHIPS, SLOTS, 2 * HEAD)),...  2.39 us
  transfers between devices with their start and end apart: 14, of which 6 were waited for; matrix products, arithmetic and copies ran while one was open for 1% of the time, Pallas kernels for 7%

profile of v6, /device:TPU:64, one launch (start us, length us, event | category | flops | bytes accessed | tf_op | source)
XLA Modules:
  0.0 60.5 jit_solution(16507241071067120239)
XLA Ops:
  0.6 2.4 %pick_kv.1 = bf16[16,128,256]{2,1,0:T(8,128)(2,1)} custom-call(s32[1,128]{1,0:T(1,128)} %bitcast.10, bf16[512,128]{1,0:T(8,128)(2,1)} %k_hbm.1, bf16[512,128]{1,0:T(8,128)(2,1)} %v_hbm.1), custom_call_target="tpu_custom_call" | custom-call | tf_op jit(solution)/shard_map/pick_kv/pallas_call | solution.py:435
  3.0 7.1 %all-to-all-start = ((bf16[16,128,256]{2,1,0:T(8,128)(2,1)}), bf16[16,128,256]{2,1,0:T(8,128)(2,1)S(1)}, u32[]{:S(2)}, u32[]{:S(2)}) async-start(bf16[16,128,256]{2,1,0:T(8,128)(2,1)} %pick_kv.1), calls=%async_computation | async-start | bytes 2097152 | tf_op jit(solution)/shard_map/all_to_all | solution.py:451
  10.1 0.7 %reshape.49.gate_ref = bf16[1,512]{1,0:T(2,128)(2,1)S(1)} reshape(bf16[512]{0:T(512)(128)(2,1)} %param.9) | data formatting | bytes 2048 | tf_op jit(solution)/shard_map/reshape | solution.py:452
  10.8 0.7 %copy-done = s32[128]{0:T(128)S(1)} copy-done((s32[128]{0:T(128)S(1)}, s32[128]{0:T(128)}, u32[]{:S(2)}) %copy-start) | copy-done | bytes 536
  11.4 1.2 %copy-done.2 = bf16[512,1024]{1,0:T(8,128)(2,1)S(1)} copy-done((bf16[512,1024]{1,0:T(8,128)(2,1)S(1)}, bf16[512,1024]{1,0:T(8,128)(2,1)}, u32[]{:S(2)}) %copy-start.2) | copy-done | bytes 1048600
  12.7 1.2 %copy-done.3 = bf16[512,1024]{1,0:T(8,128)(2,1)S(1)} copy-done((bf16[512,1024]{1,0:T(8,128)(2,1)S(1)}, bf16[512,1024]{1,0:T(8,128)(2,1)}, u32[]{:S(2)}) %copy-start.3) | copy-done | bytes 1048600
  13.9 1.0 %pick_q.1.own_ref = bf16[2,4,256,128]{3,2,1,0:T(8,128)(2,1)S(1)} custom-call(s32[1,128]{1,0:T(1,128)S(1)} %bitcast.11, bf16[1,512]{1,0:T(2,128)(2,1)S(1)} %reshape.49.gate_ref, bf16[512,1024]{1,0:T(8,128)(2,1)S(1)} %copy-done.2, bf16[512,1024]{1,0:T(8,128)(2,1)S(1)} %copy-done.3), custom_call_target="tpu_custom_call" | custom-call | flops 1073741824 | bytes 1048576 | tf_op jit(solution)/shard_map/pick_q/pallas_call | solution.py:453
  14.8 0.1 collective-permute-start.1
  14.9 0.5 collective-permute-start
  15.4 1.4 %collective-permute-done.peer_picked = s32[1,128]{1,0:T(1,128)S(1)} collective-permute-done((s32[1,128]{1,0:T(1,128)S(1)}, s32[1,128]{1,0:T(1,128)S(1)}, u32[]{:S(2)}, u32[]{:S(2)}) %collective-permute-start) | collective-permute-done | bytes 544 | tf_op jit(solution)/shard_map/ppermute | solution.py:469
  16.8 10.9 %all-to-all-done.kv_ref = bf16[16,128,256]{2,1,0:T(8,128)(2,1)S(1)} async-done(((bf16[16,128,256]{2,1,0:T(8,128)(2,1)}), bf16[16,128,256]{2,1,0:T(8,128)(2,1)S(1)}, u32[]{:S(2)}, u32[]{:S(2)}) %all-to-all-start) | async-done | bytes 1048608 | tf_op jit(solution)/shard_map/all_to_all | solution.py:451
  27.7 2.0 %stats.1 = (bf16[2048,128]{1,0:T(8,128)(2,1)S(1)}, bf16[2048,128]{1,0:T(8,128)(2,1)S(1)}, bf16[2304,128]{1,0:T(8,128)(2,1)S(1)}, bf16[2304,128]{1,0:T(8,128)(2,1...) custom-call(s32[1,128]{1,0:T(1,128)S(1)} %collective-permute-done.pe, ...), custom_call_target="tpu_custom_call" | custom-call | tf_op jit(solution)/shard_map/stats/pallas_call | solution.py:470
  29.7 0.1 collective-permute-start.2
  29.8 1.3 %collective-permute-done.2.peer_ref = f32[9,8,256]{2,1,0:T(8,128)S(1)} collective-permute-done((f32[9,8,256]{2,1,0:T(8,128)S(1)}, f32[9,8,256]{2,1,0:T(8,128)S(1)}, u32[]{:S(2)}, u32[]{:S(2)}) %collective-permute-start.2) | collective-permute-done | bytes 73760 | tf_op jit(solution)/shard_map/ppermute | solution.py:489
  31.1 0.7 %combine.1 = (f32[9,8,256]{2,1,0:T(8,128)S(1)}, f32[8,128]{1,0:T(8,128)S(1)}) custom-call(s32[32]{0:T(128)S(1)} %get-tuple-element.35.info_ref, f32[9,8,256]{2,1,0:T(8,128)S(1)} %get-tuple-element.40.stats_ref, f32[9,8,256]{2,1,0:T(8,128)S(1)} %collective-permute-done.2.peer_ref), custom_call_target="tpu_custom_call" | custom-call | tf_op jit(solution)/shard_map/combine/pallas_call | solution.py:490
  31.8 1.9 %collective-permute-start.4 = (f32[8,128]{1,0:T(8,128)S(1)}, f32[8,128]{1,0:T(8,128)S(1)}, u32[]{:S(2)}, u32[]{:S(2)}) collective-permute-start(f32[8,128]{1,0:T(8,128)S(1)} %get-tuple-element.49), channel_id=1, source_target_pairs={{0,1},{1,0},{2,3},{3,2},{4,5},{5,4},{6,7},{7,6},{8,9},{9,8},{10,11... | collective-permute-start | bytes 12296 | tf_op jit(solution)/shard_map/ppermute | solution.py:498
  33.7 2.0 %grads.1 = (bf16[4,128,256]{2,1,0:T(8,128)(2,1)S(1)}, bf16[4,128,256]{2,1,0:T(8,128)(2,1)S(1)}, bf16[4,128,256]{2,1,0:T(8,128)(2,1)S(1)}, bf16[4,128,256]{2,1,0:...) custom-call(s32[32]{0:T(128)S(1)} %get-tuple-element.35.info_ref, ...), custom_call_target="tpu_custom_call" | custom-call | flops 4294967296 | bytes 1048576 | tf_op jit(solution)/shard_map/grads/pallas_call | solution.py:499
  35.7 0.0 collective-permute-done.4
  35.7 1.2 %collective-permute-start.5 = (bf16[4,128,256]{2,1,0:T(8,128)(2,1)S(1)}, bf16[4,128,256]{2,1,0:T(8,128)(2,1)S(1)}, u32[]{:S(2)}, u32[]{:S(2)}) collective-permute-start(bf16[4,128,256]{2,1,0:T(8,128)(2,1)S(1)} %get-tuple-element.55), channel_id=1, source_target_pairs={{0,64},{8,24},{16,80},{24,40},{32,96},{40,56},{48,112},{56,8},{64,... | collective-permute-start | bytes 786440 | tf_op jit(solution)/shard_map/ppermute | solution.py:429
  36.9 5.2 %collective-permute-start.6 = (bf16[4,128,256]{2,1,0:T(8,128)(2,1)S(1)}, bf16[4,128,256]{2,1,0:T(8,128)(2,1)S(1)}, u32[]{:S(2)}, u32[]{:S(2)}) collective-permute-start(bf16[4,128,256]{2,1,0:T(8,128)(2,1)S(1)} %get-tuple-element.56), channel_id=1, source_target_pairs={{0,128},{8,40},{16,144},{24,56},{32,160},{40,8},{48,176},{56,24},{... | collective-permute-start | bytes 786440 | tf_op jit(solution)/shard_map/ppermute | solution.py:429
  42.1 0.0 collective-permute-start.7
  42.1 4.6 %collective-permute-start.8 = (f32[8,128]{1,0:T(8,128)S(1)}, f32[8,128]{1,0:T(8,128)S(1)}, u32[]{:S(2)}, u32[]{:S(2)}) collective-permute-start(f32[8,128]{1,0:T(8,128)S(1)} %add.65), channel_id=1, source_target_pairs={{0,4},{1,5},{2,6},{3,7},{4,0},{5,1},{6,2},{7,3},{8,12},{9,13},{10,... | collective-permute-start | bytes 12296 | tf_op jit(solution)/shard_map/ppermute | solution.py:522
  46.7 2.6 %collective-permute-done.6 = bf16[4,128,256]{2,1,0:T(8,128)(2,1)S(1)} collective-permute-done((bf16[4,128,256]{2,1,0:T(8,128)(2,1)S(1)}, bf16[4,128,256]{2,1,0:T(8,128)(2,1)S(1)}, u32[]{:S(2)}, u32[]{:S(2)}) %collective-permute-start.6) | collective-permute-done | bytes 262176 | tf_op jit(solution)/shard_map/ppermute | solution.py:429
  49.2 0.1 fusion.2
  49.4 0.3 collective-permute-done.8
  49.7 1.6 %collective-permute-start.9 = (bf16[128,256]{1,0:T(8,128)(2,1)S(1)}, bf16[128,256]{1,0:T(8,128)(2,1)S(1)}, u32[]{:S(2)}, u32[]{:S(2)}) collective-permute-start(bf16[128,256]{1,0:T(8,128)(2,1)S(1)} %get-tuple-element.59), channel_id=1, source_target_pairs={{0,16},{8,72},{16,32},{24,88},{32,48},{40,104},{48,0},{56,120},{64... | collective-permute-start | bytes 196616 | tf_op jit(solution)/shard_map/ppermute | solution.py:429
  51.3 2.2 %collective-permute-start.10 = (bf16[128,256]{1,0:T(8,128)(2,1)S(1)}, bf16[128,256]{1,0:T(8,128)(2,1)S(1)}, u32[]{:S(2)}, u32[]{:S(2)}) collective-permute-start(bf16[128,256]{1,0:T(8,128)(2,1)S(1)} %get-tuple-element.60), channel_id=1, source_target_pairs={{0,32},{8,136},{16,48},{24,152},{32,0},{40,168},{48,16},{56,184},{... | collective-permute-start | bytes 196616 | tf_op jit(solution)/shard_map/ppermute | solution.py:429
  53.5 1.6 %collective-permute-start.11 = (bf16[128,256]{1,0:T(8,128)(2,1)S(1)}, bf16[128,256]{1,0:T(8,128)(2,1)S(1)}, u32[]{:S(2)}, u32[]{:S(2)}) collective-permute-start(bf16[128,256]{1,0:T(8,128)(2,1)S(1)} %get-tuple-element.61), channel_id=1, source_target_pairs={{0,48},{8,200},{16,0},{24,216},{32,16},{40,232},{48,32},{56,248},{... | collective-permute-start | bytes 196616 | tf_op jit(solution)/shard_map/ppermute | solution.py:429
  55.1 0.0 collective-permute-start.12
  55.1 1.4 %place_q.1 = (bf16[512,1024]{1,0:T(8,128)(2,1)}, f32[8,128]{1,0:T(8,128)S(1)}) custom-call(s32[1,128]{1,0:T(1,128)S(1)} %bitcast.13, bf16[1,512]{1,0:T(2,128)(2,1)S(1)} %reshape.49.gate_ref, f32[4,256,128]{2,1,0:T(8,128)S(1)} %get-tuple-element.45.dq_own, bf16[4,256,128]{2,1,0:T(8,128)(2,1)S(1)} %collective-permute-done.3.dq_peer), custom_call_target="tpu_custom_call" | custom-call | flops 536870912 | bytes 1048576 | tf_op jit(solution)/shard_map/place_q/pallas_call | solution.py:524
  56.5 3.1 %collective-permute-done.12.part_b = f32[8,128]{1,0:T(8,128)S(1)} collective-permute-done((f32[8,128]{1,0:T(8,128)S(1)}, f32[8,128]{1,0:T(8,128)S(1)}, u32[]{:S(2)}, u32[]{:S(2)}) %collective-permute-start.12) | collective-permute-done | bytes 4128 | tf_op jit(solution)/shard_map/ppermute | solution.py:537
  59.6 0.9 %place_kv.1 = (bf16[512,128]{1,0:T(8,128)(2,1)}, bf16[512,128]{1,0:T(8,128)(2,1)}, bf16[4,128]{1,0:T(4,128)(2,1)}) custom-call(s32[1,128]{1,0:T(1,128)S(1)} %bitcast.14, f32[8,128]{1,0:T(8,128)S(1)} %get-tuple-element.48.closed_ref, f32[128,256]{1,0:T(8,128)S(1)} %get-tuple-element.69.own_ref, bf16[128,256]{1,0:T(8,128)(2,1)S(1)} %collective-permute-done.9.sum_1, ...), custom_call_target="tpu_custom_call" | custom-call | tf_op jit(solution)/shard_map/place_kv/pallas_call | solution.py:538
  (15 shorter events, 0.0 us)
Async XLA Ops:
  3.0 24.7 %all-to-all-start = ((bf16[16,128,256]{2,1,0:T(8,128)(2,1)}), bf16[16,128,256]{2,1,0:T(8,128)(2,1)S(1)}, u32[]{:S(2)}, u32[]{:S(2)}) async-start(bf16[16,128,256]{2,1,0:T(8,128)(2,1)} %pick_kv.1), calls=%async_computation | async-start | bytes 2097152 | tf_op jit(solution)/shard_map/all_to_all | solution.py:451
  10.8 0.7 %copy-start = (s32[128]{0:T(128)S(1)}, s32[128]{0:T(128)}, u32[]{:S(2)}) copy-start(s32[128]{0:T(128)} %param.11) | copy-start | bytes 1540
  11.4 1.2 %copy-start.2 = (bf16[512,1024]{1,0:T(8,128)(2,1)S(1)}, bf16[512,1024]{1,0:T(8,128)(2,1)}, u32[]{:S(2)}) copy-start(bf16[512,1024]{1,0:T(8,128)(2,1)} %q_hbm.1) | copy-start | bytes 3145732
  12.7 1.2 %copy-start.3 = (bf16[512,1024]{1,0:T(8,128)(2,1)S(1)}, bf16[512,1024]{1,0:T(8,128)(2,1)}, u32[]{:S(2)}) copy-start(bf16[512,1024]{1,0:T(8,128)(2,1)} %up_hbm.1) | copy-start | bytes 3145732
  14.8 2.0 %collective-permute-start.1 = (bf16[2,4,256,128]{3,2,1,0:T(8,128)(2,1)S(1)}, bf16[2,4,256,128]{3,2,1,0:T(8,128)(2,1)S(1)}, u32[]{:S(2)}, u32[]{:S(2)}) collective-permute-start(bf16[2,4,256,128]{3,2,1,0:T(8,128)(2,1)S(1)} %pick_q.1.own_ref), channel_id=1, source_target_pairs={{0,8},{8,0},{1,9},{9,1},{2,10},{10,2},{3,11},{11,3},{4,12},{12,4},... | collective-permute-start | bytes 1572872 | tf_op jit(solution)/shard_map/ppermute | solution.py:468
  14.9 1.9 %collective-permute-start = (s32[1,128]{1,0:T(1,128)S(1)}, s32[1,128]{1,0:T(1,128)S(1)}, u32[]{:S(2)}, u32[]{:S(2)}) collective-permute-start(s32[1,128]{1,0:T(1,128)S(1)} %bitcast.12), channel_id=1, source_target_pairs={{0,8},{8,0},{1,9},{9,1},{2,10},{10,2},{3,11},{11,3},{4,12},{12,4},... | collective-permute-start | bytes 1544 | tf_op jit(solution)/shard_map/ppermute | solution.py:469
  29.7 1.4 %collective-permute-start.2 = (f32[9,8,256]{2,1,0:T(8,128)S(1)}, f32[9,8,256]{2,1,0:T(8,128)S(1)}, u32[]{:S(2)}, u32[]{:S(2)}) collective-permute-start(f32[9,8,256]{2,1,0:T(8,128)S(1)} %get-tuple-element.40.stats_ref), channel_id=1, source_target_pairs={{0,8},{8,0},{1,9},{9,1},{2,10},{10,2},{3,11},{11,3},{4,12},{12,4},... | collective-permute-start | bytes 221192 | tf_op jit(solution)/shard_map/ppermute | solution.py:489
  31.8 3.9 %collective-permute-start.4 = (f32[8,128]{1,0:T(8,128)S(1)}, f32[8,128]{1,0:T(8,128)S(1)}, u32[]{:S(2)}, u32[]{:S(2)}) collective-permute-start(f32[8,128]{1,0:T(8,128)S(1)} %get-tuple-element.49), channel_id=1, source_target_pairs={{0,1},{1,0},{2,3},{3,2},{4,5},{5,4},{6,7},{7,6},{8,9},{9,8},{10,11... | collective-permute-start | bytes 12296 | tf_op jit(solution)/shard_map/ppermute | solution.py:498
  33.7 21.4 %copy-start.1 = (s32[128]{0:T(128)S(1)}, s32[128]{0:T(128)}, u32[]{:S(2)}) copy-start(s32[128]{0:T(128)} %param.11) | copy-start | bytes 1540
  35.7 11.0 %collective-permute-start.5 = (bf16[4,128,256]{2,1,0:T(8,128)(2,1)S(1)}, bf16[4,128,256]{2,1,0:T(8,128)(2,1)S(1)}, u32[]{:S(2)}, u32[]{:S(2)}) collective-permute-start(bf16[4,128,256]{2,1,0:T(8,128)(2,1)S(1)} %get-tuple-element.55), channel_id=1, source_target_pairs={{0,64},{8,24},{16,80},{24,40},{32,96},{40,56},{48,112},{56,8},{64,... | collective-permute-start | bytes 786440 | tf_op jit(solution)/shard_map/ppermute | solution.py:429
  36.9 12.3 %collective-permute-start.6 = (bf16[4,128,256]{2,1,0:T(8,128)(2,1)S(1)}, bf16[4,128,256]{2,1,0:T(8,128)(2,1)S(1)}, u32[]{:S(2)}, u32[]{:S(2)}) collective-permute-start(bf16[4,128,256]{2,1,0:T(8,128)(2,1)S(1)} %get-tuple-element.56), channel_id=1, source_target_pairs={{0,128},{8,40},{16,144},{24,56},{32,160},{40,8},{48,176},{56,24},{... | collective-permute-start | bytes 786440 | tf_op jit(solution)/shard_map/ppermute | solution.py:429
  42.1 7.2 %collective-permute-start.7 = (bf16[4,128,256]{2,1,0:T(8,128)(2,1)S(1)}, bf16[4,128,256]{2,1,0:T(8,128)(2,1)S(1)}, u32[]{:S(2)}, u32[]{:S(2)}) collective-permute-start(bf16[4,128,256]{2,1,0:T(8,128)(2,1)S(1)} %get-tuple-element.57), channel_id=1, source_target_pairs={{0,192},{8,56},{16,208},{24,8},{32,224},{40,24},{48,240},{56,40},{... | collective-permute-start | bytes 786440 | tf_op jit(solution)/shard_map/ppermute | solution.py:429
  42.1 13.0 %collective-permute-start.3 = (bf16[4,256,128]{2,1,0:T(8,128)(2,1)S(1)}, bf16[4,256,128]{2,1,0:T(8,128)(2,1)S(1)}, u32[]{:S(2)}, u32[]{:S(2)}) collective-permute-start(bf16[4,256,128]{2,1,0:T(8,128)(2,1)S(1)} %get-tuple-element.46), channel_id=1, source_target_pairs={{0,8},{8,0},{1,9},{9,1},{2,10},{10,2},{3,11},{11,3},{4,12},{12,4},... | collective-permute-start | bytes 786440 | tf_op jit(solution)/shard_map/ppermute | solution.py:523
  42.1 7.6 %collective-permute-start.8 = (f32[8,128]{1,0:T(8,128)S(1)}, f32[8,128]{1,0:T(8,128)S(1)}, u32[]{:S(2)}, u32[]{:S(2)}) collective-permute-start(f32[8,128]{1,0:T(8,128)S(1)} %add.65), channel_id=1, source_target_pairs={{0,4},{1,5},{2,6},{3,7},{4,0},{5,1},{6,2},{7,3},{8,12},{9,13},{10,... | collective-permute-start | bytes 12296 | tf_op jit(solution)/shard_map/ppermute | solution.py:522
  49.7 9.9 %collective-permute-start.9 = (bf16[128,256]{1,0:T(8,128)(2,1)S(1)}, bf16[128,256]{1,0:T(8,128)(2,1)S(1)}, u32[]{:S(2)}, u32[]{:S(2)}) collective-permute-start(bf16[128,256]{1,0:T(8,128)(2,1)S(1)} %get-tuple-element.59), channel_id=1, source_target_pairs={{0,16},{8,72},{16,32},{24,88},{32,48},{40,104},{48,0},{56,120},{64... | collective-permute-start | bytes 196616 | tf_op jit(solution)/shard_map/ppermute | solution.py:429
  51.3 8.3 %collective-permute-start.10 = (bf16[128,256]{1,0:T(8,128)(2,1)S(1)}, bf16[128,256]{1,0:T(8,128)(2,1)S(1)}, u32[]{:S(2)}, u32[]{:S(2)}) collective-permute-start(bf16[128,256]{1,0:T(8,128)(2,1)S(1)} %get-tuple-element.60), channel_id=1, source_target_pairs={{0,32},{8,136},{16,48},{24,152},{32,0},{40,168},{48,16},{56,184},{... | collective-permute-start | bytes 196616 | tf_op jit(solution)/shard_map/ppermute | solution.py:429
  53.5 6.1 %collective-permute-start.11 = (bf16[128,256]{1,0:T(8,128)(2,1)S(1)}, bf16[128,256]{1,0:T(8,128)(2,1)S(1)}, u32[]{:S(2)}, u32[]{:S(2)}) collective-permute-start(bf16[128,256]{1,0:T(8,128)(2,1)S(1)} %get-tuple-element.61), channel_id=1, source_target_pairs={{0,48},{8,200},{16,0},{24,216},{32,16},{40,232},{48,32},{56,248},{... | collective-permute-start | bytes 196616 | tf_op jit(solution)/shard_map/ppermute | solution.py:429
  55.1 4.5 %collective-permute-start.12 = (f32[8,128]{1,0:T(8,128)S(1)}, f32[8,128]{1,0:T(8,128)S(1)}, u32[]{:S(2)}, u32[]{:S(2)}) collective-permute-start(f32[8,128]{1,0:T(8,128)S(1)} %add.78.part_a), channel_id=1, source_target_pairs={{0,2},{1,3},{2,0},{3,1},{4,6},{5,7},{6,4},{7,5},{8,10},{9,11},{10,... | collective-permute-start | bytes 12296 | tf_op jit(solution)/shard_map/ppermute | solution.py:537

commit v7 on v5

--- a/solution.py
+++ b/solution.py
@@ -23,7 +23,7 @@
 ROWS = GROUP * CHUNK
 KEYS = 512
 EDGE = 256
-PART = 128
+PART = 256
 SPARE = 2 * CHUNKS
 KEPT = 1536
 KERNEL_BYTES = 16 * 1024 * 1024

time: 61.6 us -> 62.3 us (1.011); the launches traced: 60.6 us -> 62.1 us
  starting transfers between devices: 25 us -> 26.6 us
    ppermute x6, starting transfers between devices: 10.7 us -> 12.3 us  [across(): return lax.ppermute(block, ('y', 'x', 'c'), pairs)]
where the time goes in v7:
time: 62.3 us; the launch traced here: 62.1 us
  starting transfers between devices  26.6 us (43%)
  waiting for transfers between devices  19.5 us (31%)
  Pallas kernels  11.4 us (18%)
  local copies, waits for them, and re-layouts  3.79 us (6%)
  between operations  0.73 us (1%)
    ppermute x6, starting transfers between devices, across(): return lax.ppermute(block, ('y', 'x', 'c'), pairs)  12.3 us
    all_to_all x1, waiting for transfers between devices, local(): kv_all = lax.all_to_all(kv_copies, ('y', 'x'), 0, 0, tiled=True)  10.9 us
    all_to_all x1, starting transfers between devices, local(): kv_all = lax.all_to_all(kv_copies, ('y', 'x'), 0, 0, tiled=True)  7.05 us
    ppermute x1, starting transfers between devices, local(): delta_far = lax.ppermute(deltas, 'tp', [(i, i ^ 4) for i in range(8)])  4.58 us
    unnamed x8, local copies, waits for them, and re-layouts  3.11 us
    ppermute x1, waiting for transfers between devices, local(): logit_rest = lax.ppermute(logit_half, 'tp', [(i, i ^ 2) for i in range(8)])  3.05 us
    ppermute x6, waiting for transfers between devices, across(): return lax.ppermute(block, ('y', 'x', 'c'), pairs)  2.57 us
    pallas_call x1, Pallas kernels, local(): pl.pallas_call(grad_kernel, out_shape=(shape((4, SLOTS, 2 * HEAD)),) * 4...  2.55 us
  transfers between devices with their start and end apart: 14, of which 6 were waited for; matrix products, arithmetic and copies ran while one was open for 1% of the time, Pallas kernels for 8%

profile of v7, /device:TPU:64, one launch (start us, length us, event | category | flops | bytes accessed | tf_op | source)
XLA Modules:
  0.0 62.1 jit_solution(18372516136970599007)
XLA Ops:
  0.6 2.4 %pick_kv.1 = bf16[16,128,256]{2,1,0:T(8,128)(2,1)} custom-call(s32[1,128]{1,0:T(1,128)} %bitcast.10, bf16[512,128]{1,0:T(8,128)(2,1)} %k_hbm.1, bf16[512,128]{1,0:T(8,128)(2,1)} %v_hbm.1), custom_call_target="tpu_custom_call" | custom-call | tf_op jit(solution)/shard_map/pick_kv/pallas_call | solution.py:434
  3.0 7.1 %all-to-all-start = ((bf16[16,128,256]{2,1,0:T(8,128)(2,1)}), bf16[16,128,256]{2,1,0:T(8,128)(2,1)S(1)}, u32[]{:S(2)}, u32[]{:S(2)}) async-start(bf16[16,128,256]{2,1,0:T(8,128)(2,1)} %pick_kv.1), calls=%async_computation | async-start | bytes 2097152 | tf_op jit(solution)/shard_map/all_to_all | solution.py:450
  10.1 0.7 %reshape.49.gate_ref = bf16[1,512]{1,0:T(2,128)(2,1)S(1)} reshape(bf16[512]{0:T(512)(128)(2,1)} %param.9) | data formatting | bytes 2048 | tf_op jit(solution)/shard_map/reshape | solution.py:451
  10.8 0.7 %copy-done = s32[128]{0:T(128)S(1)} copy-done((s32[128]{0:T(128)S(1)}, s32[128]{0:T(128)}, u32[]{:S(2)}) %copy-start) | copy-done | bytes 536
  11.4 1.2 %copy-done.2 = bf16[512,1024]{1,0:T(8,128)(2,1)S(1)} copy-done((bf16[512,1024]{1,0:T(8,128)(2,1)S(1)}, bf16[512,1024]{1,0:T(8,128)(2,1)}, u32[]{:S(2)}) %copy-start.2) | copy-done | bytes 1048600
  12.7 1.2 %copy-done.3 = bf16[512,1024]{1,0:T(8,128)(2,1)S(1)} copy-done((bf16[512,1024]{1,0:T(8,128)(2,1)S(1)}, bf16[512,1024]{1,0:T(8,128)(2,1)}, u32[]{:S(2)}) %copy-start.3) | copy-done | bytes 1048600
  13.9 1.0 %pick_q.1.own_ref = bf16[2,4,256,128]{3,2,1,0:T(8,128)(2,1)S(1)} custom-call(s32[1,128]{1,0:T(1,128)S(1)} %bitcast.11, bf16[1,512]{1,0:T(2,128)(2,1)S(1)} %reshape.49.gate_ref, bf16[512,1024]{1,0:T(8,128)(2,1)S(1)} %copy-done.2, bf16[512,1024]{1,0:T(8,128)(2,1)S(1)} %copy-done.3), custom_call_target="tpu_custom_call" | custom-call | flops 1073741824 | bytes 1048576 | tf_op jit(solution)/shard_map/pick_q/pallas_call | solution.py:452
  14.8 0.1 collective-permute-start.1
  14.9 0.5 collective-permute-start
  15.4 1.4 %collective-permute-done.peer_picked = s32[1,128]{1,0:T(1,128)S(1)} collective-permute-done((s32[1,128]{1,0:T(1,128)S(1)}, s32[1,128]{1,0:T(1,128)S(1)}, u32[]{:S(2)}, u32[]{:S(2)}) %collective-permute-start) | collective-permute-done | bytes 544 | tf_op jit(solution)/shard_map/ppermute | solution.py:468
  16.8 10.9 %all-to-all-done.kv_ref = bf16[16,128,256]{2,1,0:T(8,128)(2,1)S(1)} async-done(((bf16[16,128,256]{2,1,0:T(8,128)(2,1)}), bf16[16,128,256]{2,1,0:T(8,128)(2,1)S(1)}, u32[]{:S(2)}, u32[]{:S(2)}) %all-to-all-start) | async-done | bytes 1048608 | tf_op jit(solution)/shard_map/all_to_all | solution.py:450
  27.7 2.4 %stats.1 = (bf16[2048,128]{1,0:T(8,128)(2,1)S(1)}, bf16[2048,128]{1,0:T(8,128)(2,1)S(1)}, bf16[2304,128]{1,0:T(8,128)(2,1)S(1)}, bf16[2304,128]{1,0:T(8,128)(2,1...) custom-call(s32[1,128]{1,0:T(1,128)S(1)} %collective-permute-done.pe, ...), custom_call_target="tpu_custom_call" | custom-call | tf_op jit(solution)/shard_map/stats/pallas_call | solution.py:469
  30.1 0.1 collective-permute-start.2
  30.2 1.3 %collective-permute-done.2.peer_ref = f32[9,8,256]{2,1,0:T(8,128)S(1)} collective-permute-done((f32[9,8,256]{2,1,0:T(8,128)S(1)}, f32[9,8,256]{2,1,0:T(8,128)S(1)}, u32[]{:S(2)}, u32[]{:S(2)}) %collective-permute-start.2) | collective-permute-done | bytes 73760 | tf_op jit(solution)/shard_map/ppermute | solution.py:488
  31.5 0.8 %combine.1 = (f32[9,8,256]{2,1,0:T(8,128)S(1)}, f32[8,128]{1,0:T(8,128)S(1)}) custom-call(s32[32]{0:T(128)S(1)} %get-tuple-element.35.info_ref, f32[9,8,256]{2,1,0:T(8,128)S(1)} %get-tuple-element.40.stats_ref, f32[9,8,256]{2,1,0:T(8,128)S(1)} %collective-permute-done.2.peer_ref), custom_call_target="tpu_custom_call" | custom-call | tf_op jit(solution)/shard_map/combine/pallas_call | solution.py:489
  32.2 2.0 %collective-permute-start.4 = (f32[8,128]{1,0:T(8,128)S(1)}, f32[8,128]{1,0:T(8,128)S(1)}, u32[]{:S(2)}, u32[]{:S(2)}) collective-permute-start(f32[8,128]{1,0:T(8,128)S(1)} %get-tuple-element.49), channel_id=1, source_target_pairs={{0,1},{1,0},{2,3},{3,2},{4,5},{5,4},{6,7},{7,6},{8,9},{9,8},{10,11... | collective-permute-start | bytes 12296 | tf_op jit(solution)/shard_map/ppermute | solution.py:497
  34.2 2.6 %grads.1 = (bf16[4,128,256]{2,1,0:T(8,128)(2,1)S(1)}, bf16[4,128,256]{2,1,0:T(8,128)(2,1)S(1)}, bf16[4,128,256]{2,1,0:T(8,128)(2,1)S(1)}, bf16[4,128,256]{2,1,0:...) custom-call(s32[32]{0:T(128)S(1)} %get-tuple-element.35.info_ref, ...), custom_call_target="tpu_custom_call" | custom-call | flops 4294967296 | bytes 1048576 | tf_op jit(solution)/shard_map/grads/pallas_call | solution.py:498
  36.8 0.1 collective-permute-start.5
  36.9 5.2 %collective-permute-start.6 = (bf16[4,128,256]{2,1,0:T(8,128)(2,1)S(1)}, bf16[4,128,256]{2,1,0:T(8,128)(2,1)S(1)}, u32[]{:S(2)}, u32[]{:S(2)}) collective-permute-start(bf16[4,128,256]{2,1,0:T(8,128)(2,1)S(1)} %get-tuple-element.56), channel_id=1, source_target_pairs={{0,128},{8,40},{16,144},{24,56},{32,160},{40,8},{48,176},{56,24},{... | collective-permute-start | bytes 786440 | tf_op jit(solution)/shard_map/ppermute | solution.py:428
  42.1 0.0 collective-permute-start.7
  42.1 0.0 collective-permute-start.3
  42.1 4.6 %collective-permute-start.8 = (f32[8,128]{1,0:T(8,128)S(1)}, f32[8,128]{1,0:T(8,128)S(1)}, u32[]{:S(2)}, u32[]{:S(2)}) collective-permute-start(f32[8,128]{1,0:T(8,128)S(1)} %add.65), channel_id=1, source_target_pairs={{0,4},{1,5},{2,6},{3,7},{4,0},{5,1},{6,2},{7,3},{8,12},{9,13},{10,... | collective-permute-start | bytes 12296 | tf_op jit(solution)/shard_map/ppermute | solution.py:520
  46.7 2.6 %collective-permute-done.6 = bf16[4,128,256]{2,1,0:T(8,128)(2,1)S(1)} collective-permute-done((bf16[4,128,256]{2,1,0:T(8,128)(2,1)S(1)}, bf16[4,128,256]{2,1,0:T(8,128)(2,1)S(1)}, u32[]{:S(2)}, u32[]{:S(2)}) %collective-permute-start.6) | collective-permute-done | bytes 262176 | tf_op jit(solution)/shard_map/ppermute | solution.py:428
  49.2 0.1 fusion.2
  49.4 0.3 collective-permute-done.8
  49.7 4.3 %collective-permute-start.9 = (bf16[128,256]{1,0:T(8,128)(2,1)S(1)}, bf16[128,256]{1,0:T(8,128)(2,1)S(1)}, u32[]{:S(2)}, u32[]{:S(2)}) collective-permute-start(bf16[128,256]{1,0:T(8,128)(2,1)S(1)} %get-tuple-element.59), channel_id=1, source_target_pairs={{0,16},{8,72},{16,32},{24,88},{32,48},{40,104},{48,0},{56,120},{64... | collective-permute-start | bytes 196616 | tf_op jit(solution)/shard_map/ppermute | solution.py:428
  54.0 2.7 %collective-permute-start.11 = (bf16[128,256]{1,0:T(8,128)(2,1)S(1)}, bf16[128,256]{1,0:T(8,128)(2,1)S(1)}, u32[]{:S(2)}, u32[]{:S(2)}) collective-permute-start(bf16[128,256]{1,0:T(8,128)(2,1)S(1)} %get-tuple-element.61), channel_id=1, source_target_pairs={{0,48},{8,200},{16,0},{24,216},{32,16},{40,232},{48,32},{56,248},{... | collective-permute-start | bytes 196616 | tf_op jit(solution)/shard_map/ppermute | solution.py:428
  56.7 0.0 collective-permute-start.12
  56.7 1.4 %place_q.1 = (bf16[512,1024]{1,0:T(8,128)(2,1)}, f32[8,128]{1,0:T(8,128)S(1)}) custom-call(s32[1,128]{1,0:T(1,128)S(1)} %bitcast.13, bf16[1,512]{1,0:T(2,128)(2,1)S(1)} %reshape.49.gate_ref, f32[4,256,128]{2,1,0:T(8,128)S(1)} %get-tuple-element.45.dq_own, bf16[4,256,128]{2,1,0:T(8,128)(2,1)S(1)} %collective-permute-done.3.dq_peer), custom_call_target="tpu_custom_call" | custom-call | flops 536870912 | bytes 1048576 | tf_op jit(solution)/shard_map/place_q/pallas_call | solution.py:522
  58.1 3.1 %collective-permute-done.12.part_b = f32[8,128]{1,0:T(8,128)S(1)} collective-permute-done((f32[8,128]{1,0:T(8,128)S(1)}, f32[8,128]{1,0:T(8,128)S(1)}, u32[]{:S(2)}, u32[]{:S(2)}) %collective-permute-start.12) | collective-permute-done | bytes 4128 | tf_op jit(solution)/shard_map/ppermute | solution.py:535
  61.2 0.0 collective-permute-done.9.sum_1
  61.2 0.9 %place_kv.1 = (bf16[512,128]{1,0:T(8,128)(2,1)}, bf16[512,128]{1,0:T(8,128)(2,1)}, bf16[4,128]{1,0:T(4,128)(2,1)}) custom-call(s32[1,128]{1,0:T(1,128)S(1)} %bitcast.14, f32[8,128]{1,0:T(8,128)S(1)} %get-tuple-element.48.closed_ref, f32[128,256]{1,0:T(8,128)S(1)} %get-tuple-element.69.own_ref, bf16[128,256]{1,0:T(8,128)(2,1)S(1)} %collective-permute-done.9.sum_1, ...), custom_call_target="tpu_custom_call" | custom-call | tf_op jit(solution)/shard_map/place_kv/pallas_call | solution.py:536
  (15 shorter events, 0.0 us)
Async XLA Ops:
  3.0 24.7 %all-to-all-start = ((bf16[16,128,256]{2,1,0:T(8,128)(2,1)}), bf16[16,128,256]{2,1,0:T(8,128)(2,1)S(1)}, u32[]{:S(2)}, u32[]{:S(2)}) async-start(bf16[16,128,256]{2,1,0:T(8,128)(2,1)} %pick_kv.1), calls=%async_computation | async-start | bytes 2097152 | tf_op jit(solution)/shard_map/all_to_all | solution.py:450
  10.8 0.7 %copy-start = (s32[128]{0:T(128)S(1)}, s32[128]{0:T(128)}, u32[]{:S(2)}) copy-start(s32[128]{0:T(128)} %param.11) | copy-start | bytes 1540
  11.4 1.2 %copy-start.2 = (bf16[512,1024]{1,0:T(8,128)(2,1)S(1)}, bf16[512,1024]{1,0:T(8,128)(2,1)}, u32[]{:S(2)}) copy-start(bf16[512,1024]{1,0:T(8,128)(2,1)} %q_hbm.1) | copy-start | bytes 3145732
  12.7 1.2 %copy-start.3 = (bf16[512,1024]{1,0:T(8,128)(2,1)S(1)}, bf16[512,1024]{1,0:T(8,128)(2,1)}, u32[]{:S(2)}) copy-start(bf16[512,1024]{1,0:T(8,128)(2,1)} %up_hbm.1) | copy-start | bytes 3145732
  14.8 2.0 %collective-permute-start.1 = (bf16[2,4,256,128]{3,2,1,0:T(8,128)(2,1)S(1)}, bf16[2,4,256,128]{3,2,1,0:T(8,128)(2,1)S(1)}, u32[]{:S(2)}, u32[]{:S(2)}) collective-permute-start(bf16[2,4,256,128]{3,2,1,0:T(8,128)(2,1)S(1)} %pick_q.1.own_ref), channel_id=1, source_target_pairs={{0,8},{8,0},{1,9},{9,1},{2,10},{10,2},{3,11},{11,3},{4,12},{12,4},... | collective-permute-start | bytes 1572872 | tf_op jit(solution)/shard_map/ppermute | solution.py:467
  14.9 1.9 %collective-permute-start = (s32[1,128]{1,0:T(1,128)S(1)}, s32[1,128]{1,0:T(1,128)S(1)}, u32[]{:S(2)}, u32[]{:S(2)}) collective-permute-start(s32[1,128]{1,0:T(1,128)S(1)} %bitcast.12), channel_id=1, source_target_pairs={{0,8},{8,0},{1,9},{9,1},{2,10},{10,2},{3,11},{11,3},{4,12},{12,4},... | collective-permute-start | bytes 1544 | tf_op jit(solution)/shard_map/ppermute | solution.py:468
  30.1 1.4 %collective-permute-start.2 = (f32[9,8,256]{2,1,0:T(8,128)S(1)}, f32[9,8,256]{2,1,0:T(8,128)S(1)}, u32[]{:S(2)}, u32[]{:S(2)}) collective-permute-start(f32[9,8,256]{2,1,0:T(8,128)S(1)} %get-tuple-element.40.stats_ref), channel_id=1, source_target_pairs={{0,8},{8,0},{1,9},{9,1},{2,10},{10,2},{3,11},{11,3},{4,12},{12,4},... | collective-permute-start | bytes 221192 | tf_op jit(solution)/shard_map/ppermute | solution.py:488
  32.2 4.6 %collective-permute-start.4 = (f32[8,128]{1,0:T(8,128)S(1)}, f32[8,128]{1,0:T(8,128)S(1)}, u32[]{:S(2)}, u32[]{:S(2)}) collective-permute-start(f32[8,128]{1,0:T(8,128)S(1)} %get-tuple-element.49), channel_id=1, source_target_pairs={{0,1},{1,0},{2,3},{3,2},{4,5},{5,4},{6,7},{7,6},{8,9},{9,8},{10,11... | collective-permute-start | bytes 12296 | tf_op jit(solution)/shard_map/ppermute | solution.py:497
  34.2 22.5 %copy-start.1 = (s32[128]{0:T(128)S(1)}, s32[128]{0:T(128)}, u32[]{:S(2)}) copy-start(s32[128]{0:T(128)} %param.11) | copy-start | bytes 1540
  36.8 9.9 %collective-permute-start.5 = (bf16[4,128,256]{2,1,0:T(8,128)(2,1)S(1)}, bf16[4,128,256]{2,1,0:T(8,128)(2,1)S(1)}, u32[]{:S(2)}, u32[]{:S(2)}) collective-permute-start(bf16[4,128,256]{2,1,0:T(8,128)(2,1)S(1)} %get-tuple-element.55), channel_id=1, source_target_pairs={{0,64},{8,24},{16,80},{24,40},{32,96},{40,56},{48,112},{56,8},{64,... | collective-permute-start | bytes 786440 | tf_op jit(solution)/shard_map/ppermute | solution.py:428
  36.9 12.3 %collective-permute-start.6 = (bf16[4,128,256]{2,1,0:T(8,128)(2,1)S(1)}, bf16[4,128,256]{2,1,0:T(8,128)(2,1)S(1)}, u32[]{:S(2)}, u32[]{:S(2)}) collective-permute-start(bf16[4,128,256]{2,1,0:T(8,128)(2,1)S(1)} %get-tuple-element.56), channel_id=1, source_target_pairs={{0,128},{8,40},{16,144},{24,56},{32,160},{40,8},{48,176},{56,24},{... | collective-permute-start | bytes 786440 | tf_op jit(solution)/shard_map/ppermute | solution.py:428
  42.1 7.2 %collective-permute-start.7 = (bf16[4,128,256]{2,1,0:T(8,128)(2,1)S(1)}, bf16[4,128,256]{2,1,0:T(8,128)(2,1)S(1)}, u32[]{:S(2)}, u32[]{:S(2)}) collective-permute-start(bf16[4,128,256]{2,1,0:T(8,128)(2,1)S(1)} %get-tuple-element.57), channel_id=1, source_target_pairs={{0,192},{8,56},{16,208},{24,8},{32,224},{40,24},{48,240},{56,40},{... | collective-permute-start | bytes 786440 | tf_op jit(solution)/shard_map/ppermute | solution.py:428
  42.1 14.6 %collective-permute-start.3 = (bf16[4,256,128]{2,1,0:T(8,128)(2,1)S(1)}, bf16[4,256,128]{2,1,0:T(8,128)(2,1)S(1)}, u32[]{:S(2)}, u32[]{:S(2)}) collective-permute-start(bf16[4,256,128]{2,1,0:T(8,128)(2,1)S(1)} %get-tuple-element.46), channel_id=1, source_target_pairs={{0,8},{8,0},{1,9},{9,1},{2,10},{10,2},{3,11},{11,3},{4,12},{12,4},... | collective-permute-start | bytes 786440 | tf_op jit(solution)/shard_map/ppermute | solution.py:521
  42.1 7.6 %collective-permute-start.8 = (f32[8,128]{1,0:T(8,128)S(1)}, f32[8,128]{1,0:T(8,128)S(1)}, u32[]{:S(2)}, u32[]{:S(2)}) collective-permute-start(f32[8,128]{1,0:T(8,128)S(1)} %add.65), channel_id=1, source_target_pairs={{0,4},{1,5},{2,6},{3,7},{4,0},{5,1},{6,2},{7,3},{8,12},{9,13},{10,... | collective-permute-start | bytes 12296 | tf_op jit(solution)/shard_map/ppermute | solution.py:520
  49.7 11.5 %collective-permute-start.9 = (bf16[128,256]{1,0:T(8,128)(2,1)S(1)}, bf16[128,256]{1,0:T(8,128)(2,1)S(1)}, u32[]{:S(2)}, u32[]{:S(2)}) collective-permute-start(bf16[128,256]{1,0:T(8,128)(2,1)S(1)} %get-tuple-element.59), channel_id=1, source_target_pairs={{0,16},{8,72},{16,32},{24,88},{32,48},{40,104},{48,0},{56,120},{64... | collective-permute-start | bytes 196616 | tf_op jit(solution)/shard_map/ppermute | solution.py:428
  54.0 7.2 %collective-permute-start.10 = (bf16[128,256]{1,0:T(8,128)(2,1)S(1)}, bf16[128,256]{1,0:T(8,128)(2,1)S(1)}, u32[]{:S(2)}, u32[]{:S(2)}) collective-permute-start(bf16[128,256]{1,0:T(8,128)(2,1)S(1)} %get-tuple-element.60), channel_id=1, source_target_pairs={{0,32},{8,136},{16,48},{24,152},{32,0},{40,168},{48,16},{56,184},{... | collective-permute-start | bytes 196616 | tf_op jit(solution)/shard_map/ppermute | solution.py:428
  54.0 7.2 %collective-permute-start.11 = (bf16[128,256]{1,0:T(8,128)(2,1)S(1)}, bf16[128,256]{1,0:T(8,128)(2,1)S(1)}, u32[]{:S(2)}, u32[]{:S(2)}) collective-permute-start(bf16[128,256]{1,0:T(8,128)(2,1)S(1)} %get-tuple-element.61), channel_id=1, source_target_pairs={{0,48},{8,200},{16,0},{24,216},{32,16},{40,232},{48,32},{56,248},{... | collective-permute-start | bytes 196616 | tf_op jit(solution)/shard_map/ppermute | solution.py:428
  56.7 4.5 %collective-permute-start.12 = (f32[8,128]{1,0:T(8,128)S(1)}, f32[8,128]{1,0:T(8,128)S(1)}, u32[]{:S(2)}, u32[]{:S(2)}) collective-permute-start(f32[8,128]{1,0:T(8,128)S(1)} %add.78.part_a), channel_id=1, source_target_pairs={{0,2},{1,3},{2,0},{3,1},{4,6},{5,7},{6,4},{7,5},{8,10},{9,11},{10,... | collective-permute-start | bytes 12296 | tf_op jit(solution)/shard_map/ppermute | solution.py:535
